TPU v7x, 128 devices: a whole 4x4x4 slice. The times are simulated.
128 devices in a mesh: rep: 16 (over z, x), row: 8 (over y, core).
Axes of the slice: x: 4, y: 4, z: 4, core: 2. Of those that a mesh axis runs over, the one named last changes fastest.
Arguments:
- delta: bfloat16 [16, 896, 28672], P('rep', 'row')
- error: bfloat16 [16, 896, 28672], P('rep', 'row'), may hold values from -2 to 2
- steps: int32 [16], P('rep'), may hold values from 16 to 64
- q_start: bfloat16 [28672, 64], replicated, may hold values from -0.03125 to 0.03125
- params: float32 [896, 28672], P('row', 'rep'), may hold values from -6 to 6
- momentum: float32 [896, 28672], P('row', 'rep'), may hold values from -2 to 2
Outputs:
- params_new: float32 [896, 28672], P('row', 'rep')
- momentum_new: float32 [896, 28672], P('row', 'rep')
- error_new: bfloat16 [16, 896, 28672], P('rep', 'row')
All inputs are finite; a program needn't handle non-finite values.
Results may differ from a plain program's by a relative error of at most 0.001.
Values sent between devices are 32-bit elements; how exact they have to be, the bound alone decides.
No kernel may reach another device: no remote copies, remote signals or barrier semaphores. Data moves between devices by JAX's collectives and lax.ppermute only.
A program may use at most 128 MiB of HBM per device.

v0:
```python
import jax
import jax.numpy as jnp
from jax import lax
from jax.sharding import PartitionSpec as P

outer_lr = 0.7
beta = 0.9


def local(delta, error, steps, q_start, params, momentum):
    highest = lax.Precision.HIGHEST
    merged = delta[0].astype(jnp.float32) + error[0].astype(jnp.float32)
    counts = steps.astype(jnp.float32)
    own_count = counts[0]
    q_wide = q_start.astype(jnp.float32)
    p_term = own_count * jnp.dot(merged, q_wide, precision=highest)
    p_local, summed_counts = lax.psum((p_term, counts), "rep")
    total = summed_counts[0]
    gram_part = lax.dot_general(p_local, p_local, (((0,), (0,)), ((), ())), precision=highest)
    gram = lax.psum(gram_part, "row")
    lower = jnp.linalg.cholesky(gram)
    p_hat = jax.scipy.linalg.solve_triangular(lower, p_local.T, lower=True).T
    weight = own_count / total
    q_term = weight * lax.dot_general(merged, p_hat, (((0,), (0,)), ((), ())), precision=highest)
    q_new = lax.psum(q_term, ("rep", "row"))
    approx = lax.dot_general(p_hat, q_new, (((1,), (1,)), ((), ())), precision=highest)
    error_new = (merged - approx).astype(jnp.bfloat16)[None]
    cols_dev = params.shape[1]
    approx_cols = lax.dynamic_slice_in_dim(approx, lax.axis_index("rep") * cols_dev, cols_dev, 1)
    momentum_new = beta * momentum + approx_cols
    params_new = params - outer_lr * (approx_cols + beta * momentum_new)
    return (params_new, momentum_new, error_new)


def solution(mesh):
    in_specs = (
        P("rep", "row", None),
        P("rep", "row", None),
        P("rep"),
        P(),
        P("row", "rep"),
        P("row", "rep"),
    )
    out_specs = (P("row", "rep"), P("row", "rep"), P("rep", "row", None))
    return jax.shard_map(local, mesh=mesh, in_specs=in_specs, out_specs=out_specs, check_vma=False)
```

profile of v0, /device:TPU:1, one launch (start us, length us, event | category | flops | bytes accessed | tf_op | source)
XLA Modules:
  0.0 332.8 jit_solution(4034346658459639940)
XLA Ops:
  7.2 0.0 all-reduce.3.cloned.1.call-start
  7.9 12.2 %fusion.5 = f32[112,64]{0,1:T(8,128)S(1)} fusion(bf16[28672,64]{0,1:T(8,128)(2,1)} %param.9, bf16[1,112,28672]{2,1,0:T(8,128)(2,1)} %param.7, bf16[1,112,28672]{2,1,0:T(8,128)(2,1)} %param.6, f32[]{:T(128)} %bitcast), kind=kOutput, calls=%fused_computation.8 | convolution fusion | flops 2475891712 | bytes 16543748 | tf_op jit(solution)/shard_map/dot_general | solution.py:16
  20.0 64.0 %all-reduce = (f32[112,64]{0,1:T(8,128)S(1)}, f32[]{:T(128)}) all-reduce(f32[112,64]{0,1:T(8,128)S(1)} %fusion.5, f32[]{:T(128)} %bitcast), channel_id=1, replica_groups=mesh['rep'=16,'row'=8] {'rep'}, use_global_device_ids=true, to_apply=%region_0.0 | all-reduce | flops 7169 | bytes 57352 | tf_op jit(solution)/shard_map/psum | solution.py:17
  84.0 0.2 fusion.12
  84.2 35.0 %psum.29 = f32[64,64]{0,1:T(8,128)S(1)} all-reduce(f32[64,64]{0,1:T(8,128)S(1)} %fusion.12), channel_id=1, replica_groups=mesh['rep'=16,'row'=8] {'row'}, use_global_device_ids=true, to_apply=%region_1.0 | all-reduce | flops 4096 | bytes 32768 | tf_op jit(solution)/shard_map/psum | solution.py:20
  119.2 0.1 copy.12
  119.3 5.8 %cholesky.16 = f32[64,64]{1,0:T(8,128)S(1)} custom-call(f32[64,64]{1,0:T(8,128)S(1)} %fusion.11), custom_call_target="Cholesky" | custom-call | tf_op jit(solution)/shard_map/jit(cholesky)/cholesky | solution.py:21
  125.2 0.6 compare_reduce_fusion
  125.8 0.7 fusion.8
  126.5 4.9 %custom-call.7 = f32[1,64,64]{1,2,0:T(8,128)S(1)} custom-call(f32[1,64,64]{2,1,0:T(8,128)S(1)} %fusion.8), custom_call_target="InvertDiagBlocksLowerTriangular" | custom-call | tf_op jit(solution)/shard_map/jit(_solve_triangular)/triangular_solve | solution.py:22
  131.4 0.3 fusion.9
  132.3 14.1 %convolution_multiply_fusion = f32[28672,64]{0,1:T(8,128)} fusion(f32[64,112]{1,0:T(8,128)S(1)} %fusion.9, bf16[1,112,28672]{2,1,0:T(8,128)(2,1)} %param.7, bf16[1,112,28672]{2,1,0:T(8,128)(2,1)} %param.6, f32[]{:T(128)S(6)} %div.13), kind=kOutput, calls=%fused_computation | convolution fusion | flops 2477719552 | bytes 20213764 | tf_op jit(solution)/shard_map/dot_general | solution.py:24
  146.4 0.0 all-reduce.3.cloned.1.call-update
  146.5 156.1 %all-reduce.3.cloned.1.call-done = f32[28672,64]{0,1:T(8,128)} async-done(((f32[28672,64]{0,1:T(8,128)}), f32[28672,64]{0,1:T(8,128)}) %all-reduce.3.cloned.1.call-update) | async-done | bytes 7340048 | tf_op jit(solution)/shard_map/psum | solution.py:25
  302.6 13.0 %fusion.13 = f32[112,28672]{1,0:T(8,128)S(1)} fusion(f32[64,112]{1,0:T(8,128)S(1)} %fusion.9, f32[28672,64]{0,1:T(8,128)} %all-reduce.3.cloned.1.call-done), kind=kOutput, calls=%fused_computation.22 | convolution fusion | flops 2466250752 | bytes 20213760 | tf_op jit(solution)/shard_map/dot_general | solution.py:26
  315.6 0.0 copy-start
  315.6 0.0 copy-start.1
  315.6 9.0 %fusion.4 = bf16[1,112,28672]{2,1,0:T(8,128)(2,1)} fusion(f32[112,28672]{1,0:T(8,128)S(1)} %fusion.13, bf16[1,112,28672]{2,1,0:T(8,128)(2,1)} %param.7, bf16[1,112,28672]{2,1,0:T(8,128)(2,1)} %param.6), kind=kLoop, calls=%fused_computation.7 | loop fusion | flops 16056320 | bytes 32112640 | tf_op jit(solution)/shard_map/broadcast_in_dim | solution.py:27
  324.6 0.0 copy-done
  324.6 0.0 copy-done.1
  324.6 1.3 multiply_subtract_fusion
  (2 shorter events, 0.0 us)
Async XLA Ops:
  7.2 295.4 %all-reduce.3.cloned.1.call-start = ((), (), s32[]{:S(2)}) async-start(), calls=%async_computation | async-start | bytes 14680064 | tf_op jit(solution)/shard_map/psum | solution.py:25
  315.6 9.0 %copy-start = (f32[112,1792]{1,0:T(8,128)S(1)}, f32[112,1792]{1,0:T(8,128)}, u32[]{:S(2)}) copy-start(f32[112,1792]{1,0:T(8,128)} %param.10) | copy-start | bytes 2408452
  315.6 9.0 %copy-start.1 = (f32[112,1792]{1,0:T(8,128)S(1)}, f32[112,1792]{1,0:T(8,128)}, u32[]{:S(2)}) copy-start(f32[112,1792]{1,0:T(8,128)} %param.11) | copy-start | bytes 2408452
Sparse Core Ops, SparseCore 0:
  146.6 155.9 all-reduce.2
where the time goes:
time: 333 us
  waiting for transfers between devices  156 us (47%)
  blocking collectives  98.9 us (30%)
  matrix products  39.8 us (12%)
  other arithmetic  22.4 us (7%)
  between operations  15.4 us (5%)
    psum x1, waiting for transfers between devices, local(): q_new = lax.psum(q_term, ('rep', 'row'))  156 us
    psum x1, blocking collectives, local(): p_local, summed_counts = lax.psum((p_term, counts), 'rep')  64 us
    psum x1, blocking collectives, local(): gram = lax.psum(gram_part, 'row')  35 us
    dot_general x1, matrix products, local(): lax.dot_general(merged, p_hat, (((0,), (0,)), ((), ())), precision=highest)  14.1 us
    dot_general x1, matrix products, local(): lax.dot_general(p_hat, q_new, (((1,), (1,)), ((), ())), precision=highest)  13 us
    dot_general x1, matrix products, local(): p_term = own_count * jnp.dot(merged, q_wide, precision=highest)  12.2 us
    broadcast_in_dim x1, other arithmetic, local(): error_new = (merged - approx).astype(jnp.bfloat16)[None]  8.99 us
  transfers between devices with their start and end apart: 1, of which 1 were waited for; matrix products, arithmetic and copies ran while one was open for 0% of the time, Pallas kernels for 0%

commit v1 on v0

v1 whole, which is shorter than its diff:
```python
import functools

import jax
import jax.numpy as jnp
from jax import lax
from jax.experimental import pallas as pl
from jax.experimental.pallas import tpu as pltpu
from jax.sharding import Mesh, PartitionSpec as P

outer_lr = 0.7
beta = 0.9

AXES = ("zh", "zl", "xh", "xl", "yh", "yl", "c")
REP = ("zh", "zl", "xh", "xl")
ROW = ("yh", "yl", "c")
HIGH = ("zh", "xh", "yh")
ROUTES = (("xl", "yl", "zl"), ("yl", "zl", "xl"), ("zl", "xl", "yl"))

TILES = 7
WIDE = TILES * 128
COUNTS = (5, 5, 6)
FIRST = (0, 5, 10)
HALF = 16
BF = jnp.bfloat16
F32 = jnp.float32
VMEM_LIMIT = 48 << 20


def params_of(**kw):
    return pltpu.CompilerParams(vmem_limit_bytes=VMEM_LIMIT, **kw)


def turn(x, axes, step):
    return lax.ppermute(x, axes, [(i, (i + step) % 4) for i in range(4)])


def swap(x, axis):
    return lax.ppermute(x, axis, [(0, 1), (1, 0)])


def p_kernel(steps_ref, d_ref, e_ref, q_ref, out_ref, acc_ref):
    i = pl.program_id(0)

    @pl.when(i == 0)
    def _():
        acc_ref[...] = jnp.zeros_like(acc_ref)

    both = jnp.concatenate([d_ref[0], e_ref[0]], axis=0)
    acc_ref[...] += lax.dot_general(both, q_ref[...], (((1,), (1,)), ((), ())), preferred_element_type=F32)

    @pl.when(i == pl.num_programs(0) - 1)
    def _():
        count = steps_ref[0].astype(F32)
        out_ref[...] = jnp.full(out_ref.shape, count, F32)
        out_ref[0:112, 0:64] = count * (acc_ref[0:112, :] + acc_ref[112:224, :])


def left_factor(delta, error, q_t, steps):
    width = delta.shape[2]
    block = 2048
    return pl.pallas_call(
        p_kernel,
        grid=(width // block,),
        in_specs=[
            pl.BlockSpec(memory_space=pltpu.SMEM),
            pl.BlockSpec((1, 112, block), lambda i: (0, 0, i)),
            pl.BlockSpec((1, 112, block), lambda i: (0, 0, i)),
            pl.BlockSpec((64, block), lambda i: (0, i)),
        ],
        out_specs=pl.BlockSpec((120, 128), lambda i: (0, 0)),
        out_shape=jax.ShapeDtypeStruct((120, 128), F32),
        scratch_shapes=[pltpu.VMEM((224, 64), F32)],
        compiler_params=params_of(),
        name="left_factor",
    )(steps, delta, error, q_t)


def prep_kernel(steps_ref, a_ref, b_ref, c_ref, d_ref, p_ref, lhs_ref, gram_ref):
    both = (a_ref[...] + b_ref[...]) + (c_ref[...] + d_ref[...])
    p = both[0:112, 0:64]
    total = both[112:113, 0:1]
    p_ref[...] = both
    top = jnp.max(jnp.abs(p), axis=0, keepdims=True)
    weight = steps_ref[0].astype(F32) / total
    unit = p * (1.0 / jnp.maximum(top, 1e-37)) * weight
    flat = unit.T
    high = flat.astype(BF).astype(F32)
    low = flat - high
    lhs_ref[0:64, :] = jnp.concatenate([high, high], axis=1).astype(BF)
    lhs_ref[64:128, :] = jnp.concatenate([low, low], axis=1).astype(BF)
    gram_ref[...] = jnp.zeros_like(gram_ref)
    gram_ref[0:64, 0:64] = lax.dot_general(p, p, (((0,), (0,)), ((), ())), precision=lax.Precision.HIGHEST, preferred_element_type=F32)
    gram_ref[64:65, 0:64] = top


def prepare(steps, a, b, c, d):
    vm = pl.BlockSpec(memory_space=pltpu.VMEM)
    return pl.pallas_call(
        prep_kernel,
        in_specs=[pl.BlockSpec(memory_space=pltpu.SMEM), vm, vm, vm, vm],
        out_specs=[vm, vm, vm],
        out_shape=[
            jax.ShapeDtypeStruct((120, 128), F32),
            jax.ShapeDtypeStruct((128, 224), BF),
            jax.ShapeDtypeStruct((72, 128), F32),
        ],
        compiler_params=params_of(),
        name="prepare",
    )(steps, a, b, c, d)


def product(lhs_ref, d_ref, e_ref):
    both = jnp.concatenate([d_ref[0], e_ref[0]], axis=0)
    r = lax.dot_general(lhs_ref[...], both, (((1,), (0,)), ((), ())), preferred_element_type=F32)
    return r[0:64] + r[64:128]


def send_kernel(s_ref, lhs_ref, d_ref, e_ref, out_ref):
    v = product(lhs_ref, d_ref, e_ref)
    for i in range(8):
        for t in range(TILES):
            out_ref[i, t] = v[8 * i:8 * i + 8, 128 * t:128 * t + 128]


def q_send(where, lhs, delta, error, k):
    n, first = COUNTS[k], FIRST[k]
    column = lambda i, s: (0, 0, (1 - s[0]) * HALF + first + i)
    return pl.pallas_call(
        send_kernel,
        grid_spec=pltpu.PrefetchScalarGridSpec(
            num_scalar_prefetch=1,
            grid=(n,),
            in_specs=[
                pl.BlockSpec((128, 224), lambda i, s: (0, 0)),
                pl.BlockSpec((1, 112, WIDE), column),
                pl.BlockSpec((1, 112, WIDE), column),
            ],
            out_specs=pl.BlockSpec((8, TILES, 8, 128), lambda i, s: (0, i, 0, 0)),
        ),
        out_shape=jax.ShapeDtypeStruct((8, n * TILES, 8, 128), F32),
        compiler_params=params_of(),
        cost_estimate=pl.CostEstimate(flops=2 * 128 * 224 * n * WIDE, bytes_accessed=n * WIDE * (448 + 256), transcendentals=0),
        name="q_send",
    )(where, lhs, delta, error)


def keep_kernel(s_ref, lhs_ref, d_ref, e_ref, r_ref, own_ref, other_ref, keep_ref, send_ref, scr_ref):
    v = product(lhs_ref, d_ref, e_ref)
    for i in range(8):
        own = own_ref[8 * i:8 * i + 8, :]
        other = other_ref[8 * i:8 * i + 8, :]
        for t in range(TILES):
            scr_ref[i, t] = own * v[8 * i:8 * i + 8, 128 * t:128 * t + 128] + other * r_ref[i, t]
    bit = s_ref[1]
    keep_ref[...] = scr_ref[pl.ds(bit * 4, 4)]
    send_ref[...] = scr_ref[pl.ds((1 - bit) * 4, 4)]


def q_keep(where, lhs, delta, error, arrived, own, other, k):
    n, first = COUNTS[k], FIRST[k]
    column = lambda i, s: (0, 0, s[0] * HALF + first + i)
    fixed = lambda i, s: (0, 0)
    moving = lambda i, s: (0, i, 0, 0)
    half = jax.ShapeDtypeStruct((4, n * TILES, 8, 128), F32)
    return pl.pallas_call(
        keep_kernel,
        grid_spec=pltpu.PrefetchScalarGridSpec(
            num_scalar_prefetch=1,
            grid=(n,),
            in_specs=[
                pl.BlockSpec((128, 224), fixed),
                pl.BlockSpec((1, 112, WIDE), column),
                pl.BlockSpec((1, 112, WIDE), column),
                pl.BlockSpec((8, TILES, 8, 128), moving),
                pl.BlockSpec((64, 128), fixed),
                pl.BlockSpec((64, 128), fixed),
            ],
            out_specs=[pl.BlockSpec((4, TILES, 8, 128), moving)] * 2,
            scratch_shapes=[pltpu.VMEM((8, TILES, 8, 128), F32)],
        ),
        out_shape=[half, half],
        compiler_params=params_of(),
        cost_estimate=pl.CostEstimate(flops=2 * 128 * 224 * n * WIDE, bytes_accessed=n * WIDE * (448 + 512), transcendentals=0),
        name="q_keep",
    )(where, lhs, delta, error, arrived, own, other)


def approx_of(bit, w_ref, a_ref, b_ref, scr_ref):
    for i in range(4):
        for t in range(TILES):
            scr_ref[pl.ds((bit * 4 + i) * 8, 8), 128 * t:128 * t + 128] = a_ref[i, t]
            scr_ref[pl.ds(((1 - bit) * 4 + i) * 8, 8), 128 * t:128 * t + 128] = b_ref[i, t]
    q = scr_ref[...]
    high = q.astype(BF)
    low = (q - high.astype(F32)).astype(BF)
    rhs = jnp.concatenate([high, low, high], axis=0)
    return lax.dot_general(w_ref[...], rhs, (((1,), (0,)), ((), ())), preferred_element_type=F32)


def error_kernel(s_ref, w_ref, a_ref, b_ref, d_ref, e_ref, *rest):
    out_ref, scr_ref = rest[-2], rest[-1]
    approx = approx_of(s_ref[1], w_ref, a_ref, b_ref, scr_ref)
    out_ref[0] = ((d_ref[0].astype(F32) + e_ref[0].astype(F32)) - approx).astype(BF)


def new_error(where, w, a, b, delta, error, base, k):
    n, first = COUNTS[k], FIRST[k]
    column = lambda i, s: (0, 0, s[0] * HALF + first + i)
    moving = lambda i, s: (0, i, 0, 0)
    specs = [
        pl.BlockSpec((112, 192), lambda i, s: (0, 0)),
        pl.BlockSpec((4, TILES, 8, 128), moving),
        pl.BlockSpec((4, TILES, 8, 128), moving),
        pl.BlockSpec((1, 112, WIDE), column),
        pl.BlockSpec((1, 112, WIDE), column),
    ]
    args = [where, w, a, b, delta, error]
    aliases = {}
    if base is not None:
        specs.append(pl.BlockSpec(memory_space=pl.ANY))
        args.append(base)
        aliases = {6: 0}
    return pl.pallas_call(
        error_kernel,
        grid_spec=pltpu.PrefetchScalarGridSpec(
            num_scalar_prefetch=1,
            grid=(n,),
            in_specs=specs,
            out_specs=pl.BlockSpec((1, 112, WIDE), column),
            scratch_shapes=[pltpu.VMEM((64, WIDE), F32)],
        ),
        out_shape=jax.ShapeDtypeStruct(delta.shape, BF),
        input_output_aliases=aliases,
        compiler_params=params_of(),
        cost_estimate=pl.CostEstimate(flops=2 * 112 * 192 * n * WIDE, bytes_accessed=n * WIDE * (672 + 256), transcendentals=0),
        name="new_error",
    )(*args)


def outer_kernel(s_ref, w_ref, *refs):
    sources = refs[0:12]
    par_ref, mom_ref, np_ref, nm_ref, a_ref, b_ref, scr_ref, sem = refs[12:]
    core = s_ref[0]
    for j in range(2):
        block = 2 * s_ref[4] + j
        for side in range(2):
            for k in range(3):
                first = side * HALF + FIRST[k]
                here = (block >= first) & (block < first + COUNTS[k])
                for own in range(2):
                    a_src, b_src = sources[(own * 3 + k) * 2], sources[(own * 3 + k) * 2 + 1]

                    @pl.when(here & (core == (side if own == 0 else 1 - side)))
                    def _():
                        tiles = pl.ds((block - first) * TILES, TILES)
                        one = pltpu.make_async_copy(a_src.at[:, tiles], a_ref.at[j, 0], sem.at[j, 0])
                        two = pltpu.make_async_copy(b_src.at[:, tiles], b_ref.at[j, 0], sem.at[j, 1])
                        one.start()
                        two.start()
                        one.wait()
                        two.wait()
    for j in range(2):
        block = 2 * s_ref[4] + j
        inner = lax.rem(block, HALF)
        bit = jnp.where(inner < FIRST[1], s_ref[1], jnp.where(inner < FIRST[2], s_ref[2], s_ref[3]))
        approx = approx_of(bit, w_ref, a_ref.at[j, 0], b_ref.at[j, 0], scr_ref)
        lanes = slice(j * WIDE, (j + 1) * WIDE)
        momentum = beta * mom_ref[:, lanes] + approx
        nm_ref[:, lanes] = momentum
        np_ref[:, lanes] = par_ref[:, lanes] - outer_lr * (approx + beta * momentum)


def outer_update(where, w, sources, params, momentum):
    vm = pl.BlockSpec(memory_space=pltpu.VMEM)
    shape = jax.ShapeDtypeStruct(params.shape, F32)
    return pl.pallas_call(
        outer_kernel,
        in_specs=[pl.BlockSpec(memory_space=pltpu.SMEM), vm] + [pl.BlockSpec(memory_space=pl.ANY)] * 12 + [vm, vm],
        out_specs=[vm, vm],
        out_shape=[shape, shape],
        scratch_shapes=[
            pltpu.VMEM((2, 1, 4, TILES, 8, 128), F32),
            pltpu.VMEM((2, 1, 4, TILES, 8, 128), F32),
            pltpu.VMEM((64, WIDE), F32),
            pltpu.SemaphoreType.DMA((2, 2)),
        ],
        compiler_params=params_of(),
        name="outer_update",
    )(where, w, *sources, params, momentum)


def local(delta, error, steps, q_start, params, momentum):
    highest = lax.Precision.HIGHEST
    bit = {a: lax.axis_index(a) for a in AXES}
    core = bit["c"]
    rep = lax.axis_index(REP)

    own = left_factor(delta, error, q_start.T, steps)
    X, Z = ("xh", "xl"), ("zh", "zl")
    own = (own + turn(own, X, 2)) + (turn(own, X, 1) + turn(own, X, 3))
    p_all, lhs, gram_own = prepare(steps, own, turn(own, Z, 2), turn(own, Z, 1), turn(own, Z, 3))

    gram_near = swap(gram_own, "c")
    top_own, top_near = gram_own[64, :64], gram_near[64, :64]
    row64 = lax.broadcasted_iota(jnp.int32, gram_own.shape, 0) == 64
    join = lambda a, b: jnp.where(row64, jnp.maximum(a, b), a + b)
    both = join(gram_own, gram_near)
    Y = ("yh", "yl")
    both = join(join(both, turn(both, Y, 2)), join(turn(both, Y, 1), turn(both, Y, 3)))
    gram, top = both[:64, :64], both[64, :64]
    scale_own = jnp.broadcast_to((top_own / top)[:, None], (64, 128))
    scale_near = jnp.broadcast_to((top_near / top)[:, None], (64, 128))

    wheres = [jnp.stack([core, bit[r[0]]]) for r in ROUTES]
    arrived = [swap(q_send(wheres[k], lhs, delta, error, k), "c") for k in range(3)]
    parts = []
    for k, (d0, d1, d2) in enumerate(ROUTES):
        keep, send = q_keep(wheres[k], lhs, delta, error, arrived[k], scale_own, scale_near, k)
        got = swap(send, d0)
        for d in (d1, d2):
            n = keep.shape[0] // 2
            take = lambda x, b: lax.dynamic_slice_in_dim(x, b * n, n, 0)
            send = take(keep, 1 - bit[d]) + take(got, 1 - bit[d])
            keep = take(keep, bit[d]) + take(got, bit[d])
            got = swap(send, d)
        parts.append(keep[0] + got[0])
    mine = jnp.concatenate(parts, axis=0)
    mine = lax.all_to_all(mine, HIGH, 0, 0, tiled=True)
    mine = jnp.sum(mine.reshape(8, 2 * TILES, 8, 128), axis=0)

    inv_top = 1.0 / top
    lower = jnp.linalg.cholesky(gram * inv_top[:, None] * inv_top[None, :])
    inverse = jax.scipy.linalg.solve_triangular(lower, jnp.eye(64, dtype=F32), lower=True)
    p_hat = jnp.dot(p_all[:112, :64] * inv_top[None, :], inverse.T, precision=highest)
    w = jnp.dot(p_hat, inverse, precision=highest)
    w_high = w.astype(BF).astype(F32)
    w_cat = jnp.concatenate([w_high, w_high, w - w_high], axis=1).astype(BF)

    full = lax.all_gather(mine, HIGH, axis=0, tiled=True)
    sides = []
    for k, (d0, d1, d2) in enumerate(ROUTES):
        v = full[FIRST[k] * TILES:(FIRST[k] + COUNTS[k]) * TILES][None]
        for d in (d2, d1):
            got = swap(v, d)
            v = jnp.where(bit[d] == 0, jnp.concatenate([v, got], 0), jnp.concatenate([got, v], 0))
        sides.append((v, swap(v, d0)))
    error_new = None
    for k in range(3):
        error_new = new_error(wheres[k], w_cat, *sides[k], delta, error, error_new, k)
    far = [(swap(a, "c"), swap(b, "c")) for a, b in sides]
    for k in range(3):
        flipped = jnp.stack([1 - core, bit[ROUTES[k][0]]])
        error_new = new_error(flipped, w_cat, *far[k], delta, error, error_new, k)
    sources = [x for pair in sides + far for x in pair]
    where = jnp.stack([core] + [bit[r[0]] for r in ROUTES] + [rep])
    params_new, momentum_new = outer_update(where, w_cat, sources, params, momentum)
    return (params_new, momentum_new, error_new)


def solution(mesh):
    fine = Mesh(mesh.devices.reshape((2,) * 7), AXES)
    in_specs = (
        P(REP, ROW, None),
        P(REP, ROW, None),
        P(REP),
        P(),
        P(ROW, REP),
        P(ROW, REP),
    )
    out_specs = (P(ROW, REP), P(ROW, REP), P(REP, ROW, None))
    return jax.shard_map(local, mesh=fine, in_specs=in_specs, out_specs=out_specs, check_vma=False)
```

time: 333 us -> 257 us (0.77)
  waiting for transfers between devices: 156 us -> 43 us
  Pallas kernels: 0 us -> 82.6 us
  starting transfers between devices: 0.04 us -> 63.4 us
  blocking collectives: 98.9 us -> 39.7 us
  matrix products: 39.8 us -> 0.69 us
  between operations: 15.4 us -> 1.8 us
    psum x1 -> x0, waiting for transfers between devices: 156 us -> none  [local(): q_new = lax.psum(q_term, ('rep', 'row'))]
    psum x2 -> x0, blocking collectives: 98.9 us -> none  [the longest x1 64 us: local(): p_local, summed_counts = lax.psum((p_term, counts), 'rep')]
    pallas_call x0 -> x15, Pallas kernels: none -> 82.6 us  [the longest x6 34.3 us: new_error(): pl.pallas_call(error_kernel, grid_spec=pltpu.PrefetchScalarGridSpec(num_s...]
    ppermute x0 -> x37, starting transfers between devices: none -> 52.1 us  [the longest x28 33.4 us: swap(): return lax.ppermute(x, axis, [(0, 1), (1, 0)])]
    all_gather x0 -> x1, blocking collectives: none -> 39.7 us  [local(): full = lax.all_gather(mine, HIGH, axis=0, tiled=True)]
    dot_general x4 -> x2, matrix products: 39.5 us -> 0.46 us  [the longest x1 0.24 us: local(): w = jnp.dot(p_hat, inverse, precision=highest)]
    ppermute x0 -> x37, waiting for transfers between devices: none -> 37.7 us  [the longest x28 31.7 us: swap(): return lax.ppermute(x, axis, [(0, 1), (1, 0)])]
    all_to_all x0 -> x1, starting transfers between devices: none -> 11.3 us  [local(): mine = lax.all_to_all(mine, HIGH, 0, 0, tiled=True)]
  transfers between devices with their start and end apart: 1 -> 38, of which waited for: 1 -> 16; matrix products, arithmetic and copies ran while one was open for 0% -> 9% of each run, Pallas kernels for 0% -> 21%
where the time goes in v1:
time: 257 us; the launch traced here: 256 us
  Pallas kernels  82.6 us (32%)
  starting transfers between devices  63.4 us (25%)
  waiting for transfers between devices  43 us (17%)
  blocking collectives  39.7 us (15%)
  other arithmetic  21.7 us (8%)
  local copies, waits for them, and re-layouts  2.77 us (1%)
    all_gather x1, blocking collectives, local(): full = lax.all_gather(mine, HIGH, axis=0, tiled=True)  39.7 us
    pallas_call x6, Pallas kernels, new_error(): pl.pallas_call(error_kernel, grid_spec=pltpu.PrefetchScalarGridSpec(num_s...  34.3 us
    ppermute x28, starting transfers between devices, swap(): return lax.ppermute(x, axis, [(0, 1), (1, 0)])  33.4 us
    ppermute x28, waiting for transfers between devices, swap(): return lax.ppermute(x, axis, [(0, 1), (1, 0)])  31.7 us
    ppermute x9, starting transfers between devices, turn(): return lax.ppermute(x, axes, [(i, (i + step) % 4) for i in range(4)])  18.7 us
    pallas_call x3, Pallas kernels, q_keep(): pl.pallas_call(keep_kernel, grid_spec=pltpu.PrefetchScalarGridSpec(num_sc...  15.9 us
    pallas_call x3, Pallas kernels, q_send(): pl.pallas_call(send_kernel, grid_spec=pltpu.PrefetchScalarGridSpec(num_sc...  15.4 us
    pallas_call x1, Pallas kernels, left_factor(): pl.pallas_call(p_kernel, grid=(width // block,), in_specs=[pl.BlockSpec(m...  11.8 us
  transfers between devices with their start and end apart: 38, of which 16 were waited for; matrix products, arithmetic and copies ran while one was open for 9% of the time, Pallas kernels for 21%

profile of v1, /device:TPU:1, one launch (start us, length us, event | category | flops | bytes accessed | tf_op | source)
XLA Modules:
  0.0 255.7 jit_solution(12666631062622856428)
XLA Ops:
  3.3 11.8 %left_factor.1 = f32[120,128]{1,0:T(8,128)S(1)} custom-call(s32[1]{0:T(128)S(6)} %copy.49.steps_ref, bf16[1,112,28672]{2,1,0:T(8,128)(2,1)} %d_ref.25, bf16[1,112,28672]{2,1,0:T(8,128)(2,1)} %e_ref.25, bf16[64,28672]{1,0:T(8,128)(2,1)S(1)} %bitcast.32), custom_call_target="tpu_custom_call" | custom-call | tf_op jit(solution)/shard_map/left_factor/pallas_call | solution.py:61
  15.1 3.7 %collective-permute-start = (f32[120,128]{1,0:T(8,128)S(1)}, f32[120,128]{1,0:T(8,128)S(1)}, u32[]{:S(2)}, u32[]{:S(2)}) collective-permute-start(f32[120,128]{1,0:T(8,128)S(1)} %left_factor.1), channel_id=1, source_target_pairs={{0,16},{8,24},{16,0},{24,8},{1,17},{9,25},{17,1},{25,9},{2,18},{10... | collective-permute-start | bytes 184328 | tf_op jit(solution)/shard_map/ppermute | solution.py:34
  19.0 2.4 collective-permute-start.2
  23.1 3.6 %collective-permute-start.3 = (f32[120,128]{1,0:T(8,128)S(1)}, f32[120,128]{1,0:T(8,128)S(1)}, u32[]{:S(2)}, u32[]{:S(2)}) collective-permute-start(f32[120,128]{1,0:T(8,128)S(1)} %add_add_fusion.a_ref), channel_id=1, source_target_pairs={{0,64},{32,96},{64,0},{96,32},{1,65},{33,97},{65,1},{97,33},{2,66}... | collective-permute-start | bytes 184328 | tf_op jit(solution)/shard_map/ppermute | solution.py:34
  31.5 5.4 %q_send.3 = f32[8,35,8,128]{3,2,1,0:T(8,128)} custom-call(s32[2]{0:T(128)S(1)} %pad_add_fusion.1.s_ref, bf16[128,224]{1,0:T(8,128)(2,1)S(1)} %get-tuple-element.16.lhs_ref, bf16[1,112,28672]{2,1,0:T(8,128)(2,1)} %d_ref.25, bf16[1,112,28672]{2,1,0:T(8,128)(2,1)} %e_ref.25), custom_call_target="tpu_custom_call" | custom-call | flops 256901120 | bytes 3153920 | tf_op jit(solution)/shard_map/q_send/pallas_call | solution.py:128
  36.9 3.3 %collective-permute-start.10 = (f32[8,35,8,128]{3,2,1,0:T(8,128)}, f32[8,35,8,128]{3,2,1,0:T(8,128)}, u32[]{:S(2)}, u32[]{:S(2)}) collective-permute-start(f32[8,35,8,128]{3,2,1,0:T(8,128)} %q_send.3), channel_id=1, source_target_pairs={{0,1},{1,0},{2,3},{3,2},{4,5},{5,4},{6,7},{7,6},{8,9},{9,8},{10,11... | collective-permute-start | bytes 3440648 | tf_op jit(solution)/shard_map/ppermute | solution.py:38
  40.3 4.7 %q_send.5 = f32[8,42,8,128]{3,2,1,0:T(8,128)S(1)} custom-call(s32[2]{0:T(128)S(1)} %pad_add_fusion.5.s_ref, bf16[128,224]{1,0:T(8,128)(2,1)S(1)} %get-tuple-element.16.lhs_ref, bf16[1,112,28672]{2,1,0:T(8,128)(2,1)} %d_ref.25, bf16[1,112,28672]{2,1,0:T(8,128)(2,1)} %e_ref.25), custom_call_target="tpu_custom_call" | custom-call | flops 308281344 | bytes 3784704 | tf_op jit(solution)/shard_map/q_send/pallas_call | solution.py:128
  45.1 5.3 %q_send.4 = f32[8,35,8,128]{3,2,1,0:T(8,128)} custom-call(s32[2]{0:T(128)S(1)} %pad_add_fusion.3.s_ref, bf16[128,224]{1,0:T(8,128)(2,1)S(1)} %get-tuple-element.16.lhs_ref, bf16[1,112,28672]{2,1,0:T(8,128)(2,1)} %d_ref.25, bf16[1,112,28672]{2,1,0:T(8,128)(2,1)} %e_ref.25), custom_call_target="tpu_custom_call" | custom-call | flops 256901120 | bytes 3153920 | tf_op jit(solution)/shard_map/q_send/pallas_call | solution.py:128
  53.5 3.0 %collective-permute-start.7 = (f32[72,128]{0,1:T(8,128)S(1)}, f32[72,128]{0,1:T(8,128)S(1)}, u32[]{:S(2)}, u32[]{:S(2)}) collective-permute-start(f32[72,128]{0,1:T(8,128)S(1)} %add_select_fusion.1), channel_id=1, source_target_pairs={{0,4},{2,6},{4,0},{6,2},{1,5},{3,7},{5,1},{7,3},{8,12},{10,14},{12... | collective-permute-start | bytes 110600 | tf_op jit(solution)/shard_map/ppermute | solution.py:34
  58.2 2.7 %collective-permute-start.9 = (f32[72,128]{0,1:T(8,128)S(1)}, f32[72,128]{0,1:T(8,128)S(1)}, u32[]{:S(2)}, u32[]{:S(2)}) collective-permute-start(f32[72,128]{0,1:T(8,128)S(1)} %add_select_fusion.1), channel_id=1, source_target_pairs={{0,6},{2,0},{4,2},{6,4},{1,7},{3,1},{5,3},{7,5},{8,14},{10,8},{12,... | collective-permute-start | bytes 110600 | tf_op jit(solution)/shard_map/ppermute | solution.py:34
  62.6 5.5 %q_keep.3 = (f32[4,35,8,128]{3,2,1,0:T(8,128)S(1)}, f32[4,35,8,128]{3,2,1,0:T(8,128)}) custom-call(s32[2]{0:T(128)S(1)} %pad_add_fusion.1.s_ref, bf16[128,224]{1,0:T(8,128)(2,1)S(1)} %get-tuple-element.16.lhs_ref, bf16[1,112,28672]{2,1,0:T(8,128)(2,1)} %d_ref.25, bf16[1,112,28672]{2,1,0:T(8,128)(2,1)} %e_ref.25, ...), custom_call_target="tpu_custom_call" | custom-call | flops 256901120 | bytes 4300800 | tf_op jit(solution)/shard_map/q_keep/pallas_call | solution.py:165
  68.1 5.5 %q_keep.4 = (f32[4,35,8,128]{3,2,1,0:T(8,128)S(1)}, f32[4,35,8,128]{3,2,1,0:T(8,128)}) custom-call(s32[2]{0:T(128)S(1)} %pad_add_fusion.3.s_ref, bf16[128,224]{1,0:T(8,128)(2,1)S(1)} %get-tuple-element.16.lhs_ref, bf16[1,112,28672]{2,1,0:T(8,128)(2,1)} %d_ref.25, bf16[1,112,28672]{2,1,0:T(8,128)(2,1)} %e_ref.25, ...), custom_call_target="tpu_custom_call" | custom-call | flops 256901120 | bytes 4300800 | tf_op jit(solution)/shard_map/q_keep/pallas_call | solution.py:165
  74.0 4.9 %q_keep.5 = (f32[4,42,8,128]{3,2,1,0:T(8,128)S(1)}, f32[4,42,8,128]{3,2,1,0:T(8,128)S(1)}) custom-call(s32[2]{0:T(128)S(1)} %pad_add_fusion.5.s_ref, bf16[128,224]{1,0:T(8,128)(2,1)S(1)} %get-tuple-element.16.lhs_ref, bf16[1,112,28672]{2,1,0:T(8,128)(2,1)} %d_ref.25, bf16[1,112,28672]{2,1,0:T(8,128)(2,1)} %e_ref.25, ...), custom_call_target="tpu_custom_call" | custom-call | flops 308281344 | bytes 5160960 | tf_op jit(solution)/shard_map/q_keep/pallas_call | solution.py:165
  82.4 3.6 %collective-permute-done.15 = f32[4,35,8,128]{3,2,1,0:T(8,128)} collective-permute-done((f32[4,35,8,128]{3,2,1,0:T(8,128)}, f32[4,35,8,128]{3,2,1,0:T(8,128)}, u32[]{:S(2)}, u32[]{:S(2)}) %collective-permute-start.15) | collective-permute-done | bytes 573472 | tf_op jit(solution)/shard_map/ppermute | solution.py:38
  88.0 4.2 %collective-permute-done.12 = f32[2,35,8,128]{3,2,1,0:T(8,128)} collective-permute-done((f32[2,35,8,128]{3,2,1,0:T(8,128)}, f32[2,35,8,128]{3,2,1,0:T(8,128)}, u32[]{:S(2)}, u32[]{:S(2)}) %collective-permute-start.12) | collective-permute-done | bytes 286752 | tf_op jit(solution)/shard_map/ppermute | solution.py:38
  94.5 4.5 %collective-permute-done.16 = f32[2,35,8,128]{3,2,1,0:T(8,128)} collective-permute-done((f32[2,35,8,128]{3,2,1,0:T(8,128)}, f32[2,35,8,128]{3,2,1,0:T(8,128)}, u32[]{:S(2)}, u32[]{:S(2)}) %collective-permute-start.16) | collective-permute-done | bytes 286752 | tf_op jit(solution)/shard_map/ppermute | solution.py:38
  108.7 11.3 %all-to-all-start = ((f32[112,8,128]{2,1,0:T(8,128)}), f32[112,8,128]{2,1,0:T(8,128)S(1)}, u32[]{:S(2)}, u32[]{:S(2)}) async-start(f32[112,8,128]{2,1,0:T(8,128)} %pad_maximum_fusion), calls=%async_computation | async-start | bytes 917504 | tf_op jit(solution)/shard_map/all_to_all | solution.py:328
  120.3 5.9 %cholesky.17 = f32[64,64]{1,0:T(8,128)S(1)} custom-call(f32[64,64]{1,0:T(8,128)S(1)} %fusion.7), custom_call_target="Cholesky" | custom-call | tf_op jit(solution)/shard_map/jit(cholesky)/cholesky | solution.py:332
  126.2 5.3 %all-to-all-done = f32[112,8,128]{2,1,0:T(8,128)S(1)} async-done(((f32[112,8,128]{2,1,0:T(8,128)}), f32[112,8,128]{2,1,0:T(8,128)S(1)}, u32[]{:S(2)}, u32[]{:S(2)}) %all-to-all-start) | async-done | bytes 458784 | tf_op jit(solution)/shard_map/all_to_all | solution.py:328
  131.5 39.7 %all_gather.3 = f32[112,8,128]{2,1,0:T(8,128)S(1)} all-gather(f32[14,8,128]{2,1,0:T(8,128)S(1)} %reduce_sum.9), channel_id=1, replica_groups=mesh['zh'=2,'zl'=2,'xh'=2,'xl'=2,'yh'=2,'yl'=2,'c'=2] {'zh','xh','yh'}, dimensions={0}, use_global_device_ids=true | all-gather | bytes 516096 | tf_op jit(solution)/shard_map/all_gather | solution.py:339
  172.2 4.0 %collective-permute-done.28 = f32[1,42,8,128]{3,2,1,0:T(8,128)S(1)} collective-permute-done((f32[1,42,8,128]{3,2,1,0:T(8,128)S(1)}, f32[1,42,8,128]{3,2,1,0:T(8,128)S(1)}, u32[]{:S(2)}, u32[]{:S(2)}) %collective-permute-start.28) | collective-permute-done | bytes 172064 | tf_op jit(solution)/shard_map/ppermute | solution.py:38
  178.5 4.2 %collective-permute-done.29 = f32[2,42,8,128]{3,2,1,0:T(8,128)S(1)} collective-permute-done((f32[2,42,8,128]{3,2,1,0:T(8,128)S(1)}, f32[2,42,8,128]{3,2,1,0:T(8,128)S(1)}, u32[]{:S(2)}, u32[]{:S(2)}) %collective-permute-start.29) | collective-permute-done | bytes 344096 | tf_op jit(solution)/shard_map/ppermute | solution.py:38
  184.0 16.1 %collective-permute-start.31 = (f32[4,35,8,128]{3,2,1,0:T(8,128)S(1)}, f32[4,35,8,128]{3,2,1,0:T(8,128)}, u32[]{:S(2)}, u32[]{:S(2)}) collective-permute-start(f32[4,35,8,128]{3,2,1,0:T(8,128)S(1)} %maximum_select_fusion.1.refs_0_.a_ref), channel_id=1, source_target_pairs={{0,1},{1,0},{2,3},{3,2},{4,5},{5,4},{6,7},{7,6},{8,9},{9,8},{10,11... | collective-permute-start | bytes 1720328 | tf_op jit(solution)/shard_map/ppermute | solution.py:38
  201.7 4.9 %custom-call.7 = f32[1,64,64]{1,2,0:T(8,128)S(1)} custom-call(f32[1,64,64]{2,1,0:T(8,128)S(1)} %fusion.3), custom_call_target="InvertDiagBlocksLowerTriangular" | custom-call | tf_op jit(solution)/shard_map/jit(_solve_triangular)/triangular_solve | solution.py:333
  209.5 4.2 %collective-permute-done.27.refs_3_.b_ref = f32[4,35,8,128]{3,2,1,0:T(8,128)} collective-permute-done((f32[4,35,8,128]{3,2,1,0:T(8,128)S(1)}, f32[4,35,8,128]{3,2,1,0:T(8,128)}, u32[]{:S(2)}, u32[]{:S(2)}) %collective-permute-start.27) | collective-permute-done | bytes 573472 | tf_op jit(solution)/shard_map/ppermute | solution.py:38
  216.3 5.5 %new_error.6.rest_0_ = bf16[1,112,28672]{2,1,0:T(8,128)(2,1)} custom-call(s32[2]{0:T(128)S(1)} %pad_add_fusion.1.s_ref, bf16[112,192]{1,0:T(8,128)(2,1)S(1)} %pad_maximum_fusion.1.w_ref, f32[4,35,8,128]{3,2,1,0:T(8,128)S(1)} %maximum_select_fusion.1.refs_0_.a_ref, f32[4,35,8,128]{3,2,1,0:T(8,128)} %collective-permute-done.24.refs_1_.b_ref, ...), custom_call_target="tpu_custom_call" | custom-call | flops 192675840 | bytes 4157440 | tf_op jit(solution)/shard_map/new_error/pallas_call | solution.py:223
  221.7 5.5 %new_error.7.rest_0_ = bf16[1,112,28672]{2,1,0:T(8,128)(2,1)} custom-call(s32[2]{0:T(128)S(1)} %pad_add_fusion.3.s_ref, bf16[112,192]{1,0:T(8,128)(2,1)S(1)} %pad_maximum_fusion.1.w_ref, f32[4,35,8,128]{3,2,1,0:T(8,128)S(1)} %maximum_select_fusion.2.refs_2_.a_ref, ...), custom_call_target="tpu_custom_call", output_to_operand_aliasing={{}: (6, {})} | custom-call | flops 192675840 | bytes 4157440 | tf_op jit(solution)/shard_map/new_error/pallas_call | solution.py:223
  227.2 6.0 %new_error.8.rest_0_ = bf16[1,112,28672]{2,1,0:T(8,128)(2,1)} custom-call(s32[2]{0:T(128)S(1)} %pad_add_fusion.5.s_ref, bf16[112,192]{1,0:T(8,128)(2,1)S(1)} %pad_maximum_fusion.1.w_ref, f32[4,42,8,128]{3,2,1,0:T(8,128)S(1)} %maximum_select_fusion.refs_4_.a_ref, ...), custom_call_target="tpu_custom_call", output_to_operand_aliasing={{}: (6, {})} | custom-call | flops 231211008 | bytes 4988928 | tf_op jit(solution)/shard_map/new_error/pallas_call | solution.py:223
  233.2 5.6 %new_error.9.rest_0_ = bf16[1,112,28672]{2,1,0:T(8,128)(2,1)} custom-call(s32[2]{0:T(128)S(1)} %pad_add_fusion.s_ref, bf16[112,192]{1,0:T(8,128)(2,1)S(1)} %pad_maximum_fusion.1.w_ref, f32[4,35,8,128]{3,2,1,0:T(8,128)} %collective-permute-done.31.refs_6_.a_ref, ...), custom_call_target="tpu_custom_call", output_to_operand_aliasing={{}: (6, {})} | custom-call | flops 192675840 | bytes 4157440 | tf_op jit(solution)/shard_map/new_error/pallas_call | solution.py:223
  238.9 5.7 %new_error.10.rest_0_ = bf16[1,112,28672]{2,1,0:T(8,128)(2,1)} custom-call(s32[2]{0:T(128)S(1)} %pad_add_fusion.2.s_ref, bf16[112,192]{1,0:T(8,128)(2,1)S(1)} %pad_maximum_fusion.1.w_ref, f32[4,35,8,128]{3,2,1,0:T(8,128)} %collective-permute-done.33.refs_8_.a_ref, ...), custom_call_target="tpu_custom_call", output_to_operand_aliasing={{}: (6, {})} | custom-call | flops 192675840 | bytes 4157440 | tf_op jit(solution)/shard_map/new_error/pallas_call | solution.py:223
  244.5 6.1 %new_error.11 = bf16[1,112,28672]{2,1,0:T(8,128)(2,1)} custom-call(s32[2]{0:T(128)S(1)} %pad_add_fusion.4.s_ref, bf16[112,192]{1,0:T(8,128)(2,1)S(1)} %pad_maximum_fusion.1.w_ref, f32[4,42,8,128]{3,2,1,0:T(8,128)S(1)} %collective-permute-done.35.refs_10_.a_ref, ...), custom_call_target="tpu_custom_call", output_to_operand_aliasing={{}: (6, {})} | custom-call | flops 231211008 | bytes 4988928 | tf_op jit(solution)/shard_map/new_error/pallas_call | solution.py:223
  250.6 4.9 %outer_update.1 = (f32[112,1792]{1,0:T(8,128)}, f32[112,1792]{1,0:T(8,128)}) custom-call(s32[5]{0:T(128)S(1)} %stack.55.s_ref, bf16[112,192]{1,0:T(8,128)(2,1)S(1)} %pad_maximum_fusion.1.w_ref, f32[4,35,8,128]{3,2,1,0:T(8,128)S(1)} %maximum_select_fusion.1.refs_0_.a_ref, f32[4,35,8,128]{3,2,1,0:T(8,128)} %collective-permute-done.24.refs_1_.b_ref, ...), custom_call_target="tpu_custom_call" | custom-call | tf_op jit(solution)/shard_map/outer_update/pallas_call | solution.py:276
  (123 shorter events, 44.9 us)
Async XLA Ops:
  15.1 6.3 %collective-permute-start = (f32[120,128]{1,0:T(8,128)S(1)}, f32[120,128]{1,0:T(8,128)S(1)}, u32[]{:S(2)}, u32[]{:S(2)}) collective-permute-start(f32[120,128]{1,0:T(8,128)S(1)} %left_factor.1), channel_id=1, source_target_pairs={{0,16},{8,24},{16,0},{24,8},{1,17},{9,25},{17,1},{25,9},{2,18},{10... | collective-permute-start | bytes 184328 | tf_op jit(solution)/shard_map/ppermute | solution.py:34
  23.1 6.4 %collective-permute-start.3 = (f32[120,128]{1,0:T(8,128)S(1)}, f32[120,128]{1,0:T(8,128)S(1)}, u32[]{:S(2)}, u32[]{:S(2)}) collective-permute-start(f32[120,128]{1,0:T(8,128)S(1)} %add_add_fusion.a_ref), channel_id=1, source_target_pairs={{0,64},{32,96},{64,0},{96,32},{1,65},{33,97},{65,1},{97,33},{2,66}... | collective-permute-start | bytes 184328 | tf_op jit(solution)/shard_map/ppermute | solution.py:34
  26.7 4.6 %collective-permute-start.4 = (f32[120,128]{1,0:T(8,128)S(1)}, f32[120,128]{1,0:T(8,128)S(1)}, u32[]{:S(2)}, u32[]{:S(2)}) collective-permute-start(f32[120,128]{1,0:T(8,128)S(1)} %add_add_fusion.a_ref), channel_id=1, source_target_pairs={{0,32},{32,64},{64,96},{96,0},{1,33},{33,65},{65,97},{97,1},{2,34}... | collective-permute-start | bytes 184328 | tf_op jit(solution)/shard_map/ppermute | solution.py:34
  36.9 25.6 %collective-permute-start.10 = (f32[8,35,8,128]{3,2,1,0:T(8,128)}, f32[8,35,8,128]{3,2,1,0:T(8,128)}, u32[]{:S(2)}, u32[]{:S(2)}) collective-permute-start(f32[8,35,8,128]{3,2,1,0:T(8,128)} %q_send.3), channel_id=1, source_target_pairs={{0,1},{1,0},{2,3},{3,2},{4,5},{5,4},{6,7},{7,6},{8,9},{9,8},{10,11... | collective-permute-start | bytes 3440648 | tf_op jit(solution)/shard_map/ppermute | solution.py:38
  45.0 29.0 %collective-permute-start.18 = (f32[8,42,8,128]{3,2,1,0:T(8,128)S(1)}, f32[8,42,8,128]{3,2,1,0:T(8,128)S(1)}, u32[]{:S(2)}, u32[]{:S(2)}) collective-permute-start(f32[8,42,8,128]{3,2,1,0:T(8,128)S(1)} %q_send.5), channel_id=1, source_target_pairs={{0,1},{1,0},{2,3},{3,2},{4,5},{5,4},{6,7},{7,6},{8,9},{9,8},{10,11... | collective-permute-start | bytes 4128776 | tf_op jit(solution)/shard_map/ppermute | solution.py:38
  50.4 17.7 %collective-permute-start.14 = (f32[8,35,8,128]{3,2,1,0:T(8,128)}, f32[8,35,8,128]{3,2,1,0:T(8,128)}, u32[]{:S(2)}, u32[]{:S(2)}) collective-permute-start(f32[8,35,8,128]{3,2,1,0:T(8,128)} %q_send.4), channel_id=1, source_target_pairs={{0,1},{1,0},{2,3},{3,2},{4,5},{5,4},{6,7},{7,6},{8,9},{9,8},{10,11... | collective-permute-start | bytes 3440648 | tf_op jit(solution)/shard_map/ppermute | solution.py:38
  53.5 4.7 %collective-permute-start.7 = (f32[72,128]{0,1:T(8,128)S(1)}, f32[72,128]{0,1:T(8,128)S(1)}, u32[]{:S(2)}, u32[]{:S(2)}) collective-permute-start(f32[72,128]{0,1:T(8,128)S(1)} %add_select_fusion.1), channel_id=1, source_target_pairs={{0,4},{2,6},{4,0},{6,2},{1,5},{3,7},{5,1},{7,3},{8,12},{10,14},{12... | collective-permute-start | bytes 110600 | tf_op jit(solution)/shard_map/ppermute | solution.py:34
  68.1 12.4 %collective-permute-start.11 = (f32[4,35,8,128]{3,2,1,0:T(8,128)}, f32[4,35,8,128]{3,2,1,0:T(8,128)}, u32[]{:S(2)}, u32[]{:S(2)}) collective-permute-start(f32[4,35,8,128]{3,2,1,0:T(8,128)} %get-tuple-element.18), channel_id=1, source_target_pairs={{0,8},{8,0},{1,9},{9,1},{2,10},{10,2},{3,11},{11,3},{4,12},{12,4},... | collective-permute-start | bytes 1720328 | tf_op jit(solution)/shard_map/ppermute | solution.py:38
  73.7 12.4 %collective-permute-start.15 = (f32[4,35,8,128]{3,2,1,0:T(8,128)}, f32[4,35,8,128]{3,2,1,0:T(8,128)}, u32[]{:S(2)}, u32[]{:S(2)}) collective-permute-start(f32[4,35,8,128]{3,2,1,0:T(8,128)} %get-tuple-element.20), channel_id=1, source_target_pairs={{0,2},{2,0},{1,3},{3,1},{4,6},{6,4},{5,7},{7,5},{8,10},{10,8},{9,1... | collective-permute-start | bytes 1720328 | tf_op jit(solution)/shard_map/ppermute | solution.py:38
  79.0 14.3 %collective-permute-start.19 = (f32[4,42,8,128]{3,2,1,0:T(8,128)S(1)}, f32[4,42,8,128]{3,2,1,0:T(8,128)S(1)}, u32[]{:S(2)}, u32[]{:S(2)}) collective-permute-start(f32[4,42,8,128]{3,2,1,0:T(8,128)S(1)} %get-tuple-element.22), channel_id=1, source_target_pairs={{0,32},{32,0},{1,33},{33,1},{2,34},{34,2},{3,35},{35,3},{4,36},{36... | collective-permute-start | bytes 2064392 | tf_op jit(solution)/shard_map/ppermute | solution.py:38
  82.4 9.8 %collective-permute-start.12 = (f32[2,35,8,128]{3,2,1,0:T(8,128)}, f32[2,35,8,128]{3,2,1,0:T(8,128)}, u32[]{:S(2)}, u32[]{:S(2)}) collective-permute-start(f32[2,35,8,128]{3,2,1,0:T(8,128)} %get-tuple-element.31), channel_id=1, source_target_pairs={{0,2},{2,0},{1,3},{3,1},{4,6},{6,4},{5,7},{7,5},{8,10},{10,8},{9,1... | collective-permute-start | bytes 860168 | tf_op jit(solution)/shard_map/ppermute | solution.py:38
  87.9 11.2 %collective-permute-start.16 = (f32[2,35,8,128]{3,2,1,0:T(8,128)}, f32[2,35,8,128]{3,2,1,0:T(8,128)}, u32[]{:S(2)}, u32[]{:S(2)}) collective-permute-start(f32[2,35,8,128]{3,2,1,0:T(8,128)} %get-tuple-element.33), channel_id=1, source_target_pairs={{0,32},{32,0},{1,33},{33,1},{2,34},{34,2},{3,35},{35,3},{4,36},{36... | collective-permute-start | bytes 860168 | tf_op jit(solution)/shard_map/ppermute | solution.py:38
  93.1 9.1 %collective-permute-start.13 = (f32[1,35,8,128]{3,2,1,0:T(8,128)S(1)}, f32[1,35,8,128]{3,2,1,0:T(8,128)S(1)}, u32[]{:S(2)}, u32[]{:S(2)}) collective-permute-start(f32[1,35,8,128]{3,2,1,0:T(8,128)S(1)} %dynamic-slice_add_fusion.8), channel_id=1, source_target_pairs={{0,32},{32,0},{1,33},{33,1},{2,34},{34,2},{3,35},{35,3},{4,36},{36... | collective-permute-start | bytes 430088 | tf_op jit(solution)/shard_map/ppermute | solution.py:38
  93.3 9.9 %collective-permute-start.20 = (f32[2,42,8,128]{3,2,1,0:T(8,128)S(1)}, f32[2,42,8,128]{3,2,1,0:T(8,128)S(1)}, u32[]{:S(2)}, u32[]{:S(2)}) collective-permute-start(f32[2,42,8,128]{3,2,1,0:T(8,128)S(1)} %get-tuple-element.29), channel_id=1, source_target_pairs={{0,8},{8,0},{1,9},{9,1},{2,10},{10,2},{3,11},{11,3},{4,12},{12,4},... | collective-permute-start | bytes 1032200 | tf_op jit(solution)/shard_map/ppermute | solution.py:38
  100.0 4.9 %collective-permute-start.17 = (f32[1,35,8,128]{3,2,1,0:T(8,128)S(1)}, f32[1,35,8,128]{3,2,1,0:T(8,128)S(1)}, u32[]{:S(2)}, u32[]{:S(2)}) collective-permute-start(f32[1,35,8,128]{3,2,1,0:T(8,128)S(1)} %dynamic-slice_add_fusion.7), channel_id=1, source_target_pairs={{0,8},{8,0},{1,9},{9,1},{2,10},{10,2},{3,11},{11,3},{4,12},{12,4},... | collective-permute-start | bytes 430088 | tf_op jit(solution)/shard_map/ppermute | solution.py:38
  103.2 4.6 %collective-permute-start.21 = (f32[1,42,8,128]{3,2,1,0:T(8,128)S(1)}, f32[1,42,8,128]{3,2,1,0:T(8,128)S(1)}, u32[]{:S(2)}, u32[]{:S(2)}) collective-permute-start(f32[1,42,8,128]{3,2,1,0:T(8,128)S(1)} %dynamic-slice_add_fusion.6), channel_id=1, source_target_pairs={{0,2},{2,0},{1,3},{3,1},{4,6},{6,4},{5,7},{7,5},{8,10},{10,8},{9,1... | collective-permute-start | bytes 516104 | tf_op jit(solution)/shard_map/ppermute | solution.py:38
  108.7 22.8 %all-to-all-start = ((f32[112,8,128]{2,1,0:T(8,128)}), f32[112,8,128]{2,1,0:T(8,128)S(1)}, u32[]{:S(2)}, u32[]{:S(2)}) async-start(f32[112,8,128]{2,1,0:T(8,128)} %pad_maximum_fusion), calls=%async_computation | async-start | bytes 917504 | tf_op jit(solution)/shard_map/all_to_all | solution.py:328
  171.3 4.9 %collective-permute-start.28 = (f32[1,42,8,128]{3,2,1,0:T(8,128)S(1)}, f32[1,42,8,128]{3,2,1,0:T(8,128)S(1)}, u32[]{:S(2)}, u32[]{:S(2)}) collective-permute-start(f32[1,42,8,128]{3,2,1,0:T(8,128)S(1)} %slice_bitcast_fusion), channel_id=1, source_target_pairs={{0,2},{2,0},{1,3},{3,1},{4,6},{6,4},{5,7},{7,5},{8,10},{10,8},{9,1... | collective-permute-start | bytes 516104 | tf_op jit(solution)/shard_map/ppermute | solution.py:38
  171.4 4.9 %collective-permute-start.22 = (f32[1,35,8,128]{3,2,1,0:T(8,128)S(1)}, f32[1,35,8,128]{3,2,1,0:T(8,128)S(1)}, u32[]{:S(2)}, u32[]{:S(2)}) collective-permute-start(f32[1,35,8,128]{3,2,1,0:T(8,128)S(1)} %get-tuple-element.35), channel_id=1, source_target_pairs={{0,32},{32,0},{1,33},{33,1},{2,34},{34,2},{3,35},{35,3},{4,36},{36... | collective-permute-start | bytes 430088 | tf_op jit(solution)/shard_map/ppermute | solution.py:38
  172.1 5.1 %collective-permute-start.25 = (f32[1,35,8,128]{3,2,1,0:T(8,128)S(1)}, f32[1,35,8,128]{3,2,1,0:T(8,128)S(1)}, u32[]{:S(2)}, u32[]{:S(2)}) collective-permute-start(f32[1,35,8,128]{3,2,1,0:T(8,128)S(1)} %get-tuple-element.34), channel_id=1, source_target_pairs={{0,8},{8,0},{1,9},{9,1},{2,10},{10,2},{3,11},{11,3},{4,12},{12,4},... | collective-permute-start | bytes 430088 | tf_op jit(solution)/shard_map/ppermute | solution.py:38
  176.2 6.5 %collective-permute-start.29 = (f32[2,42,8,128]{3,2,1,0:T(8,128)S(1)}, f32[2,42,8,128]{3,2,1,0:T(8,128)S(1)}, u32[]{:S(2)}, u32[]{:S(2)}) collective-permute-start(f32[2,42,8,128]{3,2,1,0:T(8,128)S(1)} %maximum_select_fusion.3), channel_id=1, source_target_pairs={{0,8},{8,0},{1,9},{9,1},{2,10},{10,2},{3,11},{11,3},{4,12},{12,4},... | collective-permute-start | bytes 1032200 | tf_op jit(solution)/shard_map/ppermute | solution.py:38
  176.4 7.1 %collective-permute-start.23 = (f32[2,35,8,128]{3,2,1,0:T(8,128)S(1)}, f32[2,35,8,128]{3,2,1,0:T(8,128)S(1)}, u32[]{:S(2)}, u32[]{:S(2)}) collective-permute-start(f32[2,35,8,128]{3,2,1,0:T(8,128)S(1)} %maximum_select_fusion.4), channel_id=1, source_target_pairs={{0,2},{2,0},{1,3},{3,1},{4,6},{6,4},{5,7},{7,5},{8,10},{10,8},{9,1... | collective-permute-start | bytes 860168 | tf_op jit(solution)/shard_map/ppermute | solution.py:38
  177.2 22.9 %collective-permute-start.26 = (f32[2,35,8,128]{3,2,1,0:T(8,128)S(1)}, f32[2,35,8,128]{3,2,1,0:T(8,128)S(1)}, u32[]{:S(2)}, u32[]{:S(2)}) collective-permute-start(f32[2,35,8,128]{3,2,1,0:T(8,128)S(1)} %maximum_select_fusion.5), channel_id=1, source_target_pairs={{0,32},{32,0},{1,33},{33,1},{2,34},{34,2},{3,35},{35,3},{4,36},{36... | collective-permute-start | bytes 860168 | tf_op jit(solution)/shard_map/ppermute | solution.py:38
  182.8 24.5 %collective-permute-start.30 = (f32[4,42,8,128]{3,2,1,0:T(8,128)S(1)}, f32[4,42,8,128]{3,2,1,0:T(8,128)S(1)}, u32[]{:S(2)}, u32[]{:S(2)}) collective-permute-start(f32[4,42,8,128]{3,2,1,0:T(8,128)S(1)} %maximum_select_fusion.refs_4_.a_ref), channel_id=1, source_target_pairs={{0,32},{32,0},{1,33},{33,1},{2,34},{34,2},{3,35},{35,3},{4,36},{36... | collective-permute-start | bytes 2064392 | tf_op jit(solution)/shard_map/ppermute | solution.py:38
  183.5 25.9 %collective-permute-start.24 = (f32[4,35,8,128]{3,2,1,0:T(8,128)S(1)}, f32[4,35,8,128]{3,2,1,0:T(8,128)}, u32[]{:S(2)}, u32[]{:S(2)}) collective-permute-start(f32[4,35,8,128]{3,2,1,0:T(8,128)S(1)} %maximum_select_fusion.1.refs_0_.a_ref), channel_id=1, source_target_pairs={{0,8},{8,0},{1,9},{9,1},{2,10},{10,2},{3,11},{11,3},{4,12},{12,4},... | collective-permute-start | bytes 1720328 | tf_op jit(solution)/shard_map/ppermute | solution.py:38
  184.0 31.7 %collective-permute-start.31 = (f32[4,35,8,128]{3,2,1,0:T(8,128)S(1)}, f32[4,35,8,128]{3,2,1,0:T(8,128)}, u32[]{:S(2)}, u32[]{:S(2)}) collective-permute-start(f32[4,35,8,128]{3,2,1,0:T(8,128)S(1)} %maximum_select_fusion.1.refs_0_.a_ref), channel_id=1, source_target_pairs={{0,1},{1,0},{2,3},{3,2},{4,5},{5,4},{6,7},{7,6},{8,9},{9,8},{10,11... | collective-permute-start | bytes 1720328 | tf_op jit(solution)/shard_map/ppermute | solution.py:38
  200.1 13.6 %collective-permute-start.27 = (f32[4,35,8,128]{3,2,1,0:T(8,128)S(1)}, f32[4,35,8,128]{3,2,1,0:T(8,128)}, u32[]{:S(2)}, u32[]{:S(2)}) collective-permute-start(f32[4,35,8,128]{3,2,1,0:T(8,128)S(1)} %maximum_select_fusion.2.refs_2_.a_ref), channel_id=1, source_target_pairs={{0,2},{2,0},{1,3},{3,1},{4,6},{6,4},{5,7},{7,5},{8,10},{10,8},{9,1... | collective-permute-start | bytes 1720328 | tf_op jit(solution)/shard_map/ppermute | solution.py:38
  206.9 37.7 %collective-permute-start.35 = (f32[4,42,8,128]{3,2,1,0:T(8,128)S(1)}, f32[4,42,8,128]{3,2,1,0:T(8,128)S(1)}, u32[]{:S(2)}, u32[]{:S(2)}) collective-permute-start(f32[4,42,8,128]{3,2,1,0:T(8,128)S(1)} %maximum_select_fusion.refs_4_.a_ref), channel_id=1, source_target_pairs={{0,1},{1,0},{2,3},{3,2},{4,5},{5,4},{6,7},{7,6},{8,9},{9,8},{10,11... | collective-permute-start | bytes 2064392 | tf_op jit(solution)/shard_map/ppermute | solution.py:38
  207.2 37.3 %collective-permute-start.36 = (f32[4,42,8,128]{3,2,1,0:T(8,128)S(1)}, f32[4,42,8,128]{3,2,1,0:T(8,128)}, u32[]{:S(2)}, u32[]{:S(2)}) collective-permute-start(f32[4,42,8,128]{3,2,1,0:T(8,128)S(1)} %collective-permute-done.30.refs_5_.b_ref), channel_id=1, source_target_pairs={{0,1},{1,0},{2,3},{3,2},{4,5},{5,4},{6,7},{7,6},{8,9},{9,8},{10,11... | collective-permute-start | bytes 2064392 | tf_op jit(solution)/shard_map/ppermute | solution.py:38
  209.4 29.4 %collective-permute-start.33 = (f32[4,35,8,128]{3,2,1,0:T(8,128)S(1)}, f32[4,35,8,128]{3,2,1,0:T(8,128)}, u32[]{:S(2)}, u32[]{:S(2)}) collective-permute-start(f32[4,35,8,128]{3,2,1,0:T(8,128)S(1)} %maximum_select_fusion.2.refs_2_.a_ref), channel_id=1, source_target_pairs={{0,1},{1,0},{2,3},{3,2},{4,5},{5,4},{6,7},{7,6},{8,9},{9,8},{10,11... | collective-permute-start | bytes 1720328 | tf_op jit(solution)/shard_map/ppermute | solution.py:38
  213.7 19.5 %collective-permute-start.32 = (f32[4,35,8,128]{3,2,1,0:T(8,128)}, f32[4,35,8,128]{3,2,1,0:T(8,128)}, u32[]{:S(2)}, u32[]{:S(2)}) collective-permute-start(f32[4,35,8,128]{3,2,1,0:T(8,128)} %collective-permute-done.24.refs_1_.b_ref), channel_id=1, source_target_pairs={{0,1},{1,0},{2,3},{3,2},{4,5},{5,4},{6,7},{7,6},{8,9},{9,8},{10,11... | collective-permute-start | bytes 1720328 | tf_op jit(solution)/shard_map/ppermute | solution.py:38
  215.7 23.2 %collective-permute-start.34 = (f32[4,35,8,128]{3,2,1,0:T(8,128)}, f32[4,35,8,128]{3,2,1,0:T(8,128)}, u32[]{:S(2)}, u32[]{:S(2)}) collective-permute-start(f32[4,35,8,128]{3,2,1,0:T(8,128)} %collective-permute-done.27.refs_3_.b_ref), channel_id=1, source_target_pairs={{0,1},{1,0},{2,3},{3,2},{4,5},{5,4},{6,7},{7,6},{8,9},{9,8},{10,11... | collective-permute-start | bytes 1720328 | tf_op jit(solution)/shard_map/ppermute | solution.py:38
  (12 other events, 90.2 us)

commit v2 on v0

v2 whole, which is shorter than its diff:
```python
import jax
import jax.numpy as jnp
from jax import lax
from jax.experimental import pallas as pl
from jax.experimental.pallas import tpu as pltpu
from jax.sharding import Mesh, PartitionSpec as P

outer_lr = 0.7
beta = 0.9

AXES = ("z", "x", "y", "c")
REP = ("z", "x")
ROW = ("y", "c")
ROUTES = (("x", "y", "z"), ("y", "z", "x"), ("z", "x", "y"))

HALF = 112
COUNTS = (37, 37, 38)
FIRST = (0, 37, 74)
BF = jnp.bfloat16
F32 = jnp.float32
HBM = pl.BlockSpec(memory_space=pltpu.HBM)
ANY = pl.BlockSpec(memory_space=pl.ANY)
VM = pl.BlockSpec(memory_space=pltpu.VMEM)
SM = pl.BlockSpec(memory_space=pltpu.SMEM)
DMA = pltpu.SemaphoreType.DMA


def params_of(mib=58):
    return pltpu.CompilerParams(vmem_limit_bytes=mib << 20)


def turn(x, axis, step):
    return lax.ppermute(x, axis, [(i, (i + step) % 4) for i in range(4)])


def low(x, axis):
    return lax.ppermute(x, axis, [(i, i ^ 1) for i in range(4)])


def high(x, axis):
    return lax.ppermute(x, axis, [(i, 3 - i) for i in range(4)])


def swap(x):
    return lax.ppermute(x, "c", [(0, 1), (1, 0)])


def start(src, dst, sem):
    copy = pltpu.make_async_copy(src, dst, sem)
    copy.start()
    return copy


P_BLOCK = 4096


def p_kernel(steps_ref, d_ref, e_ref, q_ref, out_ref, both_ref, qb_ref, sem):
    n = d_ref.shape[2] // P_BLOCK
    copies = []
    for i in range(n):
        cols = slice(i * P_BLOCK, (i + 1) * P_BLOCK)
        copies.append((
            start(d_ref.at[0, :, cols], both_ref.at[0:112, cols], sem.at[i, 0]),
            start(e_ref.at[0, :, cols], both_ref.at[112:224, cols], sem.at[i, 1]),
            start(q_ref.at[:, cols], qb_ref.at[:, cols], sem.at[i, 2]),
        ))
    acc_d = jnp.zeros((112, 64), F32)
    acc_e = jnp.zeros((112, 64), F32)
    dims = (((1,), (1,)), ((), ()))
    for i in range(n):
        cols = slice(i * P_BLOCK, (i + 1) * P_BLOCK)
        for copy in copies[i]:
            copy.wait()
        acc_d = acc_d + lax.dot_general(both_ref[0:112, cols], qb_ref[:, cols], dims, preferred_element_type=F32)
        acc_e = acc_e + lax.dot_general(both_ref[112:224, cols], qb_ref[:, cols], dims, preferred_element_type=F32)
    count = steps_ref[0].astype(F32)
    p = count * (acc_d + acc_e)
    out_ref[56:64, :] = jnp.full((8, 128), count, F32)
    out_ref[0:56, :] = jnp.concatenate([p[0:56], p[56:112]], axis=1)


def left_factor(delta, error, q_t, steps):
    width = delta.shape[2]
    return pl.pallas_call(
        p_kernel,
        in_specs=[SM, HBM, HBM, HBM],
        out_specs=VM,
        out_shape=jax.ShapeDtypeStruct((64, 128), F32),
        scratch_shapes=[
            pltpu.VMEM((224, width), BF),
            pltpu.VMEM((64, width), BF),
            DMA((width // P_BLOCK, 3)),
        ],
        compiler_params=params_of(),
        name="left_factor",
    )(steps, delta, error, q_t)


def prep_kernel(steps_ref, a_ref, b_ref, c_ref, d_ref, p_ref, lhs_ref, gram_ref):
    both = (a_ref[...] + b_ref[...]) + (c_ref[...] + d_ref[...])
    p = jnp.concatenate([both[0:56, 0:64], both[0:56, 64:128]], axis=0)
    total = both[56:57, 0:1]
    p_ref[...] = p
    top = jnp.max(jnp.abs(p), axis=0, keepdims=True)
    weight = steps_ref[0].astype(F32) / total
    unit = p * (1.0 / jnp.maximum(top, 1e-37)) * weight
    flat = unit.T
    upper = flat.astype(BF).astype(F32)
    rest = flat - upper
    lhs_ref[0:64, :] = jnp.concatenate([upper, upper], axis=1).astype(BF)
    lhs_ref[64:128, :] = jnp.concatenate([rest, rest], axis=1).astype(BF)
    gram_ref[...] = jnp.zeros_like(gram_ref)
    gram_ref[0:64, 0:64] = lax.dot_general(p, p, (((0,), (0,)), ((), ())), precision=lax.Precision.HIGHEST, preferred_element_type=F32)
    gram_ref[64:65, 0:64] = top


def prepare(steps, a, b, c, d):
    return pl.pallas_call(
        prep_kernel,
        in_specs=[SM, VM, VM, VM, VM],
        out_specs=[VM, VM, VM],
        out_shape=[
            jax.ShapeDtypeStruct((112, 64), F32),
            jax.ShapeDtypeStruct((128, 224), BF),
            jax.ShapeDtypeStruct((72, 128), F32),
        ],
        compiler_params=params_of(),
        name="prepare",
    )(steps, a, b, c, d)


def blocks_of(tiles):
    return [(i, i + tiles) for i in range(0, HALF, tiles)]


def columns(side, begin, end):
    return pl.ds(pl.multiple_of(side * (HALF * 128) + begin * 128, 128), (end - begin) * 128)


def load_block(side, s, begin, end, d_ref, e_ref, both_ref, sem):
    src = columns(side, begin, end)
    return [
        start(d_ref.at[0, :, src], both_ref.at[s, 0:112, :], sem.at[s, 0]),
        start(e_ref.at[0, :, src], both_ref.at[s, 112:224, :], sem.at[s, 1]),
    ]


def chunk_range(k):
    return slice(FIRST[k], FIRST[k] + COUNTS[k])


def q_half(where, lhs, delta, error, far):
    parts = blocks_of(28)
    n = len(parts)

    def kernel(s_ref, lhs_ref, d_ref, e_ref, *rest):
        out_refs, (both_ref, v_ref, sem, out_sem) = rest[:3], rest[3:]
        side = 1 - s_ref[0] if far else s_ref[0]
        copies = [load_block(side, s, *parts[s], d_ref, e_ref, both_ref, sem) for s in range(n)]
        outs = []
        for s, (begin, end) in enumerate(parts):
            for copy in copies[s]:
                copy.wait()
            r = lax.dot_general(lhs_ref[...], both_ref[s], (((1,), (0,)), ((), ())), preferred_element_type=F32)
            v = r[0:64] + r[64:128]
            for i in range(8):
                for t in range(end - begin):
                    v_ref[i, begin + t] = v[8 * i:8 * i + 8, 128 * t:128 * t + 128]
            while len(outs) < 3 and FIRST[len(outs)] + COUNTS[len(outs)] <= end:
                k = len(outs)
                outs.append(start(v_ref.at[:, chunk_range(k)], out_refs[k], out_sem.at[k]))
        for copy in outs:
            copy.wait()

    return pl.pallas_call(
        kernel,
        in_specs=[SM, VM, HBM, HBM],
        out_specs=[ANY] * 3,
        out_shape=[jax.ShapeDtypeStruct((8, c, 8, 128), F32) for c in COUNTS],
        scratch_shapes=[
            pltpu.VMEM((n, 224, 28 * 128), BF),
            pltpu.VMEM((8, HALF, 8, 128), F32),
            DMA((n, 2)),
            DMA((3,)),
        ],
        compiler_params=params_of(),
        cost_estimate=pl.CostEstimate(flops=2 * 128 * 224 * HALF * 128, bytes_accessed=HALF * 128 * (448 + 256), transcendentals=0),
        name="q_far" if far else "q_own",
    )(where, lhs, delta, error)


def scales_kernel(own_ref, near_ref, pair_ref, far_ref, both_ref, f_own_ref, f_near_ref):
    join = jnp.where(lax.broadcasted_iota(jnp.int32, (72, 128), 0) == 64, jnp.maximum(pair_ref[...], far_ref[...]), pair_ref[...] + far_ref[...])
    both_ref[...] = join
    eye = lax.broadcasted_iota(jnp.int32, (64, 64), 0) == lax.broadcasted_iota(jnp.int32, (64, 64), 1)
    top = jnp.maximum(join[64:65, 0:64], 1e-37)
    for src, dst in ((own_ref, f_own_ref), (near_ref, f_near_ref)):
        ratio = src[64:65, 0:64] / top
        column = jnp.sum(jnp.where(eye, ratio, 0.0), axis=1, keepdims=True)
        dst[...] = jnp.broadcast_to(column, (64, 128))


def scales(own, near, pair, far):
    return pl.pallas_call(
        scales_kernel,
        in_specs=[VM] * 4,
        out_specs=[VM] * 3,
        out_shape=[jax.ShapeDtypeStruct((72, 128), F32)] + [jax.ShapeDtypeStruct((64, 128), F32)] * 2,
        compiler_params=params_of(8),
        name="scales",
    )(own, near, pair, far)


def solve_kernel(gram_ref, p_ref, pass_in, w_ref, pass_out):
    highest = lax.Precision.HIGHEST
    row = lax.broadcasted_iota(jnp.int32, (64, 64), 0)
    lane = lax.broadcasted_iota(jnp.int32, (64, 64), 1)
    eye = (row == lane).astype(F32)
    inv_row = 1.0 / jnp.maximum(gram_ref[64:65, 0:64], 1e-37)
    inv_col = jnp.sum(eye * inv_row, axis=1, keepdims=True)
    unit = gram_ref[0:64, 0:64] * inv_col * inv_row
    m = jnp.concatenate([unit, eye], axis=1)
    below = lax.broadcasted_iota(jnp.int32, (64, 1), 0)
    for k in range(64):
        factor = jnp.where(below > k, m[:, k:k + 1], 0.0)
        m = m - factor * (m[k:k + 1, :] * (1.0 / m[k:k + 1, k:k + 1]))
    pivots = jnp.sum(eye * m[:, 0:64], axis=1, keepdims=True)
    inverse = m[:, 64:128] * (1.0 / jnp.sqrt(pivots))
    p_hat = lax.dot_general(p_ref[...] * inv_row, inverse, (((1,), (1,)), ((), ())), precision=highest, preferred_element_type=F32)
    w = lax.dot_general(p_hat, inverse, (((1,), (0,)), ((), ())), precision=highest, preferred_element_type=F32)
    upper = w.astype(BF).astype(F32)
    w_ref[...] = jnp.concatenate([upper, upper, w - upper], axis=1).astype(BF)


def solve(gram, p, through):
    return pl.pallas_call(
        solve_kernel,
        in_specs=[VM, VM, ANY],
        out_specs=[VM, ANY],
        out_shape=[jax.ShapeDtypeStruct((112, 192), BF), jax.ShapeDtypeStruct(through.shape, F32)],
        input_output_aliases={2: 1},
        compiler_params=params_of(8),
        cost_estimate=pl.CostEstimate(flops=10 ** 7, bytes_accessed=10 ** 7, transcendentals=0),
        name="solve",
    )(gram, p, through)


def finish(where, w, sides, delta, error, params, momentum, base, far):
    parts = blocks_of(14)
    n = len(parts)
    wide = 14 * 128
    given = len(base)

    def kernel(s_ref, w_ref, *rest):
        q_refs, (d_ref, e_ref, par_ref, mom_ref), rest = rest[:6], rest[6:10], rest[10 + given:]
        err_ref, np_ref, nm_ref, both_ref, q_ref, new_ref, pb_ref, mb_ref, po_ref, mo_ref, sem, q_sem, out_sem, par_sem = rest
        side = 1 - s_ref[0] if far else s_ref[0]
        turn_of = s_ref[4] - 8 * side
        mine = (turn_of >= 0) & (turn_of < 8)

        q_copies, copies = [], []
        for s in range(n):
            copies.append(load_block(side, s, *parts[s], d_ref, e_ref, both_ref, sem))
            k = len(q_copies)
            if k < 3 and s % 2 == 0:
                bit = s_ref[1 + k]
                q_copies.append([
                    start(q_refs[2 * k], q_ref.at[pl.ds(bit * 4, 4), chunk_range(k)], q_sem.at[k, 0]),
                    start(q_refs[2 * k + 1], q_ref.at[pl.ds((1 - bit) * 4, 4), chunk_range(k)], q_sem.at[k, 1]),
                ])

        @pl.when(mine)
        def _():
            start(par_ref, pb_ref, par_sem.at[0])
            start(mom_ref, mb_ref, par_sem.at[1])

        outs = []
        for s, (begin, end) in enumerate(parts):
            while q_copies and FIRST[3 - len(q_copies)] < end:
                for copy in q_copies.pop(0):
                    copy.wait()
            for copy in copies[s]:
                copy.wait()
            q = jnp.concatenate([jnp.concatenate([q_ref[i, t] for t in range(begin, end)], axis=1) for i in range(8)], axis=0)
            upper = q.astype(BF)
            below = (q - upper.astype(F32)).astype(BF)
            rhs = jnp.concatenate([upper, below, upper], axis=0)
            approx = lax.dot_general(w_ref[...], rhs, (((1,), (0,)), ((), ())), preferred_element_type=F32)
            merged = both_ref[s, 0:112, :].astype(F32) + both_ref[s, 112:224, :].astype(F32)
            new_ref[s] = (merged - approx).astype(BF)
            outs.append(start(new_ref.at[s], err_ref.at[0, :, columns(side, begin, end)], out_sem.at[s]))

            @pl.when(turn_of == s)
            def _():
                pltpu.make_async_copy(par_ref, pb_ref, par_sem.at[0]).wait()
                pltpu.make_async_copy(mom_ref, mb_ref, par_sem.at[1]).wait()
                fresh = beta * mb_ref[...] + approx
                mo_ref[...] = fresh
                po_ref[...] = pb_ref[...] - outer_lr * (approx + beta * fresh)
                start(po_ref, np_ref, par_sem.at[2])
                start(mo_ref, nm_ref, par_sem.at[3])

        for copy in outs:
            copy.wait()

        @pl.when(mine)
        def _():
            pltpu.make_async_copy(po_ref, np_ref, par_sem.at[2]).wait()
            pltpu.make_async_copy(mo_ref, nm_ref, par_sem.at[3]).wait()

    panel = pltpu.VMEM((112, wide), F32)
    return pl.pallas_call(
        kernel,
        in_specs=[SM, VM] + [ANY] * 6 + [HBM] * (4 + given),
        out_specs=[HBM, HBM, HBM],
        out_shape=[
            jax.ShapeDtypeStruct(delta.shape, BF),
            jax.ShapeDtypeStruct(params.shape, F32),
            jax.ShapeDtypeStruct(params.shape, F32),
        ],
        input_output_aliases={12 + i: i for i in range(given)},
        scratch_shapes=[
            pltpu.VMEM((n, 224, wide), BF),
            pltpu.VMEM((8, HALF, 8, 128), F32),
            pltpu.VMEM((n, 112, wide), BF),
            panel, panel, panel, panel,
            DMA((n, 2)),
            DMA((3, 2)),
            DMA((n,)),
            DMA((4,)),
        ],
        compiler_params=params_of(),
        cost_estimate=pl.CostEstimate(flops=2 * 112 * 192 * HALF * 128, bytes_accessed=HALF * 128 * (672 + 256), transcendentals=0),
        name="finish_far" if far else "finish_own",
    )(where, w, *sides, delta, error, params, momentum, *base)


def local(delta, error, steps, q_start, params, momentum):
    place = {a: lax.axis_index(a) for a in AXES}
    core = place["c"]
    hi_bit = {a: place[a] // 2 for a in REP + ("y",)}
    lo_bit = {a: (place[a] + place[a] // 2) % 2 for a in REP + ("y",)}
    where = jnp.stack([core] + [lo_bit[r[0]] for r in ROUTES] + [lax.axis_index(REP)])

    own = left_factor(delta, error, q_start.T, steps)
    own = (own + turn(own, "x", 2)) + (turn(own, "x", 1) + turn(own, "x", 3))
    p_all, lhs, gram_own = prepare(steps, own, turn(own, "z", 2), turn(own, "z", 1), turn(own, "z", 3))

    row64 = lax.broadcasted_iota(jnp.int32, gram_own.shape, 0) == 64
    join = lambda a, b: jnp.where(row64, jnp.maximum(a, b), a + b)
    gram_near = swap(gram_own)
    chip = join(gram_own, gram_near)
    pair = join(chip, low(chip, "y"))
    both, f_own, f_near = scales(gram_own, gram_near, pair, high(pair, "y"))
    f_own, f_near = f_own.reshape(8, 1, 8, 128), f_near.reshape(8, 1, 8, 128)

    arrived = [swap(v) for v in q_half(where, lhs, delta, error, True)]
    terms = q_half(where, lhs, delta, error, False)
    half = lambda x, b: lax.dynamic_slice_in_dim(x, b * (x.shape[0] // 2), x.shape[0] // 2, 0)
    parts = []
    for k, route in enumerate(ROUTES):
        blend = lambda b: half(terms[k], b) * half(f_own, b) + half(arrived[k], b) * half(f_near, b)
        bit = lo_bit[route[0]]
        send, keep = blend(1 - bit), blend(bit)
        got = low(send, route[0])
        if k == 2:
            w_cat, keep = solve(both, p_all, keep)
        for d in route[1:]:
            take = lambda b: half(keep, b) + half(got, b)
            send, keep = take(1 - lo_bit[d]), take(lo_bit[d])
            got = low(send, d)
        parts.append(keep[0] + got[0])
    mine = jnp.concatenate(parts, axis=0)
    mine = half(mine, hi_bit["y"]) + high(half(mine, 1 - hi_bit["y"]), "y")
    quarter = lambda a, b: lax.dynamic_slice_in_dim(mine, (2 * a + b) * 14, 14, 0)
    hz, hx = hi_bit["z"], hi_bit["x"]
    both_high = lambda x: lax.ppermute(x, REP, [(4 * i + j, 4 * (3 - i) + 3 - j) for i in range(4) for j in range(4)])
    mine = (quarter(hz, hx) + both_high(quarter(1 - hz, 1 - hx))) + (high(quarter(1 - hz, hx), "z") + high(quarter(hz, 1 - hx), "x"))

    def in_order(bit, a, b):
        return jnp.where(bit == 0, jnp.concatenate([a, b], 0), jnp.concatenate([b, a], 0))

    across = {0: mine, 1: high(mine, "x"), 2: high(mine, "z"), 3: both_high(mine)}
    by_x = [in_order(hx, across[m], across[m + 1]) for m in (0, 2)]
    mine = in_order(hz, *by_x)
    mine = in_order(hi_bit["y"], mine, high(mine, "y"))
    sides = []
    for k, route in enumerate(ROUTES):
        v = mine[chunk_range(k)][None]
        for d in route[:0:-1]:
            v = in_order(lo_bit[d], v, low(v, d))
        sides.append((v, low(v, route[0])))
    far = [swap(x) for pair in sides for x in pair]
    near = [x for pair in sides for x in pair]
    base = finish(where, w_cat, near, delta, error, params, momentum, (), False)
    base = finish(where, w_cat, far, delta, error, params, momentum, base, True)
    error_new, params_new, momentum_new = base
    return (params_new, momentum_new, error_new)


def solution(mesh):
    fine = Mesh(mesh.devices.reshape(4, 4, 4, 2), AXES)
    in_specs = (
        P(REP, ROW, None),
        P(REP, ROW, None),
        P(REP),
        P(),
        P(ROW, REP),
        P(ROW, REP),
    )
    out_specs = (P(ROW, REP), P(ROW, REP), P(REP, ROW, None))
    return jax.shard_map(local, mesh=fine, in_specs=in_specs, out_specs=out_specs, check_vma=False)
```

time: 333 us -> 179 us (0.54)
  blocking collectives: 98.9 us -> 0 us
  waiting for transfers between devices: 156 us -> 60 us
  starting transfers between devices: 0.04 us -> 56.2 us
  Pallas kernels: 0 us -> 43.7 us
  matrix products: 39.8 us -> 0 us
  between operations: 15.4 us -> 2.02 us
  other arithmetic: 22.4 us -> 12.5 us
  local copies, waits for them, and re-layouts: 0.09 us -> 3.61 us
    psum x1 -> x0, waiting for transfers between devices: 156 us -> none  [local(): q_new = lax.psum(q_term, ('rep', 'row'))]
    psum x2 -> x0, blocking collectives: 98.9 us -> none  [the longest x1 64 us: local(): p_local, summed_counts = lax.psum((p_term, counts), 'rep')]
    ppermute x0 -> x44, waiting for transfers between devices: none -> 60 us  [the longest x19 31.4 us: low(): return lax.ppermute(x, axis, [(i, i ^ 1) for i in range(4)])]
    ppermute x0 -> x44, starting transfers between devices: none -> 56.2 us  [the longest x10 25 us: swap(): return lax.ppermute(x, 'c', [(0, 1), (1, 0)])]
    pallas_call x0 -> x8, Pallas kernels: none -> 43.7 us  [the longest x2 15.7 us: finish(): pl.pallas_call(kernel, in_specs=[SM, VM] + [ANY] * 6 + [HBM] * (4 + given...]
    dot_general x4 -> x0, matrix products: 39.5 us -> none  [the longest x1 14.1 us: local(): lax.dot_general(merged, p_hat, (((0,), (0,)), ((), ())), precision=highest)]
    another operation x5 -> x0, other arithmetic: 12.1 us -> none  [the longest x3 6.52 us: local(): lower = jnp.linalg.cholesky(gram)]
    add x0 -> x15, other arithmetic: none -> 12 us  [the longest x3 5.75 us: local(): half(terms[k], b) * half(f_own, b) + half(arrived[k], b) * half(f_near, b)]
  transfers between devices with their start and end apart: 1 -> 44, of which waited for: 1 -> 19; matrix products, arithmetic and copies ran while one was open for 0% -> 7% of each run, Pallas kernels for 0% -> 10%
where the time goes in v2:
time: 179 us; the launch traced here: 178 us
  waiting for transfers between devices  60 us (34%)
  starting transfers between devices  56.2 us (31%)
  Pallas kernels  43.7 us (24%)
  other arithmetic  12.5 us (7%)
  local copies, waits for them, and re-layouts  3.61 us (2%)
  between operations  2.02 us (1%)
    ppermute x19, waiting for transfers between devices, low(): return lax.ppermute(x, axis, [(i, i ^ 1) for i in range(4)])  31.4 us
    ppermute x10, starting transfers between devices, swap(): return lax.ppermute(x, 'c', [(0, 1), (1, 0)])  25 us
    ppermute x7, waiting for transfers between devices, high(): return lax.ppermute(x, axis, [(i, 3 - i) for i in range(4)])  16.5 us
    pallas_call x2, Pallas kernels, finish(): pl.pallas_call(kernel, in_specs=[SM, VM] + [ANY] * 6 + [HBM] * (4 + given...  15.7 us
    pallas_call x2, Pallas kernels, q_half(): pl.pallas_call(kernel, in_specs=[SM, VM, HBM, HBM], out_specs=[ANY] * 3,...  10.5 us
    ppermute x6, starting transfers between devices, turn(): return lax.ppermute(x, axis, [(i, (i + step) % 4) for i in range(4)])  10.2 us
    pallas_call x1, Pallas kernels, left_factor(): pl.pallas_call(p_kernel, in_specs=[SM, HBM, HBM, HBM], out_specs=VM, out_...  9.67 us
    ppermute x19, starting transfers between devices, low(): return lax.ppermute(x, axis, [(i, i ^ 1) for i in range(4)])  7.3 us
  transfers between devices with their start and end apart: 44, of which 19 were waited for; matrix products, arithmetic and copies ran while one was open for 7% of the time, Pallas kernels for 10%

profile of v2, /device:TPU:1, one launch (start us, length us, event | category | flops | bytes accessed | tf_op | source)
XLA Modules:
  0.0 178.1 jit_solution(16808496283598685785)
XLA Ops:
  1.3 9.7 %left_factor.1 = f32[64,128]{1,0:T(8,128)} custom-call(s32[1]{0:T(128)S(6)} %copy.17.steps_ref, bf16[1,112,28672]{2,1,0:T(8,128)(2,1)} %rest_6_.3, bf16[1,112,28672]{2,1,0:T(8,128)(2,1)} %rest_7_.3, bf16[64,28672]{1,0:T(8,128)(2,1)} %bitcast.46), custom_call_target="tpu_custom_call" | custom-call | tf_op jit(solution)/shard_map/left_factor/pallas_call | solution.py:84
  11.0 3.4 %collective-permute-start.2 = (f32[64,128]{1,0:T(8,128)}, f32[64,128]{1,0:T(8,128)S(1)}, u32[]{:S(2)}, u32[]{:S(2)}) collective-permute-start(f32[64,128]{1,0:T(8,128)} %left_factor.1), channel_id=1, source_target_pairs={{0,24},{8,0},{16,8},{24,16},{1,25},{9,1},{17,9},{25,17},{2,26},{10... | collective-permute-start | bytes 98312 | tf_op jit(solution)/shard_map/ppermute | solution.py:33
  14.3 1.7 collective-permute-start
  16.1 2.5 %collective-permute-done.1 = f32[64,128]{1,0:T(8,128)S(1)} collective-permute-done((f32[64,128]{1,0:T(8,128)}, f32[64,128]{1,0:T(8,128)S(1)}, u32[]{:S(2)}, u32[]{:S(2)}) %collective-permute-start.1) | collective-permute-done | bytes 32800 | tf_op jit(solution)/shard_map/ppermute | solution.py:33
  19.8 3.8 %collective-permute-start.5 = (f32[64,128]{1,0:T(8,128)S(1)}, f32[64,128]{1,0:T(8,128)S(1)}, u32[]{:S(2)}, u32[]{:S(2)}) collective-permute-start(f32[64,128]{1,0:T(8,128)S(1)} %add_add_fusion.1.a_ref), channel_id=1, source_target_pairs={{0,96},{32,0},{64,32},{96,64},{1,97},{33,1},{65,33},{97,65},{2,98}... | collective-permute-start | bytes 98312 | tf_op jit(solution)/shard_map/ppermute | solution.py:33
  25.5 2.1 %collective-permute-done.4.c_ref = f32[64,128]{1,0:T(8,128)S(1)} collective-permute-done((f32[64,128]{1,0:T(8,128)S(1)}, f32[64,128]{1,0:T(8,128)S(1)}, u32[]{:S(2)}, u32[]{:S(2)}) %collective-permute-start.4) | collective-permute-done | bytes 32800 | tf_op jit(solution)/shard_map/ppermute | solution.py:33
  30.5 5.2 %q_far.1 = (f32[8,37,8,128]{3,2,1,0:T(8,128)}, f32[8,37,8,128]{3,2,1,0:T(8,128)}, f32[8,38,8,128]{3,2,1,0:T(8,128)}) custom-call(s32[5]{0:T(128)} %stack.23.s_ref, bf16[128,224]{1,0:T(8,128)(2,1)} %get-tuple-element.26.lhs_ref, bf16[1,112,28672]{2,1,0:T(8,128)(2,1)} %rest_6_.3, bf16[1,112,28672]{2,1,0:T(8,128)(2,1)} %rest_7_.3), custom_call_target="tpu_custom_call" | custom-call | flops 822083584 | bytes 10092544 | tf_op jit(solution)/shard_map/q_far/pallas_call | solution.py:175
  35.7 3.5 %collective-permute-start.10 = (f32[8,37,8,128]{3,2,1,0:T(8,128)}, f32[8,37,8,128]{3,2,1,0:T(8,128)S(1)}, u32[]{:S(2)}, u32[]{:S(2)}) collective-permute-start(f32[8,37,8,128]{3,2,1,0:T(8,128)} %get-tuple-element.33), channel_id=1, source_target_pairs={{0,1},{1,0},{2,3},{3,2},{4,5},{5,4},{6,7},{7,6},{8,9},{9,8},{10,11... | collective-permute-start | bytes 3637256 | tf_op jit(solution)/shard_map/ppermute | solution.py:45
  39.8 2.9 %collective-permute-done.6.near_ref = f32[72,128]{1,0:T(8,128)S(1)} collective-permute-done((f32[72,128]{1,0:T(8,128)S(1)}, f32[72,128]{1,0:T(8,128)S(1)}, u32[]{:S(2)}, u32[]{:S(2)}) %collective-permute-start.6) | collective-permute-done | bytes 36896 | tf_op jit(solution)/shard_map/ppermute | solution.py:45
  45.8 2.8 %collective-permute-start.8 = (f32[72,128]{1,0:T(8,128)S(1)}, f32[72,128]{1,0:T(8,128)S(1)}, u32[]{:S(2)}, u32[]{:S(2)}) collective-permute-start(f32[72,128]{1,0:T(8,128)S(1)} %add_select_fusion.pair_ref), channel_id=1, source_target_pairs={{0,6},{2,4},{4,2},{6,0},{1,7},{3,5},{5,3},{7,1},{8,14},{10,12},{12... | collective-permute-start | bytes 110600 | tf_op jit(solution)/shard_map/ppermute | solution.py:41
  48.6 5.2 %q_own.1 = (f32[8,37,8,128]{3,2,1,0:T(8,128)}, f32[8,37,8,128]{3,2,1,0:T(8,128)}, f32[8,38,8,128]{3,2,1,0:T(8,128)}) custom-call(s32[5]{0:T(128)} %stack.23.s_ref, bf16[128,224]{1,0:T(8,128)(2,1)} %get-tuple-element.26.lhs_ref, bf16[1,112,28672]{2,1,0:T(8,128)(2,1)} %rest_6_.3, bf16[1,112,28672]{2,1,0:T(8,128)(2,1)} %rest_7_.3), custom_call_target="tpu_custom_call" | custom-call | flops 822083584 | bytes 10092544 | tf_op jit(solution)/shard_map/q_own/pallas_call | solution.py:175
  54.0 2.4 %multiply_add_fusion.5 = (f32[4,37,8,128]{3,2,1,0:T(8,128)S(1)}, f32[4,37,8,128]{3,2,1,0:T(8,128)}) fusion(f32[8,37,8,128]{3,2,1,0:T(8,128)S(1)} %collective-permute-done.10, s32[]{:T(128)S(6)} %select_n.223, f32[8,37,8,128]{3,2,1,0:T(8,128)} %get-tuple-element.32, f32[4,8,128]{2,1,0:T(8,128)S(1)} %get-tuple-element.66, ...), kind=kLoop, calls=%fused_computation.8 | loop fusion | flops 909312 | bytes 3702792 | tf_op jit(solution)/shard_map/add | solution.py:362
  56.8 2.4 %multiply_add_fusion.3 = (f32[4,37,8,128]{3,2,1,0:T(8,128)S(1)}, f32[4,37,8,128]{3,2,1,0:T(8,128)}) fusion(f32[8,37,8,128]{3,2,1,0:T(8,128)} %collective-permute-done.14, s32[]{:T(128)S(6)} %select_n.229, f32[8,37,8,128]{3,2,1,0:T(8,128)S(1)} %copy-done.7, f32[4,8,128]{2,1,0:T(8,128)S(1)} %get-tuple-element.69, f32[4,8,128]{2,1,0:T(8,128)S(1)} %get-tuple-element.74, ...), kind=kLoop, calls=%fused_computation.6 | loop fusion | flops 909312 | bytes 3702792 | tf_op jit(solution)/shard_map/add | solution.py:362
  60.2 6.1 %solve.1 = (bf16[112,192]{1,0:T(8,128)(2,1)S(1)}, f32[4,38,8,128]{3,2,1,0:T(8,128)S(1)}) custom-call(f32[72,128]{1,0:T(8,128)S(1)} %get-tuple-element.24.gram_ref, f32[112,64]{1,0:T(8,128)S(1)} %copy-done.2, f32[4,38,8,128]{3,2,1,0:T(8,128)S(1)} %get-tuple-element.44.pass_in), custom_call_target="tpu_custom_call", output_to_operand_aliasing={{1}: (2, {})} | custom-call | flops 10000000 | bytes 10000000 | tf_op jit(solution)/shard_map/solve/pallas_call | solution.py:236
  67.0 3.1 %collective-permute-done.11 = f32[4,37,8,128]{3,2,1,0:T(8,128)} collective-permute-done((f32[4,37,8,128]{3,2,1,0:T(8,128)}, f32[4,37,8,128]{3,2,1,0:T(8,128)}, u32[]{:S(2)}, u32[]{:S(2)}) %collective-permute-start.11) | collective-permute-done | bytes 606240 | tf_op jit(solution)/shard_map/ppermute | solution.py:37
  76.1 3.4 %collective-permute-done.12 = f32[2,37,8,128]{3,2,1,0:T(8,128)} collective-permute-done((f32[2,37,8,128]{3,2,1,0:T(8,128)S(1)}, f32[2,37,8,128]{3,2,1,0:T(8,128)}, u32[]{:S(2)}, u32[]{:S(2)}) %collective-permute-start.12) | collective-permute-done | bytes 303136 | tf_op jit(solution)/shard_map/ppermute | solution.py:37
  82.5 3.4 %collective-permute-done.13 = f32[1,37,8,128]{3,2,1,0:T(8,128)S(1)} collective-permute-done((f32[1,37,8,128]{3,2,1,0:T(8,128)S(1)}, f32[1,37,8,128]{3,2,1,0:T(8,128)S(1)}, u32[]{:S(2)}, u32[]{:S(2)}) %collective-permute-start.13) | collective-permute-done | bytes 151584 | tf_op jit(solution)/shard_map/ppermute | solution.py:37
  87.1 6.0 %collective-permute-done.21 = f32[56,8,128]{2,1,0:T(8,128)S(1)} collective-permute-done((f32[56,8,128]{2,1,0:T(8,128)S(1)}, f32[56,8,128]{2,1,0:T(8,128)S(1)}, u32[]{:S(2)}, u32[]{:S(2)}) %collective-permute-start.21) | collective-permute-done | bytes 229408 | tf_op jit(solution)/shard_map/ppermute | solution.py:41
  93.2 5.1 %collective-permute-start.22 = (f32[14,8,128]{2,1,0:T(8,128)S(1)}, f32[14,8,128]{2,1,0:T(8,128)S(1)}, u32[]{:S(2)}, u32[]{:S(2)}) collective-permute-start(f32[14,8,128]{2,1,0:T(8,128)S(1)} %get-tuple-element.57), channel_id=1, source_target_pairs={{0,120},{8,112},{16,104},{24,96},{32,88},{40,80},{48,72},{56,64},{... | collective-permute-start | bytes 172040 | tf_op jit(solution)/shard_map/ppermute | solution.py:377
  99.9 2.7 %collective-permute-done.24 = f32[14,8,128]{2,1,0:T(8,128)S(1)} collective-permute-done((f32[14,8,128]{2,1,0:T(8,128)S(1)}, f32[14,8,128]{2,1,0:T(8,128)S(1)}, u32[]{:S(2)}, u32[]{:S(2)}) %collective-permute-start.24) | collective-permute-done | bytes 57376 | tf_op jit(solution)/shard_map/ppermute | solution.py:41
  102.6 2.8 %collective-permute-start.25 = (f32[14,8,128]{2,1,0:T(8,128)S(1)}, f32[14,8,128]{2,1,0:T(8,128)S(1)}, u32[]{:S(2)}, u32[]{:S(2)}) collective-permute-start(f32[14,8,128]{2,1,0:T(8,128)S(1)} %add_add_fusion), channel_id=1, source_target_pairs={{0,24},{8,16},{16,8},{24,0},{1,25},{9,17},{17,9},{25,1},{2,26},{10... | collective-permute-start | bytes 172040 | tf_op jit(solution)/shard_map/ppermute | solution.py:41
  105.9 1.9 %collective-permute-start.27 = (f32[14,8,128]{2,1,0:T(8,128)S(1)}, f32[14,8,128]{2,1,0:T(8,128)S(1)}, u32[]{:S(2)}, u32[]{:S(2)}) collective-permute-start(f32[14,8,128]{2,1,0:T(8,128)S(1)} %add_add_fusion), channel_id=1, source_target_pairs={{0,120},{8,112},{16,104},{24,96},{32,88},{40,80},{48,72},{56,64},{... | collective-permute-start | bytes 172040 | tf_op jit(solution)/shard_map/ppermute | solution.py:377
  109.6 2.7 %collective-permute-done.27 = f32[14,8,128]{2,1,0:T(8,128)S(1)} collective-permute-done((f32[14,8,128]{2,1,0:T(8,128)S(1)}, f32[14,8,128]{2,1,0:T(8,128)S(1)}, u32[]{:S(2)}, u32[]{:S(2)}) %collective-permute-start.27) | collective-permute-done | bytes 57376 | tf_op jit(solution)/shard_map/ppermute | solution.py:377
  112.4 6.1 %collective-permute-done.28 = f32[56,8,128]{2,1,0:T(8,128)S(1)} collective-permute-done((f32[56,8,128]{2,1,0:T(8,128)S(1)}, f32[56,8,128]{2,1,0:T(8,128)S(1)}, u32[]{:S(2)}, u32[]{:S(2)}) %collective-permute-start.28) | collective-permute-done | bytes 229408 | tf_op jit(solution)/shard_map/ppermute | solution.py:41
  118.9 4.1 %collective-permute-done.34 = f32[1,37,8,128]{3,2,1,0:T(8,128)S(1)} collective-permute-done((f32[1,37,8,128]{3,2,1,0:T(8,128)S(1)}, f32[1,37,8,128]{3,2,1,0:T(8,128)S(1)}, u32[]{:S(2)}, u32[]{:S(2)}) %collective-permute-start.34) | collective-permute-done | bytes 151584 | tf_op jit(solution)/shard_map/ppermute | solution.py:37
  124.5 4.5 %collective-permute-done.35 = f32[2,37,8,128]{3,2,1,0:T(8,128)S(1)} collective-permute-done((f32[2,37,8,128]{3,2,1,0:T(8,128)S(1)}, f32[2,37,8,128]{3,2,1,0:T(8,128)S(1)}, u32[]{:S(2)}, u32[]{:S(2)}) %collective-permute-start.35) | collective-permute-done | bytes 303136 | tf_op jit(solution)/shard_map/ppermute | solution.py:37
  129.2 14.3 %collective-permute-start.36 = (f32[4,37,8,128]{3,2,1,0:T(8,128)S(1)}, f32[4,37,8,128]{3,2,1,0:T(8,128)S(1)}, u32[]{:S(2)}, u32[]{:S(2)}) collective-permute-start(f32[4,37,8,128]{3,2,1,0:T(8,128)S(1)} %maximum_select_fusion.2.rest_2_), channel_id=1, source_target_pairs={{0,1},{1,0},{2,3},{3,2},{4,5},{5,4},{6,7},{7,6},{8,9},{9,8},{10,11... | collective-permute-start | bytes 1818632 | tf_op jit(solution)/shard_map/ppermute | solution.py:45
  144.2 3.4 %collective-permute-start.41 = (f32[4,38,8,128]{3,2,1,0:T(8,128)S(1)}, f32[4,38,8,128]{3,2,1,0:T(8,128)S(1)}, u32[]{:S(2)}, u32[]{:S(2)}) collective-permute-start(f32[4,38,8,128]{3,2,1,0:T(8,128)S(1)} %maximum_select_fusion.rest_4_), channel_id=1, source_target_pairs={{0,1},{1,0},{2,3},{3,2},{4,5},{5,4},{6,7},{7,6},{8,9},{9,8},{10,11... | collective-permute-start | bytes 1867784 | tf_op jit(solution)/shard_map/ppermute | solution.py:45
  147.6 10.0 %collective-permute-done.42.rest_5_ = f32[4,38,8,128]{3,2,1,0:T(8,128)S(1)} collective-permute-done((f32[4,38,8,128]{3,2,1,0:T(8,128)S(1)}, f32[4,38,8,128]{3,2,1,0:T(8,128)S(1)}, u32[]{:S(2)}, u32[]{:S(2)}) %collective-permute-start.42) | collective-permute-done | bytes 622624 | tf_op jit(solution)/shard_map/ppermute | solution.py:37
  157.6 2.5 %collective-permute-start.43 = (f32[4,38,8,128]{3,2,1,0:T(8,128)S(1)}, f32[4,38,8,128]{3,2,1,0:T(8,128)S(1)}, u32[]{:S(2)}, u32[]{:S(2)}) collective-permute-start(f32[4,38,8,128]{3,2,1,0:T(8,128)S(1)} %collective-permute-done.42.rest_5_), channel_id=1, source_target_pairs={{0,1},{1,0},{2,3},{3,2},{4,5},{5,4},{6,7},{7,6},{8,9},{9,8},{10,11... | collective-permute-start | bytes 1867784 | tf_op jit(solution)/shard_map/ppermute | solution.py:45
  160.8 7.0 %finish_own.1 = (bf16[1,112,28672]{2,1,0:T(8,128)(2,1)}, f32[112,1792]{1,0:T(8,128)}, f32[112,1792]{1,0:T(8,128)}) custom-call(s32[5]{0:T(128)} %stack.23.s_ref, bf16[112,192]{1,0:T(8,128)(2,1)} %copy-done, f32[4,37,8,128]{3,2,1,0:T(8,128)} %copy-done.5, f32[4,37,8,128]{3,2,1,0:T(8,128)} %collective-permute-done.32.rest_1_, f32[4,37,8,128]{3,2,1,0:T(8,128)} %copy-done.4, ...), custom_call_target="tpu_custom_call" | custom-call | flops 616562688 | bytes 13303808 | tf_op jit(solution)/shard_map/finish_own/pallas_call | solution.py:312
  169.3 8.6 %finish_far.1 = (bf16[1,112,28672]{2,1,0:T(8,128)(2,1)}, f32[112,1792]{1,0:T(8,128)}, f32[112,1792]{1,0:T(8,128)}) custom-call(s32[5]{0:T(128)} %stack.23.s_ref, bf16[112,192]{1,0:T(8,128)(2,1)} %copy-done, f32[4,37,8,128]{3,2,1,0:T(8,128)} %copy-done.12, ...), custom_call_target="tpu_custom_call", output_to_operand_aliasing={{0}: (12, {}), {1}: (13, {}), {2}: (14, {})} | custom-call | flops 616562688 | bytes 13303808 | tf_op jit(solution)/shard_map/finish_far/pallas_call | solution.py:312
  (135 shorter events, 30.8 us)
Async XLA Ops:
  11.0 5.1 %collective-permute-start.2 = (f32[64,128]{1,0:T(8,128)}, f32[64,128]{1,0:T(8,128)S(1)}, u32[]{:S(2)}, u32[]{:S(2)}) collective-permute-start(f32[64,128]{1,0:T(8,128)} %left_factor.1), channel_id=1, source_target_pairs={{0,24},{8,0},{16,8},{24,16},{1,25},{9,1},{17,9},{25,17},{2,26},{10... | collective-permute-start | bytes 98312 | tf_op jit(solution)/shard_map/ppermute | solution.py:33
  19.8 5.8 %collective-permute-start.5 = (f32[64,128]{1,0:T(8,128)S(1)}, f32[64,128]{1,0:T(8,128)S(1)}, u32[]{:S(2)}, u32[]{:S(2)}) collective-permute-start(f32[64,128]{1,0:T(8,128)S(1)} %add_add_fusion.1.a_ref), channel_id=1, source_target_pairs={{0,96},{32,0},{64,32},{96,64},{1,97},{33,1},{65,33},{97,65},{2,98}... | collective-permute-start | bytes 98312 | tf_op jit(solution)/shard_map/ppermute | solution.py:33
  35.7 18.2 %collective-permute-start.10 = (f32[8,37,8,128]{3,2,1,0:T(8,128)}, f32[8,37,8,128]{3,2,1,0:T(8,128)S(1)}, u32[]{:S(2)}, u32[]{:S(2)}) collective-permute-start(f32[8,37,8,128]{3,2,1,0:T(8,128)} %get-tuple-element.33), channel_id=1, source_target_pairs={{0,1},{1,0},{2,3},{3,2},{4,5},{5,4},{6,7},{7,6},{8,9},{9,8},{10,11... | collective-permute-start | bytes 3637256 | tf_op jit(solution)/shard_map/ppermute | solution.py:45
  39.2 17.6 %collective-permute-start.14 = (f32[8,37,8,128]{3,2,1,0:T(8,128)}, f32[8,37,8,128]{3,2,1,0:T(8,128)}, u32[]{:S(2)}, u32[]{:S(2)}) collective-permute-start(f32[8,37,8,128]{3,2,1,0:T(8,128)} %get-tuple-element.35), channel_id=1, source_target_pairs={{0,1},{1,0},{2,3},{3,2},{4,5},{5,4},{6,7},{7,6},{8,9},{9,8},{10,11... | collective-permute-start | bytes 3637256 | tf_op jit(solution)/shard_map/ppermute | solution.py:45
  39.7 19.4 %collective-permute-start.9 = (f32[8,38,8,128]{3,2,1,0:T(8,128)}, f32[8,38,8,128]{3,2,1,0:T(8,128)S(1)}, u32[]{:S(2)}, u32[]{:S(2)}) collective-permute-start(f32[8,38,8,128]{3,2,1,0:T(8,128)} %get-tuple-element.29), channel_id=1, source_target_pairs={{0,1},{1,0},{2,3},{3,2},{4,5},{5,4},{6,7},{7,6},{8,9},{9,8},{10,11... | collective-permute-start | bytes 3735560 | tf_op jit(solution)/shard_map/ppermute | solution.py:45
  45.8 8.1 %collective-permute-start.8 = (f32[72,128]{1,0:T(8,128)S(1)}, f32[72,128]{1,0:T(8,128)S(1)}, u32[]{:S(2)}, u32[]{:S(2)}) collective-permute-start(f32[72,128]{1,0:T(8,128)S(1)} %add_select_fusion.pair_ref), channel_id=1, source_target_pairs={{0,6},{2,4},{4,2},{6,0},{1,7},{3,5},{5,3},{7,1},{8,14},{10,12},{12... | collective-permute-start | bytes 110600 | tf_op jit(solution)/shard_map/ppermute | solution.py:41
  56.4 13.7 %collective-permute-start.11 = (f32[4,37,8,128]{3,2,1,0:T(8,128)}, f32[4,37,8,128]{3,2,1,0:T(8,128)}, u32[]{:S(2)}, u32[]{:S(2)}) collective-permute-start(f32[4,37,8,128]{3,2,1,0:T(8,128)} %get-tuple-element.46), channel_id=1, source_target_pairs={{0,8},{8,0},{16,24},{24,16},{1,9},{9,1},{17,25},{25,17},{2,10},{10... | collective-permute-start | bytes 1818632 | tf_op jit(solution)/shard_map/ppermute | solution.py:37
  59.2 13.4 %collective-permute-start.15 = (f32[4,37,8,128]{3,2,1,0:T(8,128)}, f32[4,37,8,128]{3,2,1,0:T(8,128)}, u32[]{:S(2)}, u32[]{:S(2)}) collective-permute-start(f32[4,37,8,128]{3,2,1,0:T(8,128)} %get-tuple-element.48), channel_id=1, source_target_pairs={{0,2},{2,0},{4,6},{6,4},{1,3},{3,1},{5,7},{7,5},{8,10},{10,8},{12,... | collective-permute-start | bytes 1818632 | tf_op jit(solution)/shard_map/ppermute | solution.py:37
  60.2 13.6 %collective-permute-start.18 = (f32[4,38,8,128]{3,2,1,0:T(8,128)}, f32[4,38,8,128]{3,2,1,0:T(8,128)}, u32[]{:S(2)}, u32[]{:S(2)}) collective-permute-start(f32[4,38,8,128]{3,2,1,0:T(8,128)} %get-tuple-element.43), channel_id=1, source_target_pairs={{0,32},{32,0},{64,96},{96,64},{1,33},{33,1},{65,97},{97,65},{2,34}... | collective-permute-start | bytes 1867784 | tf_op jit(solution)/shard_map/ppermute | solution.py:37
  71.2 8.3 %collective-permute-start.12 = (f32[2,37,8,128]{3,2,1,0:T(8,128)S(1)}, f32[2,37,8,128]{3,2,1,0:T(8,128)}, u32[]{:S(2)}, u32[]{:S(2)}) collective-permute-start(f32[2,37,8,128]{3,2,1,0:T(8,128)S(1)} %get-tuple-element.52), channel_id=1, source_target_pairs={{0,2},{2,0},{4,6},{6,4},{1,3},{3,1},{5,7},{7,5},{8,10},{10,8},{12,... | collective-permute-start | bytes 909320 | tf_op jit(solution)/shard_map/ppermute | solution.py:37
  73.7 6.8 %collective-permute-start.16 = (f32[2,37,8,128]{3,2,1,0:T(8,128)S(1)}, f32[2,37,8,128]{3,2,1,0:T(8,128)S(1)}, u32[]{:S(2)}, u32[]{:S(2)}) collective-permute-start(f32[2,37,8,128]{3,2,1,0:T(8,128)S(1)} %get-tuple-element.54), channel_id=1, source_target_pairs={{0,32},{32,0},{64,96},{96,64},{1,33},{33,1},{65,97},{97,65},{2,34}... | collective-permute-start | bytes 909320 | tf_op jit(solution)/shard_map/ppermute | solution.py:37
  75.0 7.3 %collective-permute-start.19 = (f32[2,38,8,128]{3,2,1,0:T(8,128)S(1)}, f32[2,38,8,128]{3,2,1,0:T(8,128)S(1)}, u32[]{:S(2)}, u32[]{:S(2)}) collective-permute-start(f32[2,38,8,128]{3,2,1,0:T(8,128)S(1)} %get-tuple-element.50), channel_id=1, source_target_pairs={{0,8},{8,0},{16,24},{24,16},{1,9},{9,1},{17,25},{25,17},{2,10},{10... | collective-permute-start | bytes 933896 | tf_op jit(solution)/shard_map/ppermute | solution.py:37
  80.4 5.4 %collective-permute-start.13 = (f32[1,37,8,128]{3,2,1,0:T(8,128)S(1)}, f32[1,37,8,128]{3,2,1,0:T(8,128)S(1)}, u32[]{:S(2)}, u32[]{:S(2)}) collective-permute-start(f32[1,37,8,128]{3,2,1,0:T(8,128)S(1)} %dynamic-slice_add_fusion.9), channel_id=1, source_target_pairs={{0,32},{32,0},{64,96},{96,64},{1,33},{33,1},{65,97},{97,65},{2,34}... | collective-permute-start | bytes 454664 | tf_op jit(solution)/shard_map/ppermute | solution.py:37
  80.6 6.2 %collective-permute-start.17 = (f32[1,37,8,128]{3,2,1,0:T(8,128)S(1)}, f32[1,37,8,128]{3,2,1,0:T(8,128)S(1)}, u32[]{:S(2)}, u32[]{:S(2)}) collective-permute-start(f32[1,37,8,128]{3,2,1,0:T(8,128)S(1)} %dynamic-slice_add_fusion.8), channel_id=1, source_target_pairs={{0,8},{8,0},{16,24},{24,16},{1,9},{9,1},{17,25},{25,17},{2,10},{10... | collective-permute-start | bytes 454664 | tf_op jit(solution)/shard_map/ppermute | solution.py:37
  87.0 6.2 %collective-permute-start.21 = (f32[56,8,128]{2,1,0:T(8,128)S(1)}, f32[56,8,128]{2,1,0:T(8,128)S(1)}, u32[]{:S(2)}, u32[]{:S(2)}) collective-permute-start(f32[56,8,128]{2,1,0:T(8,128)S(1)} %constant_dynamic-slice_fusion), channel_id=1, source_target_pairs={{0,6},{2,4},{4,2},{6,0},{1,7},{3,5},{5,3},{7,1},{8,14},{10,12},{12... | collective-permute-start | bytes 688136 | tf_op jit(solution)/shard_map/ppermute | solution.py:41
  93.2 6.7 %collective-permute-start.22 = (f32[14,8,128]{2,1,0:T(8,128)S(1)}, f32[14,8,128]{2,1,0:T(8,128)S(1)}, u32[]{:S(2)}, u32[]{:S(2)}) collective-permute-start(f32[14,8,128]{2,1,0:T(8,128)S(1)} %get-tuple-element.57), channel_id=1, source_target_pairs={{0,120},{8,112},{16,104},{24,96},{32,88},{40,80},{48,72},{56,64},{... | collective-permute-start | bytes 172040 | tf_op jit(solution)/shard_map/ppermute | solution.py:377
  102.6 5.3 %collective-permute-start.25 = (f32[14,8,128]{2,1,0:T(8,128)S(1)}, f32[14,8,128]{2,1,0:T(8,128)S(1)}, u32[]{:S(2)}, u32[]{:S(2)}) collective-permute-start(f32[14,8,128]{2,1,0:T(8,128)S(1)} %add_add_fusion), channel_id=1, source_target_pairs={{0,24},{8,16},{16,8},{24,0},{1,25},{9,17},{17,9},{25,1},{2,26},{10... | collective-permute-start | bytes 172040 | tf_op jit(solution)/shard_map/ppermute | solution.py:41
  105.9 6.3 %collective-permute-start.27 = (f32[14,8,128]{2,1,0:T(8,128)S(1)}, f32[14,8,128]{2,1,0:T(8,128)S(1)}, u32[]{:S(2)}, u32[]{:S(2)}) collective-permute-start(f32[14,8,128]{2,1,0:T(8,128)S(1)} %add_add_fusion), channel_id=1, source_target_pairs={{0,120},{8,112},{16,104},{24,96},{32,88},{40,80},{48,72},{56,64},{... | collective-permute-start | bytes 172040 | tf_op jit(solution)/shard_map/ppermute | solution.py:377
  112.3 6.2 %collective-permute-start.28 = (f32[56,8,128]{2,1,0:T(8,128)S(1)}, f32[56,8,128]{2,1,0:T(8,128)S(1)}, u32[]{:S(2)}, u32[]{:S(2)}) collective-permute-start(f32[56,8,128]{2,1,0:T(8,128)S(1)} %maximum_select_fusion.7), channel_id=1, source_target_pairs={{0,6},{2,4},{4,2},{6,0},{1,7},{3,5},{5,3},{7,1},{8,14},{10,12},{12... | collective-permute-start | bytes 688136 | tf_op jit(solution)/shard_map/ppermute | solution.py:41
  118.8 5.6 %collective-permute-start.29 = (f32[1,37,8,128]{3,2,1,0:T(8,128)S(1)}, f32[1,37,8,128]{3,2,1,0:T(8,128)S(1)}, u32[]{:S(2)}, u32[]{:S(2)}) collective-permute-start(f32[1,37,8,128]{3,2,1,0:T(8,128)S(1)} %get-tuple-element.56), channel_id=1, source_target_pairs={{0,32},{32,0},{64,96},{96,64},{1,33},{33,1},{65,97},{97,65},{2,34}... | collective-permute-start | bytes 454664 | tf_op jit(solution)/shard_map/ppermute | solution.py:37
  123.0 6.0 %collective-permute-start.35 = (f32[2,37,8,128]{3,2,1,0:T(8,128)S(1)}, f32[2,37,8,128]{3,2,1,0:T(8,128)S(1)}, u32[]{:S(2)}, u32[]{:S(2)}) collective-permute-start(f32[2,37,8,128]{3,2,1,0:T(8,128)S(1)} %maximum_select_fusion.6), channel_id=1, source_target_pairs={{0,32},{32,0},{64,96},{96,64},{1,33},{33,1},{65,97},{97,65},{2,34}... | collective-permute-start | bytes 909320 | tf_op jit(solution)/shard_map/ppermute | solution.py:37
  123.2 20.4 %collective-permute-start.40 = (f32[2,38,8,128]{3,2,1,0:T(8,128)S(1)}, f32[2,38,8,128]{3,2,1,0:T(8,128)S(1)}, u32[]{:S(2)}, u32[]{:S(2)}) collective-permute-start(f32[2,38,8,128]{3,2,1,0:T(8,128)S(1)} %maximum_select_fusion.4), channel_id=1, source_target_pairs={{0,8},{8,0},{16,24},{24,16},{1,9},{9,1},{17,25},{25,17},{2,10},{10... | collective-permute-start | bytes 933896 | tf_op jit(solution)/shard_map/ppermute | solution.py:37
  124.4 19.3 %collective-permute-start.30 = (f32[2,37,8,128]{3,2,1,0:T(8,128)S(1)}, f32[2,37,8,128]{3,2,1,0:T(8,128)S(1)}, u32[]{:S(2)}, u32[]{:S(2)}) collective-permute-start(f32[2,37,8,128]{3,2,1,0:T(8,128)S(1)} %maximum_select_fusion.5), channel_id=1, source_target_pairs={{0,2},{2,0},{4,6},{6,4},{1,3},{3,1},{5,7},{7,5},{8,10},{10,8},{12,... | collective-permute-start | bytes 909320 | tf_op jit(solution)/shard_map/ppermute | solution.py:37
  129.1 31.0 %collective-permute-start.37 = (f32[4,37,8,128]{3,2,1,0:T(8,128)S(1)}, f32[4,37,8,128]{3,2,1,0:T(8,128)}, u32[]{:S(2)}, u32[]{:S(2)}) collective-permute-start(f32[4,37,8,128]{3,2,1,0:T(8,128)S(1)} %maximum_select_fusion.2.rest_2_), channel_id=1, source_target_pairs={{0,2},{2,0},{4,6},{6,4},{1,3},{3,1},{5,7},{7,5},{8,10},{10,8},{12,... | collective-permute-start | bytes 1818632 | tf_op jit(solution)/shard_map/ppermute | solution.py:37
  129.2 31.0 %collective-permute-start.36 = (f32[4,37,8,128]{3,2,1,0:T(8,128)S(1)}, f32[4,37,8,128]{3,2,1,0:T(8,128)S(1)}, u32[]{:S(2)}, u32[]{:S(2)}) collective-permute-start(f32[4,37,8,128]{3,2,1,0:T(8,128)S(1)} %maximum_select_fusion.2.rest_2_), channel_id=1, source_target_pairs={{0,1},{1,0},{2,3},{3,2},{4,5},{5,4},{6,7},{7,6},{8,9},{9,8},{10,11... | collective-permute-start | bytes 1818632 | tf_op jit(solution)/shard_map/ppermute | solution.py:45
  143.6 14.0 %collective-permute-start.42 = (f32[4,38,8,128]{3,2,1,0:T(8,128)S(1)}, f32[4,38,8,128]{3,2,1,0:T(8,128)S(1)}, u32[]{:S(2)}, u32[]{:S(2)}) collective-permute-start(f32[4,38,8,128]{3,2,1,0:T(8,128)S(1)} %maximum_select_fusion.rest_4_), channel_id=1, source_target_pairs={{0,32},{32,0},{64,96},{96,64},{1,33},{33,1},{65,97},{97,65},{2,34}... | collective-permute-start | bytes 1867784 | tf_op jit(solution)/shard_map/ppermute | solution.py:37
  143.8 16.9 %collective-permute-start.32 = (f32[4,37,8,128]{3,2,1,0:T(8,128)S(1)}, f32[4,37,8,128]{3,2,1,0:T(8,128)}, u32[]{:S(2)}, u32[]{:S(2)}) collective-permute-start(f32[4,37,8,128]{3,2,1,0:T(8,128)S(1)} %maximum_select_fusion.1.rest_0_), channel_id=1, source_target_pairs={{0,8},{8,0},{16,24},{24,16},{1,9},{9,1},{17,25},{25,17},{2,10},{10... | collective-permute-start | bytes 1818632 | tf_op jit(solution)/shard_map/ppermute | solution.py:37
  144.2 23.7 %collective-permute-start.41 = (f32[4,38,8,128]{3,2,1,0:T(8,128)S(1)}, f32[4,38,8,128]{3,2,1,0:T(8,128)S(1)}, u32[]{:S(2)}, u32[]{:S(2)}) collective-permute-start(f32[4,38,8,128]{3,2,1,0:T(8,128)S(1)} %maximum_select_fusion.rest_4_), channel_id=1, source_target_pairs={{0,1},{1,0},{2,3},{3,2},{4,5},{5,4},{6,7},{7,6},{8,9},{9,8},{10,11... | collective-permute-start | bytes 1867784 | tf_op jit(solution)/shard_map/ppermute | solution.py:45
  157.6 10.3 %collective-permute-start.43 = (f32[4,38,8,128]{3,2,1,0:T(8,128)S(1)}, f32[4,38,8,128]{3,2,1,0:T(8,128)S(1)}, u32[]{:S(2)}, u32[]{:S(2)}) collective-permute-start(f32[4,38,8,128]{3,2,1,0:T(8,128)S(1)} %collective-permute-done.42.rest_5_), channel_id=1, source_target_pairs={{0,1},{1,0},{2,3},{3,2},{4,5},{5,4},{6,7},{7,6},{8,9},{9,8},{10,11... | collective-permute-start | bytes 1867784 | tf_op jit(solution)/shard_map/ppermute | solution.py:45
  160.1 7.7 %collective-permute-start.31 = (f32[4,37,8,128]{3,2,1,0:T(8,128)S(1)}, f32[4,37,8,128]{3,2,1,0:T(8,128)S(1)}, u32[]{:S(2)}, u32[]{:S(2)}) collective-permute-start(f32[4,37,8,128]{3,2,1,0:T(8,128)S(1)} %maximum_select_fusion.1.rest_0_), channel_id=1, source_target_pairs={{0,1},{1,0},{2,3},{3,2},{4,5},{5,4},{6,7},{7,6},{8,9},{9,8},{10,11... | collective-permute-start | bytes 1818632 | tf_op jit(solution)/shard_map/ppermute | solution.py:45
  160.2 7.6 %collective-permute-start.38 = (f32[4,37,8,128]{3,2,1,0:T(8,128)}, f32[4,37,8,128]{3,2,1,0:T(8,128)S(1)}, u32[]{:S(2)}, u32[]{:S(2)}) collective-permute-start(f32[4,37,8,128]{3,2,1,0:T(8,128)} %collective-permute-done.37.rest_3_), channel_id=1, source_target_pairs={{0,1},{1,0},{2,3},{3,2},{4,5},{5,4},{6,7},{7,6},{8,9},{9,8},{10,11... | collective-permute-start | bytes 1818632 | tf_op jit(solution)/shard_map/ppermute | solution.py:45
  160.7 7.2 %collective-permute-start.33 = (f32[4,37,8,128]{3,2,1,0:T(8,128)}, f32[4,37,8,128]{3,2,1,0:T(8,128)}, u32[]{:S(2)}, u32[]{:S(2)}) collective-permute-start(f32[4,37,8,128]{3,2,1,0:T(8,128)} %collective-permute-done.32.rest_1_), channel_id=1, source_target_pairs={{0,1},{1,0},{2,3},{3,2},{4,5},{5,4},{6,7},{7,6},{8,9},{9,8},{10,11... | collective-permute-start | bytes 1818632 | tf_op jit(solution)/shard_map/ppermute | solution.py:45
  (30 other events, 158.1 us)

commit v3 on v2

--- a/solution.py
+++ b/solution.py
@@ -124,7 +124,7 @@
             jax.ShapeDtypeStruct((128, 224), BF),
             jax.ShapeDtypeStruct((72, 128), F32),
         ],
-        compiler_params=params_of(),
+        compiler_params=params_of(8),
         name="prepare",
     )(steps, a, b, c, d)
 
@@ -149,11 +149,12 @@
     return slice(FIRST[k], FIRST[k] + COUNTS[k])
 
 
-def q_half(where, lhs, delta, error, far):
+def q_half(where, lhs, delta, error, far, *first):
     parts = blocks_of(28)
     n = len(parts)
 
     def kernel(s_ref, lhs_ref, d_ref, e_ref, *rest):
+        rest = rest[len(first):]
         out_refs, (both_ref, v_ref, sem, out_sem) = rest[:3], rest[3:]
         side = 1 - s_ref[0] if far else s_ref[0]
         copies = [load_block(side, s, *parts[s], d_ref, e_ref, both_ref, sem) for s in range(n)]
@@ -174,8 +175,8 @@
 
     return pl.pallas_call(
         kernel,
-        in_specs=[SM, VM, HBM, HBM],
-        out_specs=[ANY] * 3,
+        in_specs=[SM, VM, HBM, HBM] + [ANY] * len(first),
+        out_specs=[HBM] * 3,
         out_shape=[jax.ShapeDtypeStruct((8, c, 8, 128), F32) for c in COUNTS],
         scratch_shapes=[
             pltpu.VMEM((n, 224, 28 * 128), BF),
@@ -186,32 +187,88 @@
         compiler_params=params_of(),
         cost_estimate=pl.CostEstimate(flops=2 * 128 * 224 * HALF * 128, bytes_accessed=HALF * 128 * (448 + 256), transcendentals=0),
         name="q_far" if far else "q_own",
-    )(where, lhs, delta, error)
-
-
-def scales_kernel(own_ref, near_ref, pair_ref, far_ref, both_ref, f_own_ref, f_near_ref):
-    join = jnp.where(lax.broadcasted_iota(jnp.int32, (72, 128), 0) == 64, jnp.maximum(pair_ref[...], far_ref[...]), pair_ref[...] + far_ref[...])
-    both_ref[...] = join
+    )(where, lhs, delta, error, *first)
+
+
+def blend(where, terms, arrived, f_own, f_near, gram):
+    def kernel(s_ref, *refs):
+        a_refs, b_refs, (f_ref, g_ref, gram_ref), refs = refs[:3], refs[3:6], refs[6:9], refs[9:]
+        keep_refs, send_refs, (a_buf, b_buf, sem, out_sem) = refs[:3], refs[3:6], refs[6:]
+        copies = []
+        for k in range(3):
+            copies.append((
+                start(a_refs[k], a_buf.at[:, chunk_range(k)], sem.at[k, 0]),
+                start(b_refs[k], b_buf.at[:, chunk_range(k)], sem.at[k, 1]),
+            ))
+        outs = []
+        for k in range(3):
+            for copy in copies[k]:
+                copy.wait()
+            tiles = chunk_range(k)
+            for i in range(8):
+                f = f_ref[8 * i:8 * i + 8, :][None]
+                g = g_ref[8 * i:8 * i + 8, :][None]
+                a_buf[i, tiles] = f * a_buf[i, tiles] + g * b_buf[i, tiles]
+            bit = s_ref[1 + k]
+            outs.append(start(a_buf.at[pl.ds(bit * 4, 4), tiles], keep_refs[k], out_sem.at[k, 4]))
+            for i in range(4):
+                place = slice(i * COUNTS[k], (i + 1) * COUNTS[k])
+                outs.append(start(a_buf.at[(1 - bit) * 4 + i, tiles], send_refs[k].at[place], out_sem.at[k, i]))
+            if ROUTES[k][0] == "y":
+                outs.append(start(gram_ref, send_refs[k].at[slice(4 * COUNTS[k], 4 * COUNTS[k] + 9)], out_sem.at[k, 5]))
+        for copy in outs:
+            copy.wait()
+
+    halves = [jax.ShapeDtypeStruct((4, c, 8, 128), F32) for c in COUNTS]
+    away = [jax.ShapeDtypeStruct((4 * c + (9 if r[0] == "y" else 0), 8, 128), F32) for c, r in zip(COUNTS, ROUTES)]
+    out = pl.pallas_call(
+        kernel,
+        in_specs=[SM] + [ANY] * 6 + [VM, VM, VM],
+        out_specs=[HBM] * 6,
+        out_shape=halves + away,
+        scratch_shapes=[
+            pltpu.VMEM((8, HALF, 8, 128), F32),
+            pltpu.VMEM((8, HALF, 8, 128), F32),
+            DMA((3, 2)),
+            DMA((3, 6)),
+        ],
+        compiler_params=params_of(16),
+        cost_estimate=pl.CostEstimate(flops=10 ** 6, bytes_accessed=11 * 10 ** 6, transcendentals=0),
+        name="blend",
+    )(where, *terms, *arrived, f_own, f_near, gram.reshape(9, 8, 128))
+    return out[:3], out[3:]
+
+
+def scales_kernel(a_ref, b_ref, *refs):
+    sum_ref, f_a_ref, f_b_ref = refs[-3:]
+    both = [ref[...] for ref in refs[:-3]]
+    maxima = lax.broadcasted_iota(jnp.int32, (72, 128), 0) == 64
+    while len(both) > 1:
+        n = len(both) // 2
+        both = [jnp.where(maxima, jnp.maximum(c, d), c + d) for c, d in zip(both[:n], both[n:])]
+    both = both[0]
+    sum_ref[...] = both
     eye = lax.broadcasted_iota(jnp.int32, (64, 64), 0) == lax.broadcasted_iota(jnp.int32, (64, 64), 1)
-    top = jnp.maximum(join[64:65, 0:64], 1e-37)
-    for src, dst in ((own_ref, f_own_ref), (near_ref, f_near_ref)):
-        ratio = src[64:65, 0:64] / top
-        column = jnp.sum(jnp.where(eye, ratio, 0.0), axis=1, keepdims=True)
+    top = jnp.maximum(both[64:65, 0:64], 1e-37)
+    for src, dst in ((a_ref, f_a_ref), (b_ref, f_b_ref)):
+        column = jnp.sum(jnp.where(eye, src[64:65, 0:64] / top, 0.0), axis=1, keepdims=True)
         dst[...] = jnp.broadcast_to(column, (64, 128))
 
 
-def scales(own, near, pair, far):
-    return pl.pallas_call(
+def scales(a, b, *terms):
+    both, f_a, f_b = pl.pallas_call(
         scales_kernel,
-        in_specs=[VM] * 4,
+        in_specs=[VM] * (2 + len(terms)),
         out_specs=[VM] * 3,
         out_shape=[jax.ShapeDtypeStruct((72, 128), F32)] + [jax.ShapeDtypeStruct((64, 128), F32)] * 2,
         compiler_params=params_of(8),
         name="scales",
-    )(own, near, pair, far)
-
-
-def solve_kernel(gram_ref, p_ref, pass_in, w_ref, pass_out):
+    )(a, b, *terms)
+    return both, f_a, f_b
+
+
+def solve_kernel(gram_ref, p_ref, block_ref, w_ref, block_out, sem):
+    copy = start(block_ref, block_out, sem)
     highest = lax.Precision.HIGHEST
     row = lax.broadcasted_iota(jnp.int32, (64, 64), 0)
     lane = lax.broadcasted_iota(jnp.int32, (64, 64), 1)
@@ -230,19 +287,20 @@
     w = lax.dot_general(p_hat, inverse, (((1,), (0,)), ((), ())), precision=highest, preferred_element_type=F32)
     upper = w.astype(BF).astype(F32)
     w_ref[...] = jnp.concatenate([upper, upper, w - upper], axis=1).astype(BF)
-
-
-def solve(gram, p, through):
+    copy.wait()
+
+
+def solve(gram, p, block):
     return pl.pallas_call(
         solve_kernel,
         in_specs=[VM, VM, ANY],
-        out_specs=[VM, ANY],
-        out_shape=[jax.ShapeDtypeStruct((112, 192), BF), jax.ShapeDtypeStruct(through.shape, F32)],
-        input_output_aliases={2: 1},
+        out_specs=[VM, HBM],
+        out_shape=[jax.ShapeDtypeStruct((112, 192), BF), jax.ShapeDtypeStruct(block.shape, F32)],
+        scratch_shapes=[DMA(())],
         compiler_params=params_of(8),
         cost_estimate=pl.CostEstimate(flops=10 ** 7, bytes_accessed=10 ** 7, transcendentals=0),
         name="solve",
-    )(gram, p, through)
+    )(gram, p, block)
 
 
 def finish(where, w, sides, delta, error, params, momentum, base, far):
@@ -346,32 +404,51 @@
     own = (own + turn(own, "x", 2)) + (turn(own, "x", 1) + turn(own, "x", 3))
     p_all, lhs, gram_own = prepare(steps, own, turn(own, "z", 2), turn(own, "z", 1), turn(own, "z", 3))
 
-    row64 = lax.broadcasted_iota(jnp.int32, gram_own.shape, 0) == 64
-    join = lambda a, b: jnp.where(row64, jnp.maximum(a, b), a + b)
     gram_near = swap(gram_own)
-    chip = join(gram_own, gram_near)
-    pair = join(chip, low(chip, "y"))
-    both, f_own, f_near = scales(gram_own, gram_near, pair, high(pair, "y"))
-    f_own, f_near = f_own.reshape(8, 1, 8, 128), f_near.reshape(8, 1, 8, 128)
+    chip, f_own, f_near = scales(gram_own, gram_near, gram_own, gram_near)
 
     arrived = [swap(v) for v in q_half(where, lhs, delta, error, True)]
     terms = q_half(where, lhs, delta, error, False)
+    keeps, sends = blend(where, terms, arrived, f_own, f_near, chip)
     half = lambda x, b: lax.dynamic_slice_in_dim(x, b * (x.shape[0] // 2), x.shape[0] // 2, 0)
+    gots = [low(send, route[0]) for send, route in zip(sends, ROUTES)]
+    rest = 4 * COUNTS[1]
+    chip_near = gots[1][rest:].reshape(72, 128)
+    gots = [got[:4 * c].reshape(4, c, 8, 128) for got, c in zip(gots, COUNTS)]
+    pair, g_own, g_near = scales(chip, chip_near, chip, chip_near)
     parts = []
     for k, route in enumerate(ROUTES):
-        blend = lambda b: half(terms[k], b) * half(f_own, b) + half(arrived[k], b) * half(f_near, b)
-        bit = lo_bit[route[0]]
-        send, keep = blend(1 - bit), blend(bit)
-        got = low(send, route[0])
-        if k == 2:
-            w_cat, keep = solve(both, p_all, keep)
-        for d in route[1:]:
-            take = lambda b: half(keep, b) + half(got, b)
-            send, keep = take(1 - lo_bit[d]), take(lo_bit[d])
-            got = low(send, d)
-        parts.append(keep[0] + got[0])
+        keep, got = keeps[k], gots[k]
+        ours, theirs = [g.reshape(8, 1, 8, 128) for g in (g_own, g_near)]
+        for step in range(3):
+            ours, theirs = [half(g, lo_bit[route[step]]) for g in (ours, theirs)]
+            scaled = route[step] == "y"
+            if step == 2:
+                parts.append(keep[0] * ours[0] + got[0] * theirs[0] if scaled else keep[0] + got[0])
+                break
+            bit = lo_bit[route[step + 1]]
+
+            def take(b):
+                if scaled:
+                    return half(keep, b) * half(ours, b) + half(got, b) * half(theirs, b)
+                return half(keep, b) + half(got, b)
+
+            send, keep = take(1 - bit), take(bit)
+            got = low(send, route[step + 1])
     mine = jnp.concatenate(parts, axis=0)
-    mine = half(mine, hi_bit["y"]) + high(half(mine, 1 - hi_bit["y"]), "y")
+    got = high(jnp.concatenate([half(mine, 1 - hi_bit["y"]), pair.reshape(9, 8, 128)], axis=0), "y")
+    pair_near = got[56:].reshape(72, 128)
+    both, h_own, h_near = scales(pair, pair_near, pair, pair_near)
+
+    def per_tile(h):
+        rows = h.reshape(8, 8, 128)
+        spread = []
+        for k, route in enumerate(ROUTES):
+            block = sum(lo_bit[d] * (4 >> i) for i, d in enumerate(route))
+            spread.append(jnp.broadcast_to(lax.dynamic_slice_in_dim(rows, block, 1, 0), (COUNTS[k], 8, 128)))
+        return half(jnp.concatenate(spread, axis=0), hi_bit["y"])
+
+    mine = half(mine, hi_bit["y"]) * per_tile(h_own) + got[:56] * per_tile(h_near)
     quarter = lambda a, b: lax.dynamic_slice_in_dim(mine, (2 * a + b) * 14, 14, 0)
     hz, hx = hi_bit["z"], hi_bit["x"]
     both_high = lambda x: lax.ppermute(x, REP, [(4 * i + j, 4 * (3 - i) + 3 - j) for i in range(4) for j in range(4)])
@@ -390,7 +467,8 @@
         for d in route[:0:-1]:
             v = in_order(lo_bit[d], v, low(v, d))
         sides.append((v, low(v, route[0])))
-    far = [swap(x) for pair in sides for x in pair]
+    w_cat, last = solve(both, p_all, sides[2][0])
+    far = [swap(x) for pair in sides[:2] for x in pair] + [swap(last), swap(sides[2][1])]
     near = [x for pair in sides for x in pair]
     base = finish(where, w_cat, near, delta, error, params, momentum, (), False)
     base = finish(where, w_cat, far, delta, error, params, momentum, base, True)

time: 179 us -> 173 us (0.966)
  other arithmetic: 12.5 us -> 3.88 us
  waiting for transfers between devices: 60 us -> 54.4 us
  local copies, waits for them, and re-layouts: 3.61 us -> 7.55 us
  starting transfers between devices: 56.2 us -> 59 us
    add x13 -> x10, other arithmetic: 11.2 us -> 2.73 us  [the longest x4 2.29 us: take(): return half(keep, b) + half(got, b)]
    unnamed x36 -> x32, local copies, waits for them, and re-layouts: 2.89 us -> 6.71 us
    ppermute x7 -> x6, waiting for transfers between devices: 16.5 us -> 12.7 us  [high(): return lax.ppermute(x, axis, [(i, 3 - i) for i in range(4)])]
    pallas_call x4 -> x7, Pallas kernels: 16.7 us -> 19.8 us  [the longest x2 10.5 us: q_half(): pl.pallas_call(kernel, in_specs=[SM, VM, HBM, HBM] + [ANY] * len(first),...]
    ppermute x10, waiting for transfers between devices: 2.9 us -> 0.37 us  [swap(): return lax.ppermute(x, 'c', [(0, 1), (1, 0)])]
    ppermute x7 -> x6, starting transfers between devices: 6.74 us -> 8.79 us  [high(): return lax.ppermute(x, axis, [(i, 3 - i) for i in range(4)])]
    ppermute x10, starting transfers between devices: 25 us -> 23.2 us  [swap(): return lax.ppermute(x, 'c', [(0, 1), (1, 0)])]
    ppermute x19 -> x18, starting transfers between devices: 7.3 us -> 8.89 us  [low(): return lax.ppermute(x, axis, [(i, i ^ 1) for i in range(4)])]
  transfers between devices with their start and end apart: 44 -> 42, of which waited for: 19 -> 20; matrix products, arithmetic and copies ran while one was open for 7% -> 2% of each run, Pallas kernels for 10% -> 11%
where the time goes in v3:
time: 173 us; the launch traced here: 172 us
  starting transfers between devices  59 us (34%)
  waiting for transfers between devices  54.4 us (31%)
  Pallas kernels  45.4 us (26%)
  local copies, waits for them, and re-layouts  7.55 us (4%)
  other arithmetic  3.88 us (2%)
  between operations  1.98 us (1%)
    ppermute x18, waiting for transfers between devices, low(): return lax.ppermute(x, axis, [(i, i ^ 1) for i in range(4)])  33 us
    ppermute x10, starting transfers between devices, swap(): return lax.ppermute(x, 'c', [(0, 1), (1, 0)])  23.2 us
    pallas_call x2, Pallas kernels, finish(): pl.pallas_call(kernel, in_specs=[SM, VM] + [ANY] * 6 + [HBM] * (4 + given...  15.6 us
    ppermute x6, waiting for transfers between devices, high(): return lax.ppermute(x, axis, [(i, 3 - i) for i in range(4)])  12.7 us
    pallas_call x2, Pallas kernels, q_half(): pl.pallas_call(kernel, in_specs=[SM, VM, HBM, HBM] + [ANY] * len(first),...  10.5 us
    ppermute x6, starting transfers between devices, turn(): return lax.ppermute(x, axis, [(i, (i + step) % 4) for i in range(4)])  10.2 us
    pallas_call x1, Pallas kernels, left_factor(): pl.pallas_call(p_kernel, in_specs=[SM, HBM, HBM, HBM], out_specs=VM, out_...  9.67 us
    ppermute x18, starting transfers between devices, low(): return lax.ppermute(x, axis, [(i, i ^ 1) for i in range(4)])  8.89 us
  transfers between devices with their start and end apart: 42, of which 20 were waited for; matrix products, arithmetic and copies ran while one was open for 2% of the time, Pallas kernels for 11%

profile of v3, /device:TPU:1, one launch (start us, length us, event | category | flops | bytes accessed | tf_op | source)
XLA Modules:
  0.0 172.3 jit_solution(15656290046926622321)
XLA Ops:
  1.3 9.7 %left_factor.1 = f32[64,128]{1,0:T(8,128)} custom-call(s32[1]{0:T(128)S(6)} %copy.15.steps_ref, bf16[1,112,28672]{2,1,0:T(8,128)(2,1)} %rest_6_.3, bf16[1,112,28672]{2,1,0:T(8,128)(2,1)} %rest_7_.3, bf16[64,28672]{1,0:T(8,128)(2,1)} %bitcast.77), custom_call_target="tpu_custom_call" | custom-call | tf_op jit(solution)/shard_map/left_factor/pallas_call | solution.py:84
  11.0 3.4 %collective-permute-start.2 = (f32[64,128]{1,0:T(8,128)}, f32[64,128]{1,0:T(8,128)S(1)}, u32[]{:S(2)}, u32[]{:S(2)}) collective-permute-start(f32[64,128]{1,0:T(8,128)} %left_factor.1), channel_id=1, source_target_pairs={{0,24},{8,0},{16,8},{24,16},{1,25},{9,1},{17,9},{25,17},{2,26},{10... | collective-permute-start | bytes 98312 | tf_op jit(solution)/shard_map/ppermute | solution.py:33
  16.1 2.5 %collective-permute-done.1 = f32[64,128]{1,0:T(8,128)S(1)} collective-permute-done((f32[64,128]{1,0:T(8,128)}, f32[64,128]{1,0:T(8,128)S(1)}, u32[]{:S(2)}, u32[]{:S(2)}) %collective-permute-start.1) | collective-permute-done | bytes 32800 | tf_op jit(solution)/shard_map/ppermute | solution.py:33
  19.8 3.8 %collective-permute-start.5 = (f32[64,128]{1,0:T(8,128)S(1)}, f32[64,128]{1,0:T(8,128)S(1)}, u32[]{:S(2)}, u32[]{:S(2)}) collective-permute-start(f32[64,128]{1,0:T(8,128)S(1)} %add_add_fusion.1.a_ref), channel_id=1, source_target_pairs={{0,96},{32,0},{64,32},{96,64},{1,97},{33,1},{65,33},{97,65},{2,98}... | collective-permute-start | bytes 98312 | tf_op jit(solution)/shard_map/ppermute | solution.py:33
  25.5 2.1 %collective-permute-done.4.c_ref = f32[64,128]{1,0:T(8,128)S(1)} collective-permute-done((f32[64,128]{1,0:T(8,128)S(1)}, f32[64,128]{1,0:T(8,128)S(1)}, u32[]{:S(2)}, u32[]{:S(2)}) %collective-permute-start.4) | collective-permute-done | bytes 32800 | tf_op jit(solution)/shard_map/ppermute | solution.py:33
  28.8 5.2 %q_far.1 = (f32[8,37,8,128]{3,2,1,0:T(8,128)}, f32[8,37,8,128]{3,2,1,0:T(8,128)}, f32[8,38,8,128]{3,2,1,0:T(8,128)}) custom-call(s32[5]{0:T(128)} %stack.23.s_ref, bf16[128,224]{1,0:T(8,128)(2,1)} %copy-done.4, bf16[1,112,28672]{2,1,0:T(8,128)(2,1)} %rest_6_.3, bf16[1,112,28672]{2,1,0:T(8,128)(2,1)} %rest_7_.3), custom_call_target="tpu_custom_call" | custom-call | flops 822083584 | bytes 10092544 | tf_op jit(solution)/shard_map/q_far/pallas_call | solution.py:176
  34.1 3.5 %collective-permute-start.9 = (f32[8,38,8,128]{3,2,1,0:T(8,128)}, f32[8,38,8,128]{3,2,1,0:T(8,128)S(1)}, u32[]{:S(2)}, u32[]{:S(2)}) collective-permute-start(f32[8,38,8,128]{3,2,1,0:T(8,128)} %get-tuple-element.43), channel_id=1, source_target_pairs={{0,1},{1,0},{2,3},{3,2},{4,5},{5,4},{6,7},{7,6},{8,9},{9,8},{10,11... | collective-permute-start | bytes 3735560 | tf_op jit(solution)/shard_map/ppermute | solution.py:45
  38.2 5.2 %q_own.1 = (f32[8,37,8,128]{3,2,1,0:T(8,128)}, f32[8,37,8,128]{3,2,1,0:T(8,128)}, f32[8,38,8,128]{3,2,1,0:T(8,128)}) custom-call(s32[5]{0:T(128)} %stack.23.s_ref, bf16[128,224]{1,0:T(8,128)(2,1)} %copy-done.4, bf16[1,112,28672]{2,1,0:T(8,128)(2,1)} %rest_6_.3, bf16[1,112,28672]{2,1,0:T(8,128)(2,1)} %rest_7_.3), custom_call_target="tpu_custom_call" | custom-call | flops 822083584 | bytes 10092544 | tf_op jit(solution)/shard_map/q_own/pallas_call | solution.py:176
  47.8 2.8 %blend.1 = (f32[4,37,8,128]{3,2,1,0:T(8,128)S(1)}, f32[4,37,8,128]{3,2,1,0:T(8,128)S(1)}, f32[4,38,8,128]{3,2,1,0:T(8,128)S(1)}, f32[148,8,128]{2,1,0:T(8,128)},...) custom-call(s32[5]{0:T(128)S(1)} %copy-done.6, f32[8,37,8,128]{3,2,1,0:T(8,128)S(1)} %copy-done.2, ...), custom_call_target="tpu_custom_call" | custom-call | flops 1000000 | bytes 11000000 | tf_op jit(solution)/shard_map/blend/pallas_call | solution.py:224
  52.6 13.3 %collective-permute-done.11 = f32[148,8,128]{2,1,0:T(8,128)} collective-permute-done((f32[148,8,128]{2,1,0:T(8,128)}, f32[148,8,128]{2,1,0:T(8,128)}, u32[]{:S(2)}, u32[]{:S(2)}) %collective-permute-start.11) | collective-permute-done | bytes 606240 | tf_op jit(solution)/shard_map/ppermute | solution.py:37
  70.6 4.0 %collective-permute-done.12 = f32[2,37,8,128]{3,2,1,0:T(8,128)S(1)} collective-permute-done((f32[2,37,8,128]{3,2,1,0:T(8,128)S(1)}, f32[2,37,8,128]{3,2,1,0:T(8,128)S(1)}, u32[]{:S(2)}, u32[]{:S(2)}) %collective-permute-start.12) | collective-permute-done | bytes 303136 | tf_op jit(solution)/shard_map/ppermute | solution.py:37
  75.0 1.9 %collective-permute-done.17 = f32[2,38,8,128]{3,2,1,0:T(8,128)S(1)} collective-permute-done((f32[2,38,8,128]{3,2,1,0:T(8,128)S(1)}, f32[2,38,8,128]{3,2,1,0:T(8,128)S(1)}, u32[]{:S(2)}, u32[]{:S(2)}) %collective-permute-start.17) | collective-permute-done | bytes 311328 | tf_op jit(solution)/shard_map/ppermute | solution.py:37
  78.4 2.4 %collective-permute-done.13 = f32[1,37,8,128]{3,2,1,0:T(8,128)S(1)} collective-permute-done((f32[1,37,8,128]{3,2,1,0:T(8,128)S(1)}, f32[1,37,8,128]{3,2,1,0:T(8,128)S(1)}, u32[]{:S(2)}, u32[]{:S(2)}) %collective-permute-start.13) | collective-permute-done | bytes 151584 | tf_op jit(solution)/shard_map/ppermute | solution.py:37
  81.8 2.8 %collective-permute-start.19 = (f32[65,8,128]{2,1,0:T(8,128)S(1)}, f32[65,8,128]{2,1,0:T(8,128)S(1)}, u32[]{:S(2)}, u32[]{:S(2)}) collective-permute-start(f32[65,8,128]{2,1,0:T(8,128)S(1)} %pad_maximum_fusion.1), channel_id=1, source_target_pairs={{0,6},{2,4},{4,2},{6,0},{1,7},{3,5},{5,3},{7,1},{8,14},{10,12},{12... | collective-permute-start | bytes 798728 | tf_op jit(solution)/shard_map/ppermute | solution.py:41
  84.6 3.8 %collective-permute-done.19 = f32[65,8,128]{2,1,0:T(8,128)S(1)} collective-permute-done((f32[65,8,128]{2,1,0:T(8,128)S(1)}, f32[65,8,128]{2,1,0:T(8,128)S(1)}, u32[]{:S(2)}, u32[]{:S(2)}) %collective-permute-start.19) | collective-permute-done | bytes 266272 | tf_op jit(solution)/shard_map/ppermute | solution.py:41
  88.9 5.8 %collective-permute-start.20 = (f32[14,8,128]{2,1,0:T(8,128)S(1)}, f32[14,8,128]{2,1,0:T(8,128)S(1)}, u32[]{:S(2)}, u32[]{:S(2)}) collective-permute-start(f32[14,8,128]{2,1,0:T(8,128)S(1)} %get-tuple-element.75), channel_id=1, source_target_pairs={{0,120},{8,112},{16,104},{24,96},{32,88},{40,80},{48,72},{56,64},{... | collective-permute-start | bytes 172040 | tf_op jit(solution)/shard_map/ppermute | solution.py:454
  96.3 2.7 %collective-permute-done.22 = f32[14,8,128]{2,1,0:T(8,128)S(1)} collective-permute-done((f32[14,8,128]{2,1,0:T(8,128)S(1)}, f32[14,8,128]{2,1,0:T(8,128)S(1)}, u32[]{:S(2)}, u32[]{:S(2)}) %collective-permute-start.22) | collective-permute-done | bytes 57376 | tf_op jit(solution)/shard_map/ppermute | solution.py:41
  99.0 2.8 %collective-permute-start.23 = (f32[14,8,128]{2,1,0:T(8,128)S(1)}, f32[14,8,128]{2,1,0:T(8,128)S(1)}, u32[]{:S(2)}, u32[]{:S(2)}) collective-permute-start(f32[14,8,128]{2,1,0:T(8,128)S(1)} %add_add_fusion), channel_id=1, source_target_pairs={{0,24},{8,16},{16,8},{24,0},{1,25},{9,17},{17,9},{25,1},{2,26},{10... | collective-permute-start | bytes 172040 | tf_op jit(solution)/shard_map/ppermute | solution.py:41
  102.1 2.2 %collective-permute-start.25 = (f32[14,8,128]{2,1,0:T(8,128)S(1)}, f32[14,8,128]{2,1,0:T(8,128)S(1)}, u32[]{:S(2)}, u32[]{:S(2)}) collective-permute-start(f32[14,8,128]{2,1,0:T(8,128)S(1)} %add_add_fusion), channel_id=1, source_target_pairs={{0,120},{8,112},{16,104},{24,96},{32,88},{40,80},{48,72},{56,64},{... | collective-permute-start | bytes 172040 | tf_op jit(solution)/shard_map/ppermute | solution.py:454
  104.2 2.4 %collective-permute-done.24 = f32[14,8,128]{2,1,0:T(8,128)S(1)} collective-permute-done((f32[14,8,128]{2,1,0:T(8,128)S(1)}, f32[14,8,128]{2,1,0:T(8,128)S(1)}, u32[]{:S(2)}, u32[]{:S(2)}) %collective-permute-start.24) | collective-permute-done | bytes 57376 | tf_op jit(solution)/shard_map/ppermute | solution.py:41
  108.5 2.5 %collective-permute-start.26 = (f32[56,8,128]{2,1,0:T(8,128)S(1)}, f32[56,8,128]{2,1,0:T(8,128)S(1)}, u32[]{:S(2)}, u32[]{:S(2)}) collective-permute-start(f32[56,8,128]{2,1,0:T(8,128)S(1)} %maximum_select_fusion.7), channel_id=1, source_target_pairs={{0,6},{2,4},{4,2},{6,0},{1,7},{3,5},{5,3},{7,1},{8,14},{10,12},{12... | collective-permute-start | bytes 688136 | tf_op jit(solution)/shard_map/ppermute | solution.py:41
  111.0 3.9 %collective-permute-done.26 = f32[56,8,128]{2,1,0:T(8,128)S(1)} collective-permute-done((f32[56,8,128]{2,1,0:T(8,128)S(1)}, f32[56,8,128]{2,1,0:T(8,128)S(1)}, u32[]{:S(2)}, u32[]{:S(2)}) %collective-permute-start.26) | collective-permute-done | bytes 229408 | tf_op jit(solution)/shard_map/ppermute | solution.py:41
  115.3 3.8 %collective-permute-done.34 = f32[1,37,8,128]{3,2,1,0:T(8,128)S(1)} collective-permute-done((f32[1,37,8,128]{3,2,1,0:T(8,128)S(1)}, f32[1,37,8,128]{3,2,1,0:T(8,128)S(1)}, u32[]{:S(2)}, u32[]{:S(2)}) %collective-permute-start.34) | collective-permute-done | bytes 151584 | tf_op jit(solution)/shard_map/ppermute | solution.py:37
  119.3 1.8 %collective-permute-start.28 = (f32[2,38,8,128]{3,2,1,0:T(8,128)S(1)}, f32[2,38,8,128]{3,2,1,0:T(8,128)S(1)}, u32[]{:S(2)}, u32[]{:S(2)}) collective-permute-start(f32[2,38,8,128]{3,2,1,0:T(8,128)S(1)} %maximum_select_fusion.4), channel_id=1, source_target_pairs={{0,8},{8,0},{16,24},{24,16},{1,9},{9,1},{17,25},{25,17},{2,10},{10... | collective-permute-start | bytes 933896 | tf_op jit(solution)/shard_map/ppermute | solution.py:37
  121.2 3.6 %collective-permute-done.35 = f32[2,37,8,128]{3,2,1,0:T(8,128)S(1)} collective-permute-done((f32[2,37,8,128]{3,2,1,0:T(8,128)S(1)}, f32[2,37,8,128]{3,2,1,0:T(8,128)S(1)}, u32[]{:S(2)}, u32[]{:S(2)}) %collective-permute-start.35) | collective-permute-done | bytes 303136 | tf_op jit(solution)/shard_map/ppermute | solution.py:37
  125.0 12.5 %collective-permute-start.36 = (f32[4,37,8,128]{3,2,1,0:T(8,128)S(1)}, f32[4,37,8,128]{3,2,1,0:T(8,128)S(1)}, u32[]{:S(2)}, u32[]{:S(2)}) collective-permute-start(f32[4,37,8,128]{3,2,1,0:T(8,128)S(1)} %maximum_select_fusion.2.rest_2_), channel_id=1, source_target_pairs={{0,1},{1,0},{2,3},{3,2},{4,5},{5,4},{6,7},{7,6},{8,9},{9,8},{10,11... | collective-permute-start | bytes 1818632 | tf_op jit(solution)/shard_map/ppermute | solution.py:45
  138.2 6.3 %solve.1 = (bf16[112,192]{1,0:T(8,128)(2,1)S(1)}, f32[4,38,8,128]{3,2,1,0:T(8,128)S(1)}) custom-call(f32[72,128]{1,0:T(8,128)S(1)} %get-tuple-element.55.gram_ref, f32[112,64]{1,0:T(8,128)S(1)} %get-tuple-element.56.p_ref, f32[4,38,8,128]{3,2,1,0:T(8,128)S(1)} %maximum_select_fusion.block_ref.rest_4_), custom_call_target="tpu_custom_call" | custom-call | flops 10000000 | bytes 10000000 | tf_op jit(solution)/shard_map/solve/pallas_call | solution.py:294
  145.1 3.4 %collective-permute-start.39 = (f32[4,38,8,128]{3,2,1,0:T(8,128)S(1)}, f32[4,38,8,128]{3,2,1,0:T(8,128)S(1)}, u32[]{:S(2)}, u32[]{:S(2)}) collective-permute-start(f32[4,38,8,128]{3,2,1,0:T(8,128)S(1)} %get-tuple-element.60), channel_id=1, source_target_pairs={{0,1},{1,0},{2,3},{3,2},{4,5},{5,4},{6,7},{7,6},{8,9},{9,8},{10,11... | collective-permute-start | bytes 1867784 | tf_op jit(solution)/shard_map/ppermute | solution.py:45
  148.5 3.1 %collective-permute-done.40.rest_5_ = f32[4,38,8,128]{3,2,1,0:T(8,128)S(1)} collective-permute-done((f32[4,38,8,128]{3,2,1,0:T(8,128)S(1)}, f32[4,38,8,128]{3,2,1,0:T(8,128)S(1)}, u32[]{:S(2)}, u32[]{:S(2)}) %collective-permute-start.40) | collective-permute-done | bytes 622624 | tf_op jit(solution)/shard_map/ppermute | solution.py:37
  151.6 2.5 %collective-permute-start.41 = (f32[4,38,8,128]{3,2,1,0:T(8,128)S(1)}, f32[4,38,8,128]{3,2,1,0:T(8,128)S(1)}, u32[]{:S(2)}, u32[]{:S(2)}) collective-permute-start(f32[4,38,8,128]{3,2,1,0:T(8,128)S(1)} %collective-permute-done.40.rest_5_), channel_id=1, source_target_pairs={{0,1},{1,0},{2,3},{3,2},{4,5},{5,4},{6,7},{7,6},{8,9},{9,8},{10,11... | collective-permute-start | bytes 1867784 | tf_op jit(solution)/shard_map/ppermute | solution.py:45
  154.8 7.0 %finish_own.1 = (bf16[1,112,28672]{2,1,0:T(8,128)(2,1)}, f32[112,1792]{1,0:T(8,128)}, f32[112,1792]{1,0:T(8,128)}) custom-call(s32[5]{0:T(128)} %stack.23.s_ref, bf16[112,192]{1,0:T(8,128)(2,1)} %copy-done.5, f32[4,37,8,128]{3,2,1,0:T(8,128)} %copy-done.8, f32[4,37,8,128]{3,2,1,0:T(8,128)} %collective-permute-done.32.rest_1_, f32[4,37,8,128]{3,2,1,0:T(8,128)} %copy-done.7, ...), custom_call_target="tpu_custom_call" | custom-call | flops 616562688 | bytes 13303808 | tf_op jit(solution)/shard_map/finish_own/pallas_call | solution.py:370
  163.5 8.6 %finish_far.1 = (bf16[1,112,28672]{2,1,0:T(8,128)(2,1)}, f32[112,1792]{1,0:T(8,128)}, f32[112,1792]{1,0:T(8,128)}) custom-call(s32[5]{0:T(128)} %stack.23.s_ref, bf16[112,192]{1,0:T(8,128)(2,1)} %copy-done.5, f32[4,37,8,128]{3,2,1,0:T(8,128)} %copy-done.13, ...), custom_call_target="tpu_custom_call", output_to_operand_aliasing={{0}: (12, {}), {1}: (13, {}), {2}: (14, {})} | custom-call | flops 616562688 | bytes 13303808 | tf_op jit(solution)/shard_map/finish_far/pallas_call | solution.py:370
  (137 shorter events, 29.1 us)
Async XLA Ops:
  11.0 5.1 %collective-permute-start.2 = (f32[64,128]{1,0:T(8,128)}, f32[64,128]{1,0:T(8,128)S(1)}, u32[]{:S(2)}, u32[]{:S(2)}) collective-permute-start(f32[64,128]{1,0:T(8,128)} %left_factor.1), channel_id=1, source_target_pairs={{0,24},{8,0},{16,8},{24,16},{1,25},{9,1},{17,9},{25,17},{2,26},{10... | collective-permute-start | bytes 98312 | tf_op jit(solution)/shard_map/ppermute | solution.py:33
  19.8 5.7 %collective-permute-start.5 = (f32[64,128]{1,0:T(8,128)S(1)}, f32[64,128]{1,0:T(8,128)S(1)}, u32[]{:S(2)}, u32[]{:S(2)}) collective-permute-start(f32[64,128]{1,0:T(8,128)S(1)} %add_add_fusion.1.a_ref), channel_id=1, source_target_pairs={{0,96},{32,0},{64,32},{96,64},{1,97},{33,1},{65,33},{97,65},{2,98}... | collective-permute-start | bytes 98312 | tf_op jit(solution)/shard_map/ppermute | solution.py:33
  34.1 9.8 %collective-permute-start.9 = (f32[8,38,8,128]{3,2,1,0:T(8,128)}, f32[8,38,8,128]{3,2,1,0:T(8,128)S(1)}, u32[]{:S(2)}, u32[]{:S(2)}) collective-permute-start(f32[8,38,8,128]{3,2,1,0:T(8,128)} %get-tuple-element.43), channel_id=1, source_target_pairs={{0,1},{1,0},{2,3},{3,2},{4,5},{5,4},{6,7},{7,6},{8,9},{9,8},{10,11... | collective-permute-start | bytes 3735560 | tf_op jit(solution)/shard_map/ppermute | solution.py:45
  37.6 5.9 %collective-permute-start.7 = (f32[8,37,8,128]{3,2,1,0:T(8,128)}, f32[8,37,8,128]{3,2,1,0:T(8,128)S(1)}, u32[]{:S(2)}, u32[]{:S(2)}) collective-permute-start(f32[8,37,8,128]{3,2,1,0:T(8,128)} %get-tuple-element.41), channel_id=1, source_target_pairs={{0,1},{1,0},{2,3},{3,2},{4,5},{5,4},{6,7},{7,6},{8,9},{9,8},{10,11... | collective-permute-start | bytes 3637256 | tf_op jit(solution)/shard_map/ppermute | solution.py:45
  37.7 6.2 %collective-permute-start.8 = (f32[8,37,8,128]{3,2,1,0:T(8,128)}, f32[8,37,8,128]{3,2,1,0:T(8,128)S(1)}, u32[]{:S(2)}, u32[]{:S(2)}) collective-permute-start(f32[8,37,8,128]{3,2,1,0:T(8,128)} %get-tuple-element.42), channel_id=1, source_target_pairs={{0,1},{1,0},{2,3},{3,2},{4,5},{5,4},{6,7},{7,6},{8,9},{9,8},{10,11... | collective-permute-start | bytes 3637256 | tf_op jit(solution)/shard_map/ppermute | solution.py:45
  38.1 5.3 %collective-permute-start.6 = (f32[72,128]{1,0:T(8,128)S(1)}, f32[72,128]{1,0:T(8,128)S(1)}, u32[]{:S(2)}, u32[]{:S(2)}) collective-permute-start(f32[72,128]{1,0:T(8,128)S(1)} %get-tuple-element.35.a_ref.refs_0_), channel_id=1, source_target_pairs={{0,1},{1,0},{2,3},{3,2},{4,5},{5,4},{6,7},{7,6},{8,9},{9,8},{10,11... | collective-permute-start | bytes 110600 | tf_op jit(solution)/shard_map/ppermute | solution.py:45
  50.6 15.3 %collective-permute-start.11 = (f32[148,8,128]{2,1,0:T(8,128)}, f32[148,8,128]{2,1,0:T(8,128)}, u32[]{:S(2)}, u32[]{:S(2)}) collective-permute-start(f32[148,8,128]{2,1,0:T(8,128)} %get-tuple-element.49), channel_id=1, source_target_pairs={{0,8},{8,0},{16,24},{24,16},{1,9},{9,1},{17,25},{25,17},{2,10},{10... | collective-permute-start | bytes 1818632 | tf_op jit(solution)/shard_map/ppermute | solution.py:37
  51.1 17.3 %collective-permute-start.16 = (f32[152,8,128]{2,1,0:T(8,128)S(1)}, f32[152,8,128]{2,1,0:T(8,128)}, u32[]{:S(2)}, u32[]{:S(2)}) collective-permute-start(f32[152,8,128]{2,1,0:T(8,128)S(1)} %get-tuple-element.54), channel_id=1, source_target_pairs={{0,32},{32,0},{64,96},{96,64},{1,33},{33,1},{65,97},{97,65},{2,34}... | collective-permute-start | bytes 1867784 | tf_op jit(solution)/shard_map/ppermute | solution.py:37
  51.3 18.7 %collective-permute-start.10 = (f32[157,8,128]{2,1,0:T(8,128)}, f32[157,8,128]{2,1,0:T(8,128)S(1)}, u32[]{:S(2)}, u32[]{:S(2)}) collective-permute-start(f32[157,8,128]{2,1,0:T(8,128)} %get-tuple-element.46), channel_id=1, source_target_pairs={{0,2},{2,0},{4,6},{6,4},{1,3},{3,1},{5,7},{7,5},{8,10},{10,8},{12,... | collective-permute-start | bytes 1929224 | tf_op jit(solution)/shard_map/ppermute | solution.py:37
  67.0 7.6 %collective-permute-start.12 = (f32[2,37,8,128]{3,2,1,0:T(8,128)S(1)}, f32[2,37,8,128]{3,2,1,0:T(8,128)S(1)}, u32[]{:S(2)}, u32[]{:S(2)}) collective-permute-start(f32[2,37,8,128]{3,2,1,0:T(8,128)S(1)} %get-tuple-element.70), channel_id=1, source_target_pairs={{0,2},{2,0},{4,6},{6,4},{1,3},{3,1},{5,7},{7,5},{8,10},{10,8},{12,... | collective-permute-start | bytes 909320 | tf_op jit(solution)/shard_map/ppermute | solution.py:37
  69.5 7.5 %collective-permute-start.17 = (f32[2,38,8,128]{3,2,1,0:T(8,128)S(1)}, f32[2,38,8,128]{3,2,1,0:T(8,128)S(1)}, u32[]{:S(2)}, u32[]{:S(2)}) collective-permute-start(f32[2,38,8,128]{3,2,1,0:T(8,128)S(1)} %get-tuple-element.68), channel_id=1, source_target_pairs={{0,8},{8,0},{16,24},{24,16},{1,9},{9,1},{17,25},{25,17},{2,10},{10... | collective-permute-start | bytes 933896 | tf_op jit(solution)/shard_map/ppermute | solution.py:37
  70.3 7.0 %collective-permute-start.14 = (f32[2,37,8,128]{3,2,1,0:T(8,128)S(1)}, f32[2,37,8,128]{3,2,1,0:T(8,128)S(1)}, u32[]{:S(2)}, u32[]{:S(2)}) collective-permute-start(f32[2,37,8,128]{3,2,1,0:T(8,128)S(1)} %get-tuple-element.72), channel_id=1, source_target_pairs={{0,32},{32,0},{64,96},{96,64},{1,33},{33,1},{65,97},{97,65},{2,34}... | collective-permute-start | bytes 909320 | tf_op jit(solution)/shard_map/ppermute | solution.py:37
  74.6 6.3 %collective-permute-start.13 = (f32[1,37,8,128]{3,2,1,0:T(8,128)S(1)}, f32[1,37,8,128]{3,2,1,0:T(8,128)S(1)}, u32[]{:S(2)}, u32[]{:S(2)}) collective-permute-start(f32[1,37,8,128]{3,2,1,0:T(8,128)S(1)} %multiply_add_fusion.2), channel_id=1, source_target_pairs={{0,32},{32,0},{64,96},{96,64},{1,33},{33,1},{65,97},{97,65},{2,34}... | collective-permute-start | bytes 454664 | tf_op jit(solution)/shard_map/ppermute | solution.py:37
  81.8 6.6 %collective-permute-start.19 = (f32[65,8,128]{2,1,0:T(8,128)S(1)}, f32[65,8,128]{2,1,0:T(8,128)S(1)}, u32[]{:S(2)}, u32[]{:S(2)}) collective-permute-start(f32[65,8,128]{2,1,0:T(8,128)S(1)} %pad_maximum_fusion.1), channel_id=1, source_target_pairs={{0,6},{2,4},{4,2},{6,0},{1,7},{3,5},{5,3},{7,1},{8,14},{10,12},{12... | collective-permute-start | bytes 798728 | tf_op jit(solution)/shard_map/ppermute | solution.py:41
  88.9 7.4 %collective-permute-start.20 = (f32[14,8,128]{2,1,0:T(8,128)S(1)}, f32[14,8,128]{2,1,0:T(8,128)S(1)}, u32[]{:S(2)}, u32[]{:S(2)}) collective-permute-start(f32[14,8,128]{2,1,0:T(8,128)S(1)} %get-tuple-element.75), channel_id=1, source_target_pairs={{0,120},{8,112},{16,104},{24,96},{32,88},{40,80},{48,72},{56,64},{... | collective-permute-start | bytes 172040 | tf_op jit(solution)/shard_map/ppermute | solution.py:454
  99.0 5.3 %collective-permute-start.23 = (f32[14,8,128]{2,1,0:T(8,128)S(1)}, f32[14,8,128]{2,1,0:T(8,128)S(1)}, u32[]{:S(2)}, u32[]{:S(2)}) collective-permute-start(f32[14,8,128]{2,1,0:T(8,128)S(1)} %add_add_fusion), channel_id=1, source_target_pairs={{0,24},{8,16},{16,8},{24,0},{1,25},{9,17},{17,9},{25,1},{2,26},{10... | collective-permute-start | bytes 172040 | tf_op jit(solution)/shard_map/ppermute | solution.py:41
  101.7 4.9 %collective-permute-start.24 = (f32[14,8,128]{2,1,0:T(8,128)S(1)}, f32[14,8,128]{2,1,0:T(8,128)S(1)}, u32[]{:S(2)}, u32[]{:S(2)}) collective-permute-start(f32[14,8,128]{2,1,0:T(8,128)S(1)} %add_add_fusion), channel_id=1, source_target_pairs={{0,96},{32,64},{64,32},{96,0},{1,97},{33,65},{65,33},{97,1},{2,98}... | collective-permute-start | bytes 172040 | tf_op jit(solution)/shard_map/ppermute | solution.py:41
  102.1 6.3 %collective-permute-start.25 = (f32[14,8,128]{2,1,0:T(8,128)S(1)}, f32[14,8,128]{2,1,0:T(8,128)S(1)}, u32[]{:S(2)}, u32[]{:S(2)}) collective-permute-start(f32[14,8,128]{2,1,0:T(8,128)S(1)} %add_add_fusion), channel_id=1, source_target_pairs={{0,120},{8,112},{16,104},{24,96},{32,88},{40,80},{48,72},{56,64},{... | collective-permute-start | bytes 172040 | tf_op jit(solution)/shard_map/ppermute | solution.py:454
  108.5 6.5 %collective-permute-start.26 = (f32[56,8,128]{2,1,0:T(8,128)S(1)}, f32[56,8,128]{2,1,0:T(8,128)S(1)}, u32[]{:S(2)}, u32[]{:S(2)}) collective-permute-start(f32[56,8,128]{2,1,0:T(8,128)S(1)} %maximum_select_fusion.7), channel_id=1, source_target_pairs={{0,6},{2,4},{4,2},{6,0},{1,7},{3,5},{5,3},{7,1},{8,14},{10,12},{12... | collective-permute-start | bytes 688136 | tf_op jit(solution)/shard_map/ppermute | solution.py:41
  115.2 5.9 %collective-permute-start.29 = (f32[1,37,8,128]{3,2,1,0:T(8,128)S(1)}, f32[1,37,8,128]{3,2,1,0:T(8,128)S(1)}, u32[]{:S(2)}, u32[]{:S(2)}) collective-permute-start(f32[1,37,8,128]{3,2,1,0:T(8,128)S(1)} %get-tuple-element.74), channel_id=1, source_target_pairs={{0,32},{32,0},{64,96},{96,64},{1,33},{33,1},{65,97},{97,65},{2,34}... | collective-permute-start | bytes 454664 | tf_op jit(solution)/shard_map/ppermute | solution.py:37
  119.1 5.7 %collective-permute-start.35 = (f32[2,37,8,128]{3,2,1,0:T(8,128)S(1)}, f32[2,37,8,128]{3,2,1,0:T(8,128)S(1)}, u32[]{:S(2)}, u32[]{:S(2)}) collective-permute-start(f32[2,37,8,128]{3,2,1,0:T(8,128)S(1)} %maximum_select_fusion.6), channel_id=1, source_target_pairs={{0,32},{32,0},{64,96},{96,64},{1,33},{33,1},{65,97},{97,65},{2,34}... | collective-permute-start | bytes 909320 | tf_op jit(solution)/shard_map/ppermute | solution.py:37
  119.3 18.3 %collective-permute-start.28 = (f32[2,38,8,128]{3,2,1,0:T(8,128)S(1)}, f32[2,38,8,128]{3,2,1,0:T(8,128)S(1)}, u32[]{:S(2)}, u32[]{:S(2)}) collective-permute-start(f32[2,38,8,128]{3,2,1,0:T(8,128)S(1)} %maximum_select_fusion.4), channel_id=1, source_target_pairs={{0,8},{8,0},{16,24},{24,16},{1,9},{9,1},{17,25},{25,17},{2,10},{10... | collective-permute-start | bytes 933896 | tf_op jit(solution)/shard_map/ppermute | solution.py:37
  121.1 16.6 %collective-permute-start.30 = (f32[2,37,8,128]{3,2,1,0:T(8,128)S(1)}, f32[2,37,8,128]{3,2,1,0:T(8,128)S(1)}, u32[]{:S(2)}, u32[]{:S(2)}) collective-permute-start(f32[2,37,8,128]{3,2,1,0:T(8,128)S(1)} %maximum_select_fusion.5), channel_id=1, source_target_pairs={{0,2},{2,0},{4,6},{6,4},{1,3},{3,1},{5,7},{7,5},{8,10},{10,8},{12,... | collective-permute-start | bytes 909320 | tf_op jit(solution)/shard_map/ppermute | solution.py:37
  124.9 29.2 %collective-permute-start.37 = (f32[4,37,8,128]{3,2,1,0:T(8,128)S(1)}, f32[4,37,8,128]{3,2,1,0:T(8,128)}, u32[]{:S(2)}, u32[]{:S(2)}) collective-permute-start(f32[4,37,8,128]{3,2,1,0:T(8,128)S(1)} %maximum_select_fusion.2.rest_2_), channel_id=1, source_target_pairs={{0,2},{2,0},{4,6},{6,4},{1,3},{3,1},{5,7},{7,5},{8,10},{10,8},{12,... | collective-permute-start | bytes 1818632 | tf_op jit(solution)/shard_map/ppermute | solution.py:37
  125.0 29.2 %collective-permute-start.36 = (f32[4,37,8,128]{3,2,1,0:T(8,128)S(1)}, f32[4,37,8,128]{3,2,1,0:T(8,128)S(1)}, u32[]{:S(2)}, u32[]{:S(2)}) collective-permute-start(f32[4,37,8,128]{3,2,1,0:T(8,128)S(1)} %maximum_select_fusion.2.rest_2_), channel_id=1, source_target_pairs={{0,1},{1,0},{2,3},{3,2},{4,5},{5,4},{6,7},{7,6},{8,9},{9,8},{10,11... | collective-permute-start | bytes 1818632 | tf_op jit(solution)/shard_map/ppermute | solution.py:45
  137.6 14.0 %collective-permute-start.40 = (f32[4,38,8,128]{3,2,1,0:T(8,128)S(1)}, f32[4,38,8,128]{3,2,1,0:T(8,128)S(1)}, u32[]{:S(2)}, u32[]{:S(2)}) collective-permute-start(f32[4,38,8,128]{3,2,1,0:T(8,128)S(1)} %maximum_select_fusion.block_ref.rest_4_), channel_id=1, source_target_pairs={{0,32},{32,0},{64,96},{96,64},{1,33},{33,1},{65,97},{97,65},{2,34}... | collective-permute-start | bytes 1867784 | tf_op jit(solution)/shard_map/ppermute | solution.py:37
  137.8 16.9 %collective-permute-start.32 = (f32[4,37,8,128]{3,2,1,0:T(8,128)S(1)}, f32[4,37,8,128]{3,2,1,0:T(8,128)}, u32[]{:S(2)}, u32[]{:S(2)}) collective-permute-start(f32[4,37,8,128]{3,2,1,0:T(8,128)S(1)} %maximum_select_fusion.1.rest_0_), channel_id=1, source_target_pairs={{0,8},{8,0},{16,24},{24,16},{1,9},{9,1},{17,25},{25,17},{2,10},{10... | collective-permute-start | bytes 1818632 | tf_op jit(solution)/shard_map/ppermute | solution.py:37
  145.1 16.7 %collective-permute-start.39 = (f32[4,38,8,128]{3,2,1,0:T(8,128)S(1)}, f32[4,38,8,128]{3,2,1,0:T(8,128)S(1)}, u32[]{:S(2)}, u32[]{:S(2)}) collective-permute-start(f32[4,38,8,128]{3,2,1,0:T(8,128)S(1)} %get-tuple-element.60), channel_id=1, source_target_pairs={{0,1},{1,0},{2,3},{3,2},{4,5},{5,4},{6,7},{7,6},{8,9},{9,8},{10,11... | collective-permute-start | bytes 1867784 | tf_op jit(solution)/shard_map/ppermute | solution.py:45
  151.6 10.3 %collective-permute-start.41 = (f32[4,38,8,128]{3,2,1,0:T(8,128)S(1)}, f32[4,38,8,128]{3,2,1,0:T(8,128)S(1)}, u32[]{:S(2)}, u32[]{:S(2)}) collective-permute-start(f32[4,38,8,128]{3,2,1,0:T(8,128)S(1)} %collective-permute-done.40.rest_5_), channel_id=1, source_target_pairs={{0,1},{1,0},{2,3},{3,2},{4,5},{5,4},{6,7},{7,6},{8,9},{9,8},{10,11... | collective-permute-start | bytes 1867784 | tf_op jit(solution)/shard_map/ppermute | solution.py:45
  154.2 7.7 %collective-permute-start.31 = (f32[4,37,8,128]{3,2,1,0:T(8,128)S(1)}, f32[4,37,8,128]{3,2,1,0:T(8,128)S(1)}, u32[]{:S(2)}, u32[]{:S(2)}) collective-permute-start(f32[4,37,8,128]{3,2,1,0:T(8,128)S(1)} %maximum_select_fusion.1.rest_0_), channel_id=1, source_target_pairs={{0,1},{1,0},{2,3},{3,2},{4,5},{5,4},{6,7},{7,6},{8,9},{9,8},{10,11... | collective-permute-start | bytes 1818632 | tf_op jit(solution)/shard_map/ppermute | solution.py:45
  154.3 7.6 %collective-permute-start.38 = (f32[4,37,8,128]{3,2,1,0:T(8,128)}, f32[4,37,8,128]{3,2,1,0:T(8,128)S(1)}, u32[]{:S(2)}, u32[]{:S(2)}) collective-permute-start(f32[4,37,8,128]{3,2,1,0:T(8,128)} %collective-permute-done.37.rest_3_), channel_id=1, source_target_pairs={{0,1},{1,0},{2,3},{3,2},{4,5},{5,4},{6,7},{7,6},{8,9},{9,8},{10,11... | collective-permute-start | bytes 1818632 | tf_op jit(solution)/shard_map/ppermute | solution.py:45
  154.7 7.2 %collective-permute-start.33 = (f32[4,37,8,128]{3,2,1,0:T(8,128)}, f32[4,37,8,128]{3,2,1,0:T(8,128)S(1)}, u32[]{:S(2)}, u32[]{:S(2)}) collective-permute-start(f32[4,37,8,128]{3,2,1,0:T(8,128)} %collective-permute-done.32.rest_1_), channel_id=1, source_target_pairs={{0,1},{1,0},{2,3},{3,2},{4,5},{5,4},{6,7},{7,6},{8,9},{9,8},{10,11... | collective-permute-start | bytes 1818632 | tf_op jit(solution)/shard_map/ppermute | solution.py:45
  (26 other events, 124.4 us)

commit v4 on v3

--- a/solution.py
+++ b/solution.py
@@ -155,7 +155,9 @@
 
     def kernel(s_ref, lhs_ref, d_ref, e_ref, *rest):
         rest = rest[len(first):]
-        out_refs, (both_ref, v_ref, sem, out_sem) = rest[:3], rest[3:]
+        out_refs, (both_ref, sem), rest = rest[:3], rest[3:5], rest[5:]
+        if far:
+            v_ref, out_sem = rest
         side = 1 - s_ref[0] if far else s_ref[0]
         copies = [load_block(side, s, *parts[s], d_ref, e_ref, both_ref, sem) for s in range(n)]
         outs = []
@@ -164,10 +166,15 @@
                 copy.wait()
             r = lax.dot_general(lhs_ref[...], both_ref[s], (((1,), (0,)), ((), ())), preferred_element_type=F32)
             v = r[0:64] + r[64:128]
-            for i in range(8):
-                for t in range(end - begin):
-                    v_ref[i, begin + t] = v[8 * i:8 * i + 8, 128 * t:128 * t + 128]
-            while len(outs) < 3 and FIRST[len(outs)] + COUNTS[len(outs)] <= end:
+            for t in range(begin, end):
+                k = sum(t >= first for first in FIRST) - 1
+                lanes = slice(128 * (t - begin), 128 * (t - begin) + 128)
+                for i in range(8):
+                    if far:
+                        v_ref[i, t] = v[8 * i:8 * i + 8, lanes]
+                    else:
+                        out_refs[k][i, t - FIRST[k]] = v[8 * i:8 * i + 8, lanes]
+            while far and len(outs) < 3 and FIRST[len(outs)] + COUNTS[len(outs)] <= end:
                 k = len(outs)
                 outs.append(start(v_ref.at[:, chunk_range(k)], out_refs[k], out_sem.at[k]))
         for copy in outs:
@@ -176,15 +183,13 @@
     return pl.pallas_call(
         kernel,
         in_specs=[SM, VM, HBM, HBM] + [ANY] * len(first),
-        out_specs=[HBM] * 3,
+        out_specs=[HBM if far else VM] * 3,
         out_shape=[jax.ShapeDtypeStruct((8, c, 8, 128), F32) for c in COUNTS],
         scratch_shapes=[
             pltpu.VMEM((n, 224, 28 * 128), BF),
-            pltpu.VMEM((8, HALF, 8, 128), F32),
             DMA((n, 2)),
-            DMA((3,)),
-        ],
-        compiler_params=params_of(),
+        ] + [pltpu.VMEM((8, HALF, 8, 128), F32), DMA((3,))] * far,
+        compiler_params=params_of(58 if far else 55),
         cost_estimate=pl.CostEstimate(flops=2 * 128 * 224 * HALF * 128, bytes_accessed=HALF * 128 * (448 + 256), transcendentals=0),
         name="q_far" if far else "q_own",
     )(where, lhs, delta, error, *first)
@@ -232,7 +237,7 @@
             DMA((3, 2)),
             DMA((3, 6)),
         ],
-        compiler_params=params_of(16),
+        compiler_params=params_of(60),
         cost_estimate=pl.CostEstimate(flops=10 ** 6, bytes_accessed=11 * 10 ** 6, transcendentals=0),
         name="blend",
     )(where, *terms, *arrived, f_own, f_near, gram.reshape(9, 8, 128))

time: 173 us -> 175 us (1.012)
  Pallas kernels: 45.4 us -> 48.9 us
    pallas_call x1, Pallas kernels: 2.79 us -> 5.94 us  [blend(): pl.pallas_call(kernel, in_specs=[SM] + [ANY] * 6 + [VM, VM, VM], out_spec...]
    unnamed x32 -> x40, local copies, waits for them, and re-layouts: 6.71 us -> 6.96 us
  transfers between devices with their start and end apart: 42 -> 42, of which waited for: 20 -> 19; matrix products, arithmetic and copies ran while one was open for 2% -> 1% of each run, Pallas kernels for 11% -> 11%
where the time goes in v4:
time: 175 us; the launch traced here: 174 us
  starting transfers between devices  57.8 us (33%)
  waiting for transfers between devices  55.1 us (31%)
  Pallas kernels  48.9 us (28%)
  local copies, waits for them, and re-layouts  7.8 us (4%)
  other arithmetic  2.79 us (2%)
  between operations  2.03 us (1%)
    ppermute x18, waiting for transfers between devices, low(): return lax.ppermute(x, axis, [(i, i ^ 1) for i in range(4)])  33.5 us
    ppermute x10, starting transfers between devices, swap(): return lax.ppermute(x, 'c', [(0, 1), (1, 0)])  23.2 us
    pallas_call x2, Pallas kernels, finish(): pl.pallas_call(kernel, in_specs=[SM, VM] + [ANY] * 6 + [HBM] * (4 + given...  15.6 us
    ppermute x6, waiting for transfers between devices, high(): return lax.ppermute(x, axis, [(i, 3 - i) for i in range(4)])  13 us
    pallas_call x2, Pallas kernels, q_half(): pl.pallas_call(kernel, in_specs=[SM, VM, HBM, HBM] + [ANY] * len(first),...  10.8 us
    ppermute x6, starting transfers between devices, turn(): return lax.ppermute(x, axis, [(i, (i + step) % 4) for i in range(4)])  10.2 us
    pallas_call x1, Pallas kernels, left_factor(): pl.pallas_call(p_kernel, in_specs=[SM, HBM, HBM, HBM], out_specs=VM, out_...  9.67 us
    ppermute x18, starting transfers between devices, low(): return lax.ppermute(x, axis, [(i, i ^ 1) for i in range(4)])  8.36 us
  transfers between devices with their start and end apart: 42, of which 19 were waited for; matrix products, arithmetic and copies ran while one was open for 1% of the time, Pallas kernels for 11%

profile of v4, /device:TPU:1, one launch (start us, length us, event | category | flops | bytes accessed | tf_op | source)
XLA Modules:
  0.0 174.5 jit_solution(613543858992801285)
XLA Ops:
  1.3 9.7 %left_factor.1 = f32[64,128]{1,0:T(8,128)} custom-call(s32[1]{0:T(128)S(6)} %copy.15.steps_ref, bf16[1,112,28672]{2,1,0:T(8,128)(2,1)} %rest_6_.3, bf16[1,112,28672]{2,1,0:T(8,128)(2,1)} %rest_7_.3, bf16[64,28672]{1,0:T(8,128)(2,1)} %bitcast.77), custom_call_target="tpu_custom_call" | custom-call | tf_op jit(solution)/shard_map/left_factor/pallas_call | solution.py:84
  11.0 3.4 %collective-permute-start.2 = (f32[64,128]{1,0:T(8,128)}, f32[64,128]{1,0:T(8,128)S(1)}, u32[]{:S(2)}, u32[]{:S(2)}) collective-permute-start(f32[64,128]{1,0:T(8,128)} %left_factor.1), channel_id=1, source_target_pairs={{0,24},{8,0},{16,8},{24,16},{1,25},{9,1},{17,9},{25,17},{2,26},{10... | collective-permute-start | bytes 98312 | tf_op jit(solution)/shard_map/ppermute | solution.py:33
  16.1 2.5 %collective-permute-done.1 = f32[64,128]{1,0:T(8,128)S(1)} collective-permute-done((f32[64,128]{1,0:T(8,128)}, f32[64,128]{1,0:T(8,128)S(1)}, u32[]{:S(2)}, u32[]{:S(2)}) %collective-permute-start.1) | collective-permute-done | bytes 32800 | tf_op jit(solution)/shard_map/ppermute | solution.py:33
  19.8 3.8 %collective-permute-start.5 = (f32[64,128]{1,0:T(8,128)S(1)}, f32[64,128]{1,0:T(8,128)S(1)}, u32[]{:S(2)}, u32[]{:S(2)}) collective-permute-start(f32[64,128]{1,0:T(8,128)S(1)} %add_add_fusion.1.a_ref), channel_id=1, source_target_pairs={{0,96},{32,0},{64,32},{96,64},{1,97},{33,1},{65,33},{97,65},{2,98}... | collective-permute-start | bytes 98312 | tf_op jit(solution)/shard_map/ppermute | solution.py:33
  25.5 2.1 %collective-permute-done.4.c_ref = f32[64,128]{1,0:T(8,128)S(1)} collective-permute-done((f32[64,128]{1,0:T(8,128)S(1)}, f32[64,128]{1,0:T(8,128)S(1)}, u32[]{:S(2)}, u32[]{:S(2)}) %collective-permute-start.4) | collective-permute-done | bytes 32800 | tf_op jit(solution)/shard_map/ppermute | solution.py:33
  28.8 5.2 %q_far.1 = (f32[8,37,8,128]{3,2,1,0:T(8,128)}, f32[8,37,8,128]{3,2,1,0:T(8,128)}, f32[8,38,8,128]{3,2,1,0:T(8,128)}) custom-call(s32[5]{0:T(128)} %stack.23.s_ref, bf16[128,224]{1,0:T(8,128)(2,1)} %copy-done.3, bf16[1,112,28672]{2,1,0:T(8,128)(2,1)} %rest_6_.3, bf16[1,112,28672]{2,1,0:T(8,128)(2,1)} %rest_7_.3), custom_call_target="tpu_custom_call" | custom-call | flops 822083584 | bytes 10092544 | tf_op jit(solution)/shard_map/q_far/pallas_call | solution.py:183
  34.1 3.5 %collective-permute-start.9 = (f32[8,38,8,128]{3,2,1,0:T(8,128)}, f32[8,38,8,128]{3,2,1,0:T(8,128)S(1)}, u32[]{:S(2)}, u32[]{:S(2)}) collective-permute-start(f32[8,38,8,128]{3,2,1,0:T(8,128)} %get-tuple-element.43), channel_id=1, source_target_pairs={{0,1},{1,0},{2,3},{3,2},{4,5},{5,4},{6,7},{7,6},{8,9},{9,8},{10,11... | collective-permute-start | bytes 3735560 | tf_op jit(solution)/shard_map/ppermute | solution.py:45
  38.2 5.6 %q_own.1 = (f32[8,37,8,128]{3,2,1,0:T(8,128)}, f32[8,37,8,128]{3,2,1,0:T(8,128)}, f32[8,38,8,128]{3,2,1,0:T(8,128)}) custom-call(s32[5]{0:T(128)} %stack.23.s_ref, bf16[128,224]{1,0:T(8,128)(2,1)} %copy-done.3, bf16[1,112,28672]{2,1,0:T(8,128)(2,1)} %rest_6_.3, bf16[1,112,28672]{2,1,0:T(8,128)(2,1)} %rest_7_.3), custom_call_target="tpu_custom_call" | custom-call | flops 822083584 | bytes 10092544 | tf_op jit(solution)/shard_map/q_own/pallas_call | solution.py:183
  47.9 5.9 %blend.1 = (f32[4,37,8,128]{3,2,1,0:T(8,128)}, f32[4,37,8,128]{3,2,1,0:T(8,128)}, f32[4,38,8,128]{3,2,1,0:T(8,128)}, f32[148,8,128]{2,1,0:T(8,128)}, f32[157,8,128]{2,1,0:T(8,128)}, /*index=5*/f32[152,8,128]{2,1,0:T(8,128)}) custom-call(s32[5]{0:T(128)} %stack.23.s_ref, f32[8,37,8,128]{3,2,1,0:T(8,128)} %get-tuple-element.38.refs_0_, ...), custom_call_target="tpu_custom_call" | custom-call | flops 1000000 | bytes 11000000 | tf_op jit(solution)/shard_map/blend/pallas_call | solution.py:229
  55.9 13.1 %collective-permute-done.11 = f32[148,8,128]{2,1,0:T(8,128)S(1)} collective-permute-done((f32[148,8,128]{2,1,0:T(8,128)}, f32[148,8,128]{2,1,0:T(8,128)S(1)}, u32[]{:S(2)}, u32[]{:S(2)}) %collective-permute-start.11) | collective-permute-done | bytes 606240 | tf_op jit(solution)/shard_map/ppermute | solution.py:37
  73.0 4.6 %collective-permute-done.12 = f32[2,37,8,128]{3,2,1,0:T(8,128)S(1)} collective-permute-done((f32[2,37,8,128]{3,2,1,0:T(8,128)S(1)}, f32[2,37,8,128]{3,2,1,0:T(8,128)S(1)}, u32[]{:S(2)}, u32[]{:S(2)}) %collective-permute-start.12) | collective-permute-done | bytes 303136 | tf_op jit(solution)/shard_map/ppermute | solution.py:37
  80.5 3.3 %collective-permute-done.13 = f32[1,37,8,128]{3,2,1,0:T(8,128)S(1)} collective-permute-done((f32[1,37,8,128]{3,2,1,0:T(8,128)S(1)}, f32[1,37,8,128]{3,2,1,0:T(8,128)S(1)}, u32[]{:S(2)}, u32[]{:S(2)}) %collective-permute-start.13) | collective-permute-done | bytes 151584 | tf_op jit(solution)/shard_map/ppermute | solution.py:37
  84.5 2.4 %collective-permute-start.19 = (f32[65,8,128]{2,1,0:T(8,128)S(1)}, f32[65,8,128]{2,1,0:T(8,128)S(1)}, u32[]{:S(2)}, u32[]{:S(2)}) collective-permute-start(f32[65,8,128]{2,1,0:T(8,128)S(1)} %pad_maximum_fusion.1), channel_id=1, source_target_pairs={{0,6},{2,4},{4,2},{6,0},{1,7},{3,5},{5,3},{7,1},{8,14},{10,12},{12... | collective-permute-start | bytes 798728 | tf_op jit(solution)/shard_map/ppermute | solution.py:41
  86.8 4.2 %collective-permute-done.19 = f32[65,8,128]{2,1,0:T(8,128)S(1)} collective-permute-done((f32[65,8,128]{2,1,0:T(8,128)S(1)}, f32[65,8,128]{2,1,0:T(8,128)S(1)}, u32[]{:S(2)}, u32[]{:S(2)}) %collective-permute-start.19) | collective-permute-done | bytes 266272 | tf_op jit(solution)/shard_map/ppermute | solution.py:41
  91.5 5.6 %collective-permute-start.20 = (f32[14,8,128]{2,1,0:T(8,128)S(1)}, f32[14,8,128]{2,1,0:T(8,128)S(1)}, u32[]{:S(2)}, u32[]{:S(2)}) collective-permute-start(f32[14,8,128]{2,1,0:T(8,128)S(1)} %get-tuple-element.75), channel_id=1, source_target_pairs={{0,120},{8,112},{16,104},{24,96},{32,88},{40,80},{48,72},{56,64},{... | collective-permute-start | bytes 172040 | tf_op jit(solution)/shard_map/ppermute | solution.py:459
  98.7 2.7 %collective-permute-done.22 = f32[14,8,128]{2,1,0:T(8,128)S(1)} collective-permute-done((f32[14,8,128]{2,1,0:T(8,128)S(1)}, f32[14,8,128]{2,1,0:T(8,128)S(1)}, u32[]{:S(2)}, u32[]{:S(2)}) %collective-permute-start.22) | collective-permute-done | bytes 57376 | tf_op jit(solution)/shard_map/ppermute | solution.py:41
  101.4 2.8 %collective-permute-start.23 = (f32[14,8,128]{2,1,0:T(8,128)S(1)}, f32[14,8,128]{2,1,0:T(8,128)S(1)}, u32[]{:S(2)}, u32[]{:S(2)}) collective-permute-start(f32[14,8,128]{2,1,0:T(8,128)S(1)} %add_add_fusion), channel_id=1, source_target_pairs={{0,24},{8,16},{16,8},{24,0},{1,25},{9,17},{17,9},{25,1},{2,26},{10... | collective-permute-start | bytes 172040 | tf_op jit(solution)/shard_map/ppermute | solution.py:41
  104.5 2.2 %collective-permute-start.25 = (f32[14,8,128]{2,1,0:T(8,128)S(1)}, f32[14,8,128]{2,1,0:T(8,128)S(1)}, u32[]{:S(2)}, u32[]{:S(2)}) collective-permute-start(f32[14,8,128]{2,1,0:T(8,128)S(1)} %add_add_fusion), channel_id=1, source_target_pairs={{0,120},{8,112},{16,104},{24,96},{32,88},{40,80},{48,72},{56,64},{... | collective-permute-start | bytes 172040 | tf_op jit(solution)/shard_map/ppermute | solution.py:459
  106.7 2.0 %collective-permute-done.24 = f32[14,8,128]{2,1,0:T(8,128)S(1)} collective-permute-done((f32[14,8,128]{2,1,0:T(8,128)S(1)}, f32[14,8,128]{2,1,0:T(8,128)S(1)}, u32[]{:S(2)}, u32[]{:S(2)}) %collective-permute-start.24) | collective-permute-done | bytes 57376 | tf_op jit(solution)/shard_map/ppermute | solution.py:41
  108.7 2.1 %collective-permute-done.25 = f32[14,8,128]{2,1,0:T(8,128)S(1)} collective-permute-done((f32[14,8,128]{2,1,0:T(8,128)S(1)}, f32[14,8,128]{2,1,0:T(8,128)S(1)}, u32[]{:S(2)}, u32[]{:S(2)}) %collective-permute-start.25) | collective-permute-done | bytes 57376 | tf_op jit(solution)/shard_map/ppermute | solution.py:459
  110.9 2.4 %collective-permute-start.26 = (f32[56,8,128]{2,1,0:T(8,128)S(1)}, f32[56,8,128]{2,1,0:T(8,128)S(1)}, u32[]{:S(2)}, u32[]{:S(2)}) collective-permute-start(f32[56,8,128]{2,1,0:T(8,128)S(1)} %maximum_select_fusion.7), channel_id=1, source_target_pairs={{0,6},{2,4},{4,2},{6,0},{1,7},{3,5},{5,3},{7,1},{8,14},{10,12},{12... | collective-permute-start | bytes 688136 | tf_op jit(solution)/shard_map/ppermute | solution.py:41
  113.2 4.1 %collective-permute-done.26 = f32[56,8,128]{2,1,0:T(8,128)S(1)} collective-permute-done((f32[56,8,128]{2,1,0:T(8,128)S(1)}, f32[56,8,128]{2,1,0:T(8,128)S(1)}, u32[]{:S(2)}, u32[]{:S(2)}) %collective-permute-start.26) | collective-permute-done | bytes 229408 | tf_op jit(solution)/shard_map/ppermute | solution.py:41
  117.7 3.8 %collective-permute-done.34 = f32[1,37,8,128]{3,2,1,0:T(8,128)S(1)} collective-permute-done((f32[1,37,8,128]{3,2,1,0:T(8,128)S(1)}, f32[1,37,8,128]{3,2,1,0:T(8,128)S(1)}, u32[]{:S(2)}, u32[]{:S(2)}) %collective-permute-start.34) | collective-permute-done | bytes 151584 | tf_op jit(solution)/shard_map/ppermute | solution.py:37
  121.7 1.8 %collective-permute-start.28 = (f32[2,38,8,128]{3,2,1,0:T(8,128)S(1)}, f32[2,38,8,128]{3,2,1,0:T(8,128)S(1)}, u32[]{:S(2)}, u32[]{:S(2)}) collective-permute-start(f32[2,38,8,128]{3,2,1,0:T(8,128)S(1)} %maximum_select_fusion.4), channel_id=1, source_target_pairs={{0,8},{8,0},{16,24},{24,16},{1,9},{9,1},{17,25},{25,17},{2,10},{10... | collective-permute-start | bytes 933896 | tf_op jit(solution)/shard_map/ppermute | solution.py:37
  123.6 3.6 %collective-permute-done.35 = f32[2,37,8,128]{3,2,1,0:T(8,128)S(1)} collective-permute-done((f32[2,37,8,128]{3,2,1,0:T(8,128)S(1)}, f32[2,37,8,128]{3,2,1,0:T(8,128)S(1)}, u32[]{:S(2)}, u32[]{:S(2)}) %collective-permute-start.35) | collective-permute-done | bytes 303136 | tf_op jit(solution)/shard_map/ppermute | solution.py:37
  127.4 12.5 %collective-permute-start.36 = (f32[4,37,8,128]{3,2,1,0:T(8,128)S(1)}, f32[4,37,8,128]{3,2,1,0:T(8,128)S(1)}, u32[]{:S(2)}, u32[]{:S(2)}) collective-permute-start(f32[4,37,8,128]{3,2,1,0:T(8,128)S(1)} %maximum_select_fusion.2.rest_2_), channel_id=1, source_target_pairs={{0,1},{1,0},{2,3},{3,2},{4,5},{5,4},{6,7},{7,6},{8,9},{9,8},{10,11... | collective-permute-start | bytes 1818632 | tf_op jit(solution)/shard_map/ppermute | solution.py:45
  140.6 6.3 %solve.1 = (bf16[112,192]{1,0:T(8,128)(2,1)S(1)}, f32[4,38,8,128]{3,2,1,0:T(8,128)S(1)}) custom-call(f32[72,128]{1,0:T(8,128)S(1)} %get-tuple-element.55.gram_ref, f32[112,64]{1,0:T(8,128)S(1)} %get-tuple-element.56.p_ref, f32[4,38,8,128]{3,2,1,0:T(8,128)S(1)} %maximum_select_fusion.block_ref.rest_4_), custom_call_target="tpu_custom_call" | custom-call | flops 10000000 | bytes 10000000 | tf_op jit(solution)/shard_map/solve/pallas_call | solution.py:299
  147.5 3.4 %collective-permute-start.39 = (f32[4,38,8,128]{3,2,1,0:T(8,128)S(1)}, f32[4,38,8,128]{3,2,1,0:T(8,128)S(1)}, u32[]{:S(2)}, u32[]{:S(2)}) collective-permute-start(f32[4,38,8,128]{3,2,1,0:T(8,128)S(1)} %get-tuple-element.60), channel_id=1, source_target_pairs={{0,1},{1,0},{2,3},{3,2},{4,5},{5,4},{6,7},{7,6},{8,9},{9,8},{10,11... | collective-permute-start | bytes 1867784 | tf_op jit(solution)/shard_map/ppermute | solution.py:45
  150.9 3.0 %collective-permute-done.40.rest_5_ = f32[4,38,8,128]{3,2,1,0:T(8,128)S(1)} collective-permute-done((f32[4,38,8,128]{3,2,1,0:T(8,128)S(1)}, f32[4,38,8,128]{3,2,1,0:T(8,128)S(1)}, u32[]{:S(2)}, u32[]{:S(2)}) %collective-permute-start.40) | collective-permute-done | bytes 622624 | tf_op jit(solution)/shard_map/ppermute | solution.py:37
  154.0 2.5 %collective-permute-start.41 = (f32[4,38,8,128]{3,2,1,0:T(8,128)S(1)}, f32[4,38,8,128]{3,2,1,0:T(8,128)S(1)}, u32[]{:S(2)}, u32[]{:S(2)}) collective-permute-start(f32[4,38,8,128]{3,2,1,0:T(8,128)S(1)} %collective-permute-done.40.rest_5_), channel_id=1, source_target_pairs={{0,1},{1,0},{2,3},{3,2},{4,5},{5,4},{6,7},{7,6},{8,9},{9,8},{10,11... | collective-permute-start | bytes 1867784 | tf_op jit(solution)/shard_map/ppermute | solution.py:45
  157.2 7.0 %finish_own.1 = (bf16[1,112,28672]{2,1,0:T(8,128)(2,1)}, f32[112,1792]{1,0:T(8,128)}, f32[112,1792]{1,0:T(8,128)}) custom-call(s32[5]{0:T(128)} %stack.23.s_ref, bf16[112,192]{1,0:T(8,128)(2,1)} %copy-done.4, f32[4,37,8,128]{3,2,1,0:T(8,128)} %copy-done.8, f32[4,37,8,128]{3,2,1,0:T(8,128)} %collective-permute-done.32.rest_1_, f32[4,37,8,128]{3,2,1,0:T(8,128)} %copy-done.7, ...), custom_call_target="tpu_custom_call" | custom-call | flops 616562688 | bytes 13303808 | tf_op jit(solution)/shard_map/finish_own/pallas_call | solution.py:375
  165.7 8.6 %finish_far.1 = (bf16[1,112,28672]{2,1,0:T(8,128)(2,1)}, f32[112,1792]{1,0:T(8,128)}, f32[112,1792]{1,0:T(8,128)}) custom-call(s32[5]{0:T(128)} %stack.23.s_ref, bf16[112,192]{1,0:T(8,128)(2,1)} %copy-done.4, f32[4,37,8,128]{3,2,1,0:T(8,128)} %copy-done.17, ...), custom_call_target="tpu_custom_call", output_to_operand_aliasing={{0}: (12, {}), {1}: (13, {}), {2}: (14, {})} | custom-call | flops 616562688 | bytes 13303808 | tf_op jit(solution)/shard_map/finish_far/pallas_call | solution.py:375
  (145 shorter events, 26.6 us)
Async XLA Ops:
  11.0 5.1 %collective-permute-start.2 = (f32[64,128]{1,0:T(8,128)}, f32[64,128]{1,0:T(8,128)S(1)}, u32[]{:S(2)}, u32[]{:S(2)}) collective-permute-start(f32[64,128]{1,0:T(8,128)} %left_factor.1), channel_id=1, source_target_pairs={{0,24},{8,0},{16,8},{24,16},{1,25},{9,1},{17,9},{25,17},{2,26},{10... | collective-permute-start | bytes 98312 | tf_op jit(solution)/shard_map/ppermute | solution.py:33
  19.8 5.7 %collective-permute-start.5 = (f32[64,128]{1,0:T(8,128)S(1)}, f32[64,128]{1,0:T(8,128)S(1)}, u32[]{:S(2)}, u32[]{:S(2)}) collective-permute-start(f32[64,128]{1,0:T(8,128)S(1)} %add_add_fusion.1.a_ref), channel_id=1, source_target_pairs={{0,96},{32,0},{64,32},{96,64},{1,97},{33,1},{65,33},{97,65},{2,98}... | collective-permute-start | bytes 98312 | tf_op jit(solution)/shard_map/ppermute | solution.py:33
  34.1 11.7 %collective-permute-start.9 = (f32[8,38,8,128]{3,2,1,0:T(8,128)}, f32[8,38,8,128]{3,2,1,0:T(8,128)S(1)}, u32[]{:S(2)}, u32[]{:S(2)}) collective-permute-start(f32[8,38,8,128]{3,2,1,0:T(8,128)} %get-tuple-element.43), channel_id=1, source_target_pairs={{0,1},{1,0},{2,3},{3,2},{4,5},{5,4},{6,7},{7,6},{8,9},{9,8},{10,11... | collective-permute-start | bytes 3735560 | tf_op jit(solution)/shard_map/ppermute | solution.py:45
  37.6 8.2 %collective-permute-start.7 = (f32[8,37,8,128]{3,2,1,0:T(8,128)}, f32[8,37,8,128]{3,2,1,0:T(8,128)S(1)}, u32[]{:S(2)}, u32[]{:S(2)}) collective-permute-start(f32[8,37,8,128]{3,2,1,0:T(8,128)} %get-tuple-element.41), channel_id=1, source_target_pairs={{0,1},{1,0},{2,3},{3,2},{4,5},{5,4},{6,7},{7,6},{8,9},{9,8},{10,11... | collective-permute-start | bytes 3637256 | tf_op jit(solution)/shard_map/ppermute | solution.py:45
  37.7 8.1 %collective-permute-start.8 = (f32[8,37,8,128]{3,2,1,0:T(8,128)}, f32[8,37,8,128]{3,2,1,0:T(8,128)S(1)}, u32[]{:S(2)}, u32[]{:S(2)}) collective-permute-start(f32[8,37,8,128]{3,2,1,0:T(8,128)} %get-tuple-element.42), channel_id=1, source_target_pairs={{0,1},{1,0},{2,3},{3,2},{4,5},{5,4},{6,7},{7,6},{8,9},{9,8},{10,11... | collective-permute-start | bytes 3637256 | tf_op jit(solution)/shard_map/ppermute | solution.py:45
  38.1 5.7 %collective-permute-start.6 = (f32[72,128]{1,0:T(8,128)S(1)}, f32[72,128]{1,0:T(8,128)S(1)}, u32[]{:S(2)}, u32[]{:S(2)}) collective-permute-start(f32[72,128]{1,0:T(8,128)S(1)} %get-tuple-element.35.a_ref.refs_0_), channel_id=1, source_target_pairs={{0,1},{1,0},{2,3},{3,2},{4,5},{5,4},{6,7},{7,6},{8,9},{9,8},{10,11... | collective-permute-start | bytes 110600 | tf_op jit(solution)/shard_map/ppermute | solution.py:45
  53.9 15.1 %collective-permute-start.11 = (f32[148,8,128]{2,1,0:T(8,128)}, f32[148,8,128]{2,1,0:T(8,128)S(1)}, u32[]{:S(2)}, u32[]{:S(2)}) collective-permute-start(f32[148,8,128]{2,1,0:T(8,128)} %get-tuple-element.49), channel_id=1, source_target_pairs={{0,8},{8,0},{16,24},{24,16},{1,9},{9,1},{17,25},{25,17},{2,10},{10... | collective-permute-start | bytes 1818632 | tf_op jit(solution)/shard_map/ppermute | solution.py:37
  54.3 17.2 %collective-permute-start.16 = (f32[152,8,128]{2,1,0:T(8,128)}, f32[152,8,128]{2,1,0:T(8,128)S(1)}, u32[]{:S(2)}, u32[]{:S(2)}) collective-permute-start(f32[152,8,128]{2,1,0:T(8,128)} %get-tuple-element.54), channel_id=1, source_target_pairs={{0,32},{32,0},{64,96},{96,64},{1,33},{33,1},{65,97},{97,65},{2,34}... | collective-permute-start | bytes 1867784 | tf_op jit(solution)/shard_map/ppermute | solution.py:37
  54.6 17.5 %collective-permute-start.10 = (f32[157,8,128]{2,1,0:T(8,128)}, f32[157,8,128]{2,1,0:T(8,128)S(1)}, u32[]{:S(2)}, u32[]{:S(2)}) collective-permute-start(f32[157,8,128]{2,1,0:T(8,128)} %get-tuple-element.46), channel_id=1, source_target_pairs={{0,2},{2,0},{4,6},{6,4},{1,3},{3,1},{5,7},{7,5},{8,10},{10,8},{12,... | collective-permute-start | bytes 1929224 | tf_op jit(solution)/shard_map/ppermute | solution.py:37
  70.1 7.5 %collective-permute-start.12 = (f32[2,37,8,128]{3,2,1,0:T(8,128)S(1)}, f32[2,37,8,128]{3,2,1,0:T(8,128)S(1)}, u32[]{:S(2)}, u32[]{:S(2)}) collective-permute-start(f32[2,37,8,128]{3,2,1,0:T(8,128)S(1)} %get-tuple-element.70), channel_id=1, source_target_pairs={{0,2},{2,0},{4,6},{6,4},{1,3},{3,1},{5,7},{7,5},{8,10},{10,8},{12,... | collective-permute-start | bytes 909320 | tf_op jit(solution)/shard_map/ppermute | solution.py:37
  71.6 7.4 %collective-permute-start.17 = (f32[2,38,8,128]{3,2,1,0:T(8,128)S(1)}, f32[2,38,8,128]{3,2,1,0:T(8,128)S(1)}, u32[]{:S(2)}, u32[]{:S(2)}) collective-permute-start(f32[2,38,8,128]{3,2,1,0:T(8,128)S(1)} %get-tuple-element.68), channel_id=1, source_target_pairs={{0,8},{8,0},{16,24},{24,16},{1,9},{9,1},{17,25},{25,17},{2,10},{10... | collective-permute-start | bytes 933896 | tf_op jit(solution)/shard_map/ppermute | solution.py:37
  72.7 7.2 %collective-permute-start.14 = (f32[2,37,8,128]{3,2,1,0:T(8,128)S(1)}, f32[2,37,8,128]{3,2,1,0:T(8,128)S(1)}, u32[]{:S(2)}, u32[]{:S(2)}) collective-permute-start(f32[2,37,8,128]{3,2,1,0:T(8,128)S(1)} %get-tuple-element.72), channel_id=1, source_target_pairs={{0,32},{32,0},{64,96},{96,64},{1,33},{33,1},{65,97},{97,65},{2,34}... | collective-permute-start | bytes 909320 | tf_op jit(solution)/shard_map/ppermute | solution.py:37
  77.7 6.1 %collective-permute-start.13 = (f32[1,37,8,128]{3,2,1,0:T(8,128)S(1)}, f32[1,37,8,128]{3,2,1,0:T(8,128)S(1)}, u32[]{:S(2)}, u32[]{:S(2)}) collective-permute-start(f32[1,37,8,128]{3,2,1,0:T(8,128)S(1)} %multiply_add_fusion.2), channel_id=1, source_target_pairs={{0,32},{32,0},{64,96},{96,64},{1,33},{33,1},{65,97},{97,65},{2,34}... | collective-permute-start | bytes 454664 | tf_op jit(solution)/shard_map/ppermute | solution.py:37
  79.0 4.8 %collective-permute-start.18 = (f32[1,38,8,128]{3,2,1,0:T(8,128)S(1)}, f32[1,38,8,128]{3,2,1,0:T(8,128)S(1)}, u32[]{:S(2)}, u32[]{:S(2)}) collective-permute-start(f32[1,38,8,128]{3,2,1,0:T(8,128)S(1)} %dynamic-slice_add_fusion.4), channel_id=1, source_target_pairs={{0,2},{2,0},{4,6},{6,4},{1,3},{3,1},{5,7},{7,5},{8,10},{10,8},{12,... | collective-permute-start | bytes 466952 | tf_op jit(solution)/shard_map/ppermute | solution.py:37
  84.5 6.6 %collective-permute-start.19 = (f32[65,8,128]{2,1,0:T(8,128)S(1)}, f32[65,8,128]{2,1,0:T(8,128)S(1)}, u32[]{:S(2)}, u32[]{:S(2)}) collective-permute-start(f32[65,8,128]{2,1,0:T(8,128)S(1)} %pad_maximum_fusion.1), channel_id=1, source_target_pairs={{0,6},{2,4},{4,2},{6,0},{1,7},{3,5},{5,3},{7,1},{8,14},{10,12},{12... | collective-permute-start | bytes 798728 | tf_op jit(solution)/shard_map/ppermute | solution.py:41
  91.5 7.2 %collective-permute-start.20 = (f32[14,8,128]{2,1,0:T(8,128)S(1)}, f32[14,8,128]{2,1,0:T(8,128)S(1)}, u32[]{:S(2)}, u32[]{:S(2)}) collective-permute-start(f32[14,8,128]{2,1,0:T(8,128)S(1)} %get-tuple-element.75), channel_id=1, source_target_pairs={{0,120},{8,112},{16,104},{24,96},{32,88},{40,80},{48,72},{56,64},{... | collective-permute-start | bytes 172040 | tf_op jit(solution)/shard_map/ppermute | solution.py:459
  101.4 5.3 %collective-permute-start.23 = (f32[14,8,128]{2,1,0:T(8,128)S(1)}, f32[14,8,128]{2,1,0:T(8,128)S(1)}, u32[]{:S(2)}, u32[]{:S(2)}) collective-permute-start(f32[14,8,128]{2,1,0:T(8,128)S(1)} %add_add_fusion), channel_id=1, source_target_pairs={{0,24},{8,16},{16,8},{24,0},{1,25},{9,17},{17,9},{25,1},{2,26},{10... | collective-permute-start | bytes 172040 | tf_op jit(solution)/shard_map/ppermute | solution.py:41
  104.5 6.3 %collective-permute-start.25 = (f32[14,8,128]{2,1,0:T(8,128)S(1)}, f32[14,8,128]{2,1,0:T(8,128)S(1)}, u32[]{:S(2)}, u32[]{:S(2)}) collective-permute-start(f32[14,8,128]{2,1,0:T(8,128)S(1)} %add_add_fusion), channel_id=1, source_target_pairs={{0,120},{8,112},{16,104},{24,96},{32,88},{40,80},{48,72},{56,64},{... | collective-permute-start | bytes 172040 | tf_op jit(solution)/shard_map/ppermute | solution.py:459
  110.9 6.5 %collective-permute-start.26 = (f32[56,8,128]{2,1,0:T(8,128)S(1)}, f32[56,8,128]{2,1,0:T(8,128)S(1)}, u32[]{:S(2)}, u32[]{:S(2)}) collective-permute-start(f32[56,8,128]{2,1,0:T(8,128)S(1)} %maximum_select_fusion.7), channel_id=1, source_target_pairs={{0,6},{2,4},{4,2},{6,0},{1,7},{3,5},{5,3},{7,1},{8,14},{10,12},{12... | collective-permute-start | bytes 688136 | tf_op jit(solution)/shard_map/ppermute | solution.py:41
  117.6 5.9 %collective-permute-start.29 = (f32[1,37,8,128]{3,2,1,0:T(8,128)S(1)}, f32[1,37,8,128]{3,2,1,0:T(8,128)S(1)}, u32[]{:S(2)}, u32[]{:S(2)}) collective-permute-start(f32[1,37,8,128]{3,2,1,0:T(8,128)S(1)} %get-tuple-element.74), channel_id=1, source_target_pairs={{0,32},{32,0},{64,96},{96,64},{1,33},{33,1},{65,97},{97,65},{2,34}... | collective-permute-start | bytes 454664 | tf_op jit(solution)/shard_map/ppermute | solution.py:37
  121.5 5.7 %collective-permute-start.35 = (f32[2,37,8,128]{3,2,1,0:T(8,128)S(1)}, f32[2,37,8,128]{3,2,1,0:T(8,128)S(1)}, u32[]{:S(2)}, u32[]{:S(2)}) collective-permute-start(f32[2,37,8,128]{3,2,1,0:T(8,128)S(1)} %maximum_select_fusion.6), channel_id=1, source_target_pairs={{0,32},{32,0},{64,96},{96,64},{1,33},{33,1},{65,97},{97,65},{2,34}... | collective-permute-start | bytes 909320 | tf_op jit(solution)/shard_map/ppermute | solution.py:37
  121.7 18.3 %collective-permute-start.28 = (f32[2,38,8,128]{3,2,1,0:T(8,128)S(1)}, f32[2,38,8,128]{3,2,1,0:T(8,128)S(1)}, u32[]{:S(2)}, u32[]{:S(2)}) collective-permute-start(f32[2,38,8,128]{3,2,1,0:T(8,128)S(1)} %maximum_select_fusion.4), channel_id=1, source_target_pairs={{0,8},{8,0},{16,24},{24,16},{1,9},{9,1},{17,25},{25,17},{2,10},{10... | collective-permute-start | bytes 933896 | tf_op jit(solution)/shard_map/ppermute | solution.py:37
  123.5 16.6 %collective-permute-start.30 = (f32[2,37,8,128]{3,2,1,0:T(8,128)S(1)}, f32[2,37,8,128]{3,2,1,0:T(8,128)S(1)}, u32[]{:S(2)}, u32[]{:S(2)}) collective-permute-start(f32[2,37,8,128]{3,2,1,0:T(8,128)S(1)} %maximum_select_fusion.5), channel_id=1, source_target_pairs={{0,2},{2,0},{4,6},{6,4},{1,3},{3,1},{5,7},{7,5},{8,10},{10,8},{12,... | collective-permute-start | bytes 909320 | tf_op jit(solution)/shard_map/ppermute | solution.py:37
  127.3 29.2 %collective-permute-start.37 = (f32[4,37,8,128]{3,2,1,0:T(8,128)S(1)}, f32[4,37,8,128]{3,2,1,0:T(8,128)}, u32[]{:S(2)}, u32[]{:S(2)}) collective-permute-start(f32[4,37,8,128]{3,2,1,0:T(8,128)S(1)} %maximum_select_fusion.2.rest_2_), channel_id=1, source_target_pairs={{0,2},{2,0},{4,6},{6,4},{1,3},{3,1},{5,7},{7,5},{8,10},{10,8},{12,... | collective-permute-start | bytes 1818632 | tf_op jit(solution)/shard_map/ppermute | solution.py:37
  127.4 29.2 %collective-permute-start.36 = (f32[4,37,8,128]{3,2,1,0:T(8,128)S(1)}, f32[4,37,8,128]{3,2,1,0:T(8,128)S(1)}, u32[]{:S(2)}, u32[]{:S(2)}) collective-permute-start(f32[4,37,8,128]{3,2,1,0:T(8,128)S(1)} %maximum_select_fusion.2.rest_2_), channel_id=1, source_target_pairs={{0,1},{1,0},{2,3},{3,2},{4,5},{5,4},{6,7},{7,6},{8,9},{9,8},{10,11... | collective-permute-start | bytes 1818632 | tf_op jit(solution)/shard_map/ppermute | solution.py:45
  140.0 14.0 %collective-permute-start.40 = (f32[4,38,8,128]{3,2,1,0:T(8,128)S(1)}, f32[4,38,8,128]{3,2,1,0:T(8,128)S(1)}, u32[]{:S(2)}, u32[]{:S(2)}) collective-permute-start(f32[4,38,8,128]{3,2,1,0:T(8,128)S(1)} %maximum_select_fusion.block_ref.rest_4_), channel_id=1, source_target_pairs={{0,32},{32,0},{64,96},{96,64},{1,33},{33,1},{65,97},{97,65},{2,34}... | collective-permute-start | bytes 1867784 | tf_op jit(solution)/shard_map/ppermute | solution.py:37
  140.2 16.9 %collective-permute-start.32 = (f32[4,37,8,128]{3,2,1,0:T(8,128)S(1)}, f32[4,37,8,128]{3,2,1,0:T(8,128)}, u32[]{:S(2)}, u32[]{:S(2)}) collective-permute-start(f32[4,37,8,128]{3,2,1,0:T(8,128)S(1)} %maximum_select_fusion.1.rest_0_), channel_id=1, source_target_pairs={{0,8},{8,0},{16,24},{24,16},{1,9},{9,1},{17,25},{25,17},{2,10},{10... | collective-permute-start | bytes 1818632 | tf_op jit(solution)/shard_map/ppermute | solution.py:37
  147.5 16.7 %collective-permute-start.39 = (f32[4,38,8,128]{3,2,1,0:T(8,128)S(1)}, f32[4,38,8,128]{3,2,1,0:T(8,128)S(1)}, u32[]{:S(2)}, u32[]{:S(2)}) collective-permute-start(f32[4,38,8,128]{3,2,1,0:T(8,128)S(1)} %get-tuple-element.60), channel_id=1, source_target_pairs={{0,1},{1,0},{2,3},{3,2},{4,5},{5,4},{6,7},{7,6},{8,9},{9,8},{10,11... | collective-permute-start | bytes 1867784 | tf_op jit(solution)/shard_map/ppermute | solution.py:45
  154.0 10.3 %collective-permute-start.41 = (f32[4,38,8,128]{3,2,1,0:T(8,128)S(1)}, f32[4,38,8,128]{3,2,1,0:T(8,128)S(1)}, u32[]{:S(2)}, u32[]{:S(2)}) collective-permute-start(f32[4,38,8,128]{3,2,1,0:T(8,128)S(1)} %collective-permute-done.40.rest_5_), channel_id=1, source_target_pairs={{0,1},{1,0},{2,3},{3,2},{4,5},{5,4},{6,7},{7,6},{8,9},{9,8},{10,11... | collective-permute-start | bytes 1867784 | tf_op jit(solution)/shard_map/ppermute | solution.py:45
  156.5 7.7 %collective-permute-start.31 = (f32[4,37,8,128]{3,2,1,0:T(8,128)S(1)}, f32[4,37,8,128]{3,2,1,0:T(8,128)S(1)}, u32[]{:S(2)}, u32[]{:S(2)}) collective-permute-start(f32[4,37,8,128]{3,2,1,0:T(8,128)S(1)} %maximum_select_fusion.1.rest_0_), channel_id=1, source_target_pairs={{0,1},{1,0},{2,3},{3,2},{4,5},{5,4},{6,7},{7,6},{8,9},{9,8},{10,11... | collective-permute-start | bytes 1818632 | tf_op jit(solution)/shard_map/ppermute | solution.py:45
  156.6 7.6 %collective-permute-start.38 = (f32[4,37,8,128]{3,2,1,0:T(8,128)}, f32[4,37,8,128]{3,2,1,0:T(8,128)S(1)}, u32[]{:S(2)}, u32[]{:S(2)}) collective-permute-start(f32[4,37,8,128]{3,2,1,0:T(8,128)} %collective-permute-done.37.rest_3_), channel_id=1, source_target_pairs={{0,1},{1,0},{2,3},{3,2},{4,5},{5,4},{6,7},{7,6},{8,9},{9,8},{10,11... | collective-permute-start | bytes 1818632 | tf_op jit(solution)/shard_map/ppermute | solution.py:45
  157.1 7.2 %collective-permute-start.33 = (f32[4,37,8,128]{3,2,1,0:T(8,128)}, f32[4,37,8,128]{3,2,1,0:T(8,128)}, u32[]{:S(2)}, u32[]{:S(2)}) collective-permute-start(f32[4,37,8,128]{3,2,1,0:T(8,128)} %collective-permute-done.32.rest_1_), channel_id=1, source_target_pairs={{0,1},{1,0},{2,3},{3,2},{4,5},{5,4},{6,7},{7,6},{8,9},{9,8},{10,11... | collective-permute-start | bytes 1818632 | tf_op jit(solution)/shard_map/ppermute | solution.py:45
  (30 other events, 139.1 us)

commit v5 on v3

--- a/solution.py
+++ b/solution.py
@@ -14,8 +14,8 @@
 ROUTES = (("x", "y", "z"), ("y", "z", "x"), ("z", "x", "y"))
 
 HALF = 112
-COUNTS = (37, 37, 38)
-FIRST = (0, 37, 74)
+COUNTS = (38, 36, 38)
+FIRST = (0, 38, 74)
 BF = jnp.bfloat16
 F32 = jnp.float32
 HBM = pl.BlockSpec(memory_space=pltpu.HBM)

time: 173 us -> 176 us (1.017)
  waiting for transfers between devices: 54.4 us -> 57.4 us
  local copies, waits for them, and re-layouts: 7.55 us -> 9.96 us
  starting transfers between devices: 59 us -> 56.7 us
    ppermute x10, starting transfers between devices: 23.2 us -> 20.8 us  [swap(): return lax.ppermute(x, 'c', [(0, 1), (1, 0)])]
    ppermute x18, waiting for transfers between devices: 33 us -> 35 us  [low(): return lax.ppermute(x, axis, [(i, i ^ 1) for i in range(4)])]
  transfers between devices with their start and end apart: 42 -> 42, of which waited for: 20 -> 22; matrix products, arithmetic and copies ran while one was open for 2% -> 2% of each run, Pallas kernels for 11% -> 11%
where the time goes in v5:
time: 176 us; the launch traced here: 175 us
  waiting for transfers between devices  57.4 us (33%)
  starting transfers between devices  56.7 us (32%)
  Pallas kernels  46.2 us (26%)
  local copies, waits for them, and re-layouts  9.96 us (6%)
  other arithmetic  2.8 us (2%)
  between operations  1.97 us (1%)
    ppermute x18, waiting for transfers between devices, low(): return lax.ppermute(x, axis, [(i, i ^ 1) for i in range(4)])  35 us
    ppermute x10, starting transfers between devices, swap(): return lax.ppermute(x, 'c', [(0, 1), (1, 0)])  20.8 us
    pallas_call x2, Pallas kernels, finish(): pl.pallas_call(kernel, in_specs=[SM, VM] + [ANY] * 6 + [HBM] * (4 + given...  15.7 us
    ppermute x6, waiting for transfers between devices, high(): return lax.ppermute(x, axis, [(i, 3 - i) for i in range(4)])  13.1 us
    pallas_call x2, Pallas kernels, q_half(): pl.pallas_call(kernel, in_specs=[SM, VM, HBM, HBM] + [ANY] * len(first),...  10.5 us
    ppermute x6, starting transfers between devices, turn(): return lax.ppermute(x, axis, [(i, (i + step) % 4) for i in range(4)])  10.2 us
    ppermute x18, starting transfers between devices, low(): return lax.ppermute(x, axis, [(i, i ^ 1) for i in range(4)])  9.85 us
    pallas_call x1, Pallas kernels, left_factor(): pl.pallas_call(p_kernel, in_specs=[SM, HBM, HBM, HBM], out_specs=VM, out_...  9.67 us
  transfers between devices with their start and end apart: 42, of which 22 were waited for; matrix products, arithmetic and copies ran while one was open for 2% of the time, Pallas kernels for 11%

profile of v5, /device:TPU:1, one launch (start us, length us, event | category | flops | bytes accessed | tf_op | source)
XLA Modules:
  0.0 175.1 jit_solution(18075700940443230406)
XLA Ops:
  1.3 9.7 %left_factor.1 = f32[64,128]{1,0:T(8,128)} custom-call(s32[1]{0:T(128)S(6)} %copy.15.steps_ref, bf16[1,112,28672]{2,1,0:T(8,128)(2,1)} %rest_6_.3, bf16[1,112,28672]{2,1,0:T(8,128)(2,1)} %rest_7_.3, bf16[64,28672]{1,0:T(8,128)(2,1)} %bitcast.77), custom_call_target="tpu_custom_call" | custom-call | tf_op jit(solution)/shard_map/left_factor/pallas_call | solution.py:84
  11.0 3.4 %collective-permute-start.2 = (f32[64,128]{1,0:T(8,128)}, f32[64,128]{1,0:T(8,128)S(1)}, u32[]{:S(2)}, u32[]{:S(2)}) collective-permute-start(f32[64,128]{1,0:T(8,128)} %left_factor.1), channel_id=1, source_target_pairs={{0,24},{8,0},{16,8},{24,16},{1,25},{9,1},{17,9},{25,17},{2,26},{10... | collective-permute-start | bytes 98312 | tf_op jit(solution)/shard_map/ppermute | solution.py:33
  14.3 1.7 collective-permute-start
  16.1 2.5 %collective-permute-done.1 = f32[64,128]{1,0:T(8,128)S(1)} collective-permute-done((f32[64,128]{1,0:T(8,128)}, f32[64,128]{1,0:T(8,128)S(1)}, u32[]{:S(2)}, u32[]{:S(2)}) %collective-permute-start.1) | collective-permute-done | bytes 32800 | tf_op jit(solution)/shard_map/ppermute | solution.py:33
  19.8 3.8 %collective-permute-start.5 = (f32[64,128]{1,0:T(8,128)S(1)}, f32[64,128]{1,0:T(8,128)S(1)}, u32[]{:S(2)}, u32[]{:S(2)}) collective-permute-start(f32[64,128]{1,0:T(8,128)S(1)} %add_add_fusion.1.a_ref), channel_id=1, source_target_pairs={{0,96},{32,0},{64,32},{96,64},{1,97},{33,1},{65,33},{97,65},{2,98}... | collective-permute-start | bytes 98312 | tf_op jit(solution)/shard_map/ppermute | solution.py:33
  25.5 2.1 %collective-permute-done.4.c_ref = f32[64,128]{1,0:T(8,128)S(1)} collective-permute-done((f32[64,128]{1,0:T(8,128)S(1)}, f32[64,128]{1,0:T(8,128)S(1)}, u32[]{:S(2)}, u32[]{:S(2)}) %collective-permute-start.4) | collective-permute-done | bytes 32800 | tf_op jit(solution)/shard_map/ppermute | solution.py:33
  28.8 5.2 %q_far.1 = (f32[8,38,8,128]{3,2,1,0:T(8,128)}, f32[8,36,8,128]{3,2,1,0:T(8,128)}, f32[8,38,8,128]{3,2,1,0:T(8,128)}) custom-call(s32[5]{0:T(128)} %stack.23.s_ref, bf16[128,224]{1,0:T(8,128)(2,1)} %copy-done.4, bf16[1,112,28672]{2,1,0:T(8,128)(2,1)} %rest_6_.3, bf16[1,112,28672]{2,1,0:T(8,128)(2,1)} %rest_7_.3), custom_call_target="tpu_custom_call" | custom-call | flops 822083584 | bytes 10092544 | tf_op jit(solution)/shard_map/q_far/pallas_call | solution.py:176
  34.1 3.5 %collective-permute-start.7 = (f32[8,38,8,128]{3,2,1,0:T(8,128)}, f32[8,38,8,128]{3,2,1,0:T(8,128)S(1)}, u32[]{:S(2)}, u32[]{:S(2)}) collective-permute-start(f32[8,38,8,128]{3,2,1,0:T(8,128)} %get-tuple-element.41), channel_id=1, source_target_pairs={{0,1},{1,0},{2,3},{3,2},{4,5},{5,4},{6,7},{7,6},{8,9},{9,8},{10,11... | collective-permute-start | bytes 3735560 | tf_op jit(solution)/shard_map/ppermute | solution.py:45
  38.2 5.2 %q_own.1 = (f32[8,38,8,128]{3,2,1,0:T(8,128)}, f32[8,36,8,128]{3,2,1,0:T(8,128)}, f32[8,38,8,128]{3,2,1,0:T(8,128)}) custom-call(s32[5]{0:T(128)} %stack.23.s_ref, bf16[128,224]{1,0:T(8,128)(2,1)} %copy-done.4, bf16[1,112,28672]{2,1,0:T(8,128)(2,1)} %rest_6_.3, bf16[1,112,28672]{2,1,0:T(8,128)(2,1)} %rest_7_.3), custom_call_target="tpu_custom_call" | custom-call | flops 822083584 | bytes 10092544 | tf_op jit(solution)/shard_map/q_own/pallas_call | solution.py:176
  47.7 3.6 %blend.1 = (f32[4,38,8,128]{3,2,1,0:T(8,128)S(1)}, f32[4,36,8,128]{3,2,1,0:T(8,128)S(1)}, f32[4,38,8,128]{3,2,1,0:T(8,128)S(1)}, f32[152,8,128]{2,1,0:T(8,128)S(...) custom-call(s32[5]{0:T(128)S(1)} %copy-done.6, f32[8,38,8,128]{3,2,1,0:T(8,128)S(1)} %copy-done.1, ...), custom_call_target="tpu_custom_call" | custom-call | flops 1000000 | bytes 11000000 | tf_op jit(solution)/shard_map/blend/pallas_call | solution.py:224
  51.3 1.4 collective-permute-start.10
  53.4 13.7 %collective-permute-done.10 = f32[153,8,128]{2,1,0:T(8,128)} collective-permute-done((f32[153,8,128]{2,1,0:T(8,128)}, f32[153,8,128]{2,1,0:T(8,128)}, u32[]{:S(2)}, u32[]{:S(2)}) %collective-permute-start.10) | collective-permute-done | bytes 626720 | tf_op jit(solution)/shard_map/ppermute | solution.py:37
  72.6 4.0 %collective-permute-done.14 = f32[2,36,8,128]{3,2,1,0:T(8,128)S(1)} collective-permute-done((f32[2,36,8,128]{3,2,1,0:T(8,128)S(1)}, f32[2,36,8,128]{3,2,1,0:T(8,128)S(1)}, u32[]{:S(2)}, u32[]{:S(2)}) %collective-permute-start.14) | collective-permute-done | bytes 294944 | tf_op jit(solution)/shard_map/ppermute | solution.py:37
  83.8 2.2 %collective-permute-start.19 = (f32[65,8,128]{2,1,0:T(8,128)S(1)}, f32[65,8,128]{2,1,0:T(8,128)S(1)}, u32[]{:S(2)}, u32[]{:S(2)}) collective-permute-start(f32[65,8,128]{2,1,0:T(8,128)S(1)} %pad_maximum_fusion.1), channel_id=1, source_target_pairs={{0,6},{2,4},{4,2},{6,0},{1,7},{3,5},{5,3},{7,1},{8,14},{10,12},{12... | collective-permute-start | bytes 798728 | tf_op jit(solution)/shard_map/ppermute | solution.py:41
  86.1 4.3 %collective-permute-done.19 = f32[65,8,128]{2,1,0:T(8,128)S(1)} collective-permute-done((f32[65,8,128]{2,1,0:T(8,128)S(1)}, f32[65,8,128]{2,1,0:T(8,128)S(1)}, u32[]{:S(2)}, u32[]{:S(2)}) %collective-permute-start.19) | collective-permute-done | bytes 266272 | tf_op jit(solution)/shard_map/ppermute | solution.py:41
  90.9 5.9 %collective-permute-start.20 = (f32[14,8,128]{2,1,0:T(8,128)S(1)}, f32[14,8,128]{2,1,0:T(8,128)S(1)}, u32[]{:S(2)}, u32[]{:S(2)}) collective-permute-start(f32[14,8,128]{2,1,0:T(8,128)S(1)} %get-tuple-element.75), channel_id=1, source_target_pairs={{0,120},{8,112},{16,104},{24,96},{32,88},{40,80},{48,72},{56,64},{... | collective-permute-start | bytes 172040 | tf_op jit(solution)/shard_map/ppermute | solution.py:454
  98.4 2.7 %collective-permute-done.22 = f32[14,8,128]{2,1,0:T(8,128)S(1)} collective-permute-done((f32[14,8,128]{2,1,0:T(8,128)S(1)}, f32[14,8,128]{2,1,0:T(8,128)S(1)}, u32[]{:S(2)}, u32[]{:S(2)}) %collective-permute-start.22) | collective-permute-done | bytes 57376 | tf_op jit(solution)/shard_map/ppermute | solution.py:41
  101.1 2.8 %collective-permute-start.23 = (f32[14,8,128]{2,1,0:T(8,128)S(1)}, f32[14,8,128]{2,1,0:T(8,128)S(1)}, u32[]{:S(2)}, u32[]{:S(2)}) collective-permute-start(f32[14,8,128]{2,1,0:T(8,128)S(1)} %add_add_fusion), channel_id=1, source_target_pairs={{0,24},{8,16},{16,8},{24,0},{1,25},{9,17},{17,9},{25,1},{2,26},{10... | collective-permute-start | bytes 172040 | tf_op jit(solution)/shard_map/ppermute | solution.py:41
  104.2 2.2 %collective-permute-start.25 = (f32[14,8,128]{2,1,0:T(8,128)S(1)}, f32[14,8,128]{2,1,0:T(8,128)S(1)}, u32[]{:S(2)}, u32[]{:S(2)}) collective-permute-start(f32[14,8,128]{2,1,0:T(8,128)S(1)} %add_add_fusion), channel_id=1, source_target_pairs={{0,120},{8,112},{16,104},{24,96},{32,88},{40,80},{48,72},{56,64},{... | collective-permute-start | bytes 172040 | tf_op jit(solution)/shard_map/ppermute | solution.py:454
  106.4 1.7 collective-permute-done.24
  108.1 2.4 %collective-permute-done.25 = f32[14,8,128]{2,1,0:T(8,128)S(1)} collective-permute-done((f32[14,8,128]{2,1,0:T(8,128)S(1)}, f32[14,8,128]{2,1,0:T(8,128)S(1)}, u32[]{:S(2)}, u32[]{:S(2)}) %collective-permute-start.25) | collective-permute-done | bytes 57376 | tf_op jit(solution)/shard_map/ppermute | solution.py:454
  110.6 2.0 %collective-permute-start.26 = (f32[56,8,128]{2,1,0:T(8,128)S(1)}, f32[56,8,128]{2,1,0:T(8,128)S(1)}, u32[]{:S(2)}, u32[]{:S(2)}) collective-permute-start(f32[56,8,128]{2,1,0:T(8,128)S(1)} %maximum_select_fusion.7), channel_id=1, source_target_pairs={{0,6},{2,4},{4,2},{6,0},{1,7},{3,5},{5,3},{7,1},{8,14},{10,12},{12... | collective-permute-start | bytes 688136 | tf_op jit(solution)/shard_map/ppermute | solution.py:41
  112.5 4.4 %collective-permute-done.26 = f32[56,8,128]{2,1,0:T(8,128)S(1)} collective-permute-done((f32[56,8,128]{2,1,0:T(8,128)S(1)}, f32[56,8,128]{2,1,0:T(8,128)S(1)}, u32[]{:S(2)}, u32[]{:S(2)}) %collective-permute-start.26) | collective-permute-done | bytes 229408 | tf_op jit(solution)/shard_map/ppermute | solution.py:41
  117.2 4.0 %collective-permute-done.29 = f32[1,38,8,128]{3,2,1,0:T(8,128)S(1)} collective-permute-done((f32[1,38,8,128]{3,2,1,0:T(8,128)S(1)}, f32[1,38,8,128]{3,2,1,0:T(8,128)S(1)}, u32[]{:S(2)}, u32[]{:S(2)}) %collective-permute-start.29) | collective-permute-done | bytes 155680 | tf_op jit(solution)/shard_map/ppermute | solution.py:37
  121.5 1.5 collective-permute-start.28
  123.0 2.7 %collective-permute-done.34 = f32[1,36,8,128]{3,2,1,0:T(8,128)S(1)} collective-permute-done((f32[1,36,8,128]{3,2,1,0:T(8,128)S(1)}, f32[1,36,8,128]{3,2,1,0:T(8,128)S(1)}, u32[]{:S(2)}, u32[]{:S(2)}) %collective-permute-start.34) | collective-permute-done | bytes 147488 | tf_op jit(solution)/shard_map/ppermute | solution.py:37
  127.2 1.5 collective-permute-done.28
  128.9 4.2 %collective-permute-done.35 = f32[2,36,8,128]{3,2,1,0:T(8,128)S(1)} collective-permute-done((f32[2,36,8,128]{3,2,1,0:T(8,128)S(1)}, f32[2,36,8,128]{3,2,1,0:T(8,128)S(1)}, u32[]{:S(2)}, u32[]{:S(2)}) %collective-permute-start.35) | collective-permute-done | bytes 294944 | tf_op jit(solution)/shard_map/ppermute | solution.py:37
  133.3 15.0 %collective-permute-start.36 = (f32[4,36,8,128]{3,2,1,0:T(8,128)S(1)}, f32[4,36,8,128]{3,2,1,0:T(8,128)S(1)}, u32[]{:S(2)}, u32[]{:S(2)}) collective-permute-start(f32[4,36,8,128]{3,2,1,0:T(8,128)S(1)} %maximum_select_fusion.2.rest_2_), channel_id=1, source_target_pairs={{0,1},{1,0},{2,3},{3,2},{4,5},{5,4},{6,7},{7,6},{8,9},{9,8},{10,11... | collective-permute-start | bytes 1769480 | tf_op jit(solution)/shard_map/ppermute | solution.py:45
  148.3 6.3 %solve.1 = (bf16[112,192]{1,0:T(8,128)(2,1)S(1)}, f32[4,38,8,128]{3,2,1,0:T(8,128)S(1)}) custom-call(f32[72,128]{1,0:T(8,128)S(1)} %get-tuple-element.55.gram_ref, f32[112,64]{1,0:T(8,128)S(1)} %get-tuple-element.56.p_ref, f32[4,38,8,128]{3,2,1,0:T(8,128)S(1)} %maximum_select_fusion.block_ref.rest_4_), custom_call_target="tpu_custom_call" | custom-call | flops 10000000 | bytes 10000000 | tf_op jit(solution)/shard_map/solve/pallas_call | solution.py:294
  157.8 7.0 %finish_own.1 = (bf16[1,112,28672]{2,1,0:T(8,128)(2,1)}, f32[112,1792]{1,0:T(8,128)}, f32[112,1792]{1,0:T(8,128)}) custom-call(s32[5]{0:T(128)} %stack.23.s_ref, bf16[112,192]{1,0:T(8,128)(2,1)} %copy-done.5, f32[4,38,8,128]{3,2,1,0:T(8,128)} %copy-done.7, f32[4,38,8,128]{3,2,1,0:T(8,128)} %copy-done.9, f32[4,36,8,128]{3,2,1,0:T(8,128)} %copy-done.8, ...), custom_call_target="tpu_custom_call" | custom-call | flops 616562688 | bytes 13303808 | tf_op jit(solution)/shard_map/finish_own/pallas_call | solution.py:370
  166.3 8.6 %finish_far.1 = (bf16[1,112,28672]{2,1,0:T(8,128)(2,1)}, f32[112,1792]{1,0:T(8,128)}, f32[112,1792]{1,0:T(8,128)}) custom-call(s32[5]{0:T(128)} %stack.23.s_ref, bf16[112,192]{1,0:T(8,128)(2,1)} %copy-done.5, f32[4,38,8,128]{3,2,1,0:T(8,128)} %copy-done.11, ...), custom_call_target="tpu_custom_call", output_to_operand_aliasing={{0}: (12, {}), {1}: (13, {}), {2}: (14, {})} | custom-call | flops 616562688 | bytes 13303808 | tf_op jit(solution)/shard_map/finish_far/pallas_call | solution.py:370
  (137 shorter events, 31.9 us)
Async XLA Ops:
  11.0 5.1 %collective-permute-start.2 = (f32[64,128]{1,0:T(8,128)}, f32[64,128]{1,0:T(8,128)S(1)}, u32[]{:S(2)}, u32[]{:S(2)}) collective-permute-start(f32[64,128]{1,0:T(8,128)} %left_factor.1), channel_id=1, source_target_pairs={{0,24},{8,0},{16,8},{24,16},{1,25},{9,1},{17,9},{25,17},{2,26},{10... | collective-permute-start | bytes 98312 | tf_op jit(solution)/shard_map/ppermute | solution.py:33
  14.3 4.7 %collective-permute-start = (f32[64,128]{1,0:T(8,128)}, f32[64,128]{1,0:T(8,128)S(1)}, u32[]{:S(2)}, u32[]{:S(2)}) collective-permute-start(f32[64,128]{1,0:T(8,128)} %left_factor.1), channel_id=1, source_target_pairs={{0,16},{8,24},{16,0},{24,8},{1,17},{9,25},{17,1},{25,9},{2,18},{10... | collective-permute-start | bytes 98312 | tf_op jit(solution)/shard_map/ppermute | solution.py:33
  19.8 5.7 %collective-permute-start.5 = (f32[64,128]{1,0:T(8,128)S(1)}, f32[64,128]{1,0:T(8,128)S(1)}, u32[]{:S(2)}, u32[]{:S(2)}) collective-permute-start(f32[64,128]{1,0:T(8,128)S(1)} %add_add_fusion.1.a_ref), channel_id=1, source_target_pairs={{0,96},{32,0},{64,32},{96,64},{1,97},{33,1},{65,33},{97,65},{2,98}... | collective-permute-start | bytes 98312 | tf_op jit(solution)/shard_map/ppermute | solution.py:33
  34.1 9.8 %collective-permute-start.7 = (f32[8,38,8,128]{3,2,1,0:T(8,128)}, f32[8,38,8,128]{3,2,1,0:T(8,128)S(1)}, u32[]{:S(2)}, u32[]{:S(2)}) collective-permute-start(f32[8,38,8,128]{3,2,1,0:T(8,128)} %get-tuple-element.41), channel_id=1, source_target_pairs={{0,1},{1,0},{2,3},{3,2},{4,5},{5,4},{6,7},{7,6},{8,9},{9,8},{10,11... | collective-permute-start | bytes 3735560 | tf_op jit(solution)/shard_map/ppermute | solution.py:45
  37.6 6.3 %collective-permute-start.9 = (f32[8,38,8,128]{3,2,1,0:T(8,128)}, f32[8,38,8,128]{3,2,1,0:T(8,128)S(1)}, u32[]{:S(2)}, u32[]{:S(2)}) collective-permute-start(f32[8,38,8,128]{3,2,1,0:T(8,128)} %get-tuple-element.43), channel_id=1, source_target_pairs={{0,1},{1,0},{2,3},{3,2},{4,5},{5,4},{6,7},{7,6},{8,9},{9,8},{10,11... | collective-permute-start | bytes 3735560 | tf_op jit(solution)/shard_map/ppermute | solution.py:45
  37.7 6.2 %collective-permute-start.8 = (f32[8,36,8,128]{3,2,1,0:T(8,128)}, f32[8,36,8,128]{3,2,1,0:T(8,128)S(1)}, u32[]{:S(2)}, u32[]{:S(2)}) collective-permute-start(f32[8,36,8,128]{3,2,1,0:T(8,128)} %get-tuple-element.42), channel_id=1, source_target_pairs={{0,1},{1,0},{2,3},{3,2},{4,5},{5,4},{6,7},{7,6},{8,9},{9,8},{10,11... | collective-permute-start | bytes 3538952 | tf_op jit(solution)/shard_map/ppermute | solution.py:45
  38.1 5.3 %collective-permute-start.6 = (f32[72,128]{1,0:T(8,128)S(1)}, f32[72,128]{1,0:T(8,128)S(1)}, u32[]{:S(2)}, u32[]{:S(2)}) collective-permute-start(f32[72,128]{1,0:T(8,128)S(1)} %get-tuple-element.35.a_ref.refs_0_), channel_id=1, source_target_pairs={{0,1},{1,0},{2,3},{3,2},{4,5},{5,4},{6,7},{7,6},{8,9},{9,8},{10,11... | collective-permute-start | bytes 110600 | tf_op jit(solution)/shard_map/ppermute | solution.py:45
  51.3 15.7 %collective-permute-start.10 = (f32[153,8,128]{2,1,0:T(8,128)}, f32[153,8,128]{2,1,0:T(8,128)}, u32[]{:S(2)}, u32[]{:S(2)}) collective-permute-start(f32[153,8,128]{2,1,0:T(8,128)} %get-tuple-element.46), channel_id=1, source_target_pairs={{0,2},{2,0},{4,6},{6,4},{1,3},{3,1},{5,7},{7,5},{8,10},{10,8},{12,... | collective-permute-start | bytes 1880072 | tf_op jit(solution)/shard_map/ppermute | solution.py:37
  52.7 16.8 %collective-permute-start.16 = (f32[152,8,128]{2,1,0:T(8,128)}, f32[152,8,128]{2,1,0:T(8,128)}, u32[]{:S(2)}, u32[]{:S(2)}) collective-permute-start(f32[152,8,128]{2,1,0:T(8,128)} %get-tuple-element.54), channel_id=1, source_target_pairs={{0,32},{32,0},{64,96},{96,64},{1,33},{33,1},{65,97},{97,65},{2,34}... | collective-permute-start | bytes 1867784 | tf_op jit(solution)/shard_map/ppermute | solution.py:37
  52.9 18.2 %collective-permute-start.11 = (f32[152,8,128]{2,1,0:T(8,128)S(1)}, f32[152,8,128]{2,1,0:T(8,128)S(1)}, u32[]{:S(2)}, u32[]{:S(2)}) collective-permute-start(f32[152,8,128]{2,1,0:T(8,128)S(1)} %get-tuple-element.49), channel_id=1, source_target_pairs={{0,8},{8,0},{16,24},{24,16},{1,9},{9,1},{17,25},{25,17},{2,10},{10... | collective-permute-start | bytes 1867784 | tf_op jit(solution)/shard_map/ppermute | solution.py:37
  69.2 7.4 %collective-permute-start.14 = (f32[2,36,8,128]{3,2,1,0:T(8,128)S(1)}, f32[2,36,8,128]{3,2,1,0:T(8,128)S(1)}, u32[]{:S(2)}, u32[]{:S(2)}) collective-permute-start(f32[2,36,8,128]{3,2,1,0:T(8,128)S(1)} %get-tuple-element.72), channel_id=1, source_target_pairs={{0,32},{32,0},{64,96},{96,64},{1,33},{33,1},{65,97},{97,65},{2,34}... | collective-permute-start | bytes 884744 | tf_op jit(solution)/shard_map/ppermute | solution.py:37
  70.6 7.5 %collective-permute-start.17 = (f32[2,38,8,128]{3,2,1,0:T(8,128)S(1)}, f32[2,38,8,128]{3,2,1,0:T(8,128)S(1)}, u32[]{:S(2)}, u32[]{:S(2)}) collective-permute-start(f32[2,38,8,128]{3,2,1,0:T(8,128)S(1)} %get-tuple-element.70), channel_id=1, source_target_pairs={{0,8},{8,0},{16,24},{24,16},{1,9},{9,1},{17,25},{25,17},{2,10},{10... | collective-permute-start | bytes 933896 | tf_op jit(solution)/shard_map/ppermute | solution.py:37
  71.2 8.3 %collective-permute-start.12 = (f32[2,38,8,128]{3,2,1,0:T(8,128)S(1)}, f32[2,38,8,128]{3,2,1,0:T(8,128)S(1)}, u32[]{:S(2)}, u32[]{:S(2)}) collective-permute-start(f32[2,38,8,128]{3,2,1,0:T(8,128)S(1)} %get-tuple-element.68), channel_id=1, source_target_pairs={{0,2},{2,0},{4,6},{6,4},{1,3},{3,1},{5,7},{7,5},{8,10},{10,8},{12,... | collective-permute-start | bytes 933896 | tf_op jit(solution)/shard_map/ppermute | solution.py:37
  76.6 4.8 %collective-permute-start.15 = (f32[1,36,8,128]{3,2,1,0:T(8,128)S(1)}, f32[1,36,8,128]{3,2,1,0:T(8,128)S(1)}, u32[]{:S(2)}, u32[]{:S(2)}) collective-permute-start(f32[1,36,8,128]{3,2,1,0:T(8,128)S(1)} %dynamic-slice_add_fusion.5), channel_id=1, source_target_pairs={{0,8},{8,0},{16,24},{24,16},{1,9},{9,1},{17,25},{25,17},{2,10},{10... | collective-permute-start | bytes 442376 | tf_op jit(solution)/shard_map/ppermute | solution.py:37
  78.1 4.5 %collective-permute-start.18 = (f32[1,38,8,128]{3,2,1,0:T(8,128)S(1)}, f32[1,38,8,128]{3,2,1,0:T(8,128)S(1)}, u32[]{:S(2)}, u32[]{:S(2)}) collective-permute-start(f32[1,38,8,128]{3,2,1,0:T(8,128)S(1)} %dynamic-slice_add_fusion.4), channel_id=1, source_target_pairs={{0,2},{2,0},{4,6},{6,4},{1,3},{3,1},{5,7},{7,5},{8,10},{10,8},{12,... | collective-permute-start | bytes 466952 | tf_op jit(solution)/shard_map/ppermute | solution.py:37
  83.8 6.6 %collective-permute-start.19 = (f32[65,8,128]{2,1,0:T(8,128)S(1)}, f32[65,8,128]{2,1,0:T(8,128)S(1)}, u32[]{:S(2)}, u32[]{:S(2)}) collective-permute-start(f32[65,8,128]{2,1,0:T(8,128)S(1)} %pad_maximum_fusion.1), channel_id=1, source_target_pairs={{0,6},{2,4},{4,2},{6,0},{1,7},{3,5},{5,3},{7,1},{8,14},{10,12},{12... | collective-permute-start | bytes 798728 | tf_op jit(solution)/shard_map/ppermute | solution.py:41
  90.9 7.5 %collective-permute-start.20 = (f32[14,8,128]{2,1,0:T(8,128)S(1)}, f32[14,8,128]{2,1,0:T(8,128)S(1)}, u32[]{:S(2)}, u32[]{:S(2)}) collective-permute-start(f32[14,8,128]{2,1,0:T(8,128)S(1)} %get-tuple-element.75), channel_id=1, source_target_pairs={{0,120},{8,112},{16,104},{24,96},{32,88},{40,80},{48,72},{56,64},{... | collective-permute-start | bytes 172040 | tf_op jit(solution)/shard_map/ppermute | solution.py:454
  101.1 5.3 %collective-permute-start.23 = (f32[14,8,128]{2,1,0:T(8,128)S(1)}, f32[14,8,128]{2,1,0:T(8,128)S(1)}, u32[]{:S(2)}, u32[]{:S(2)}) collective-permute-start(f32[14,8,128]{2,1,0:T(8,128)S(1)} %add_add_fusion), channel_id=1, source_target_pairs={{0,24},{8,16},{16,8},{24,0},{1,25},{9,17},{17,9},{25,1},{2,26},{10... | collective-permute-start | bytes 172040 | tf_op jit(solution)/shard_map/ppermute | solution.py:41
  104.2 6.3 %collective-permute-start.25 = (f32[14,8,128]{2,1,0:T(8,128)S(1)}, f32[14,8,128]{2,1,0:T(8,128)S(1)}, u32[]{:S(2)}, u32[]{:S(2)}) collective-permute-start(f32[14,8,128]{2,1,0:T(8,128)S(1)} %add_add_fusion), channel_id=1, source_target_pairs={{0,120},{8,112},{16,104},{24,96},{32,88},{40,80},{48,72},{56,64},{... | collective-permute-start | bytes 172040 | tf_op jit(solution)/shard_map/ppermute | solution.py:454
  110.6 6.4 %collective-permute-start.26 = (f32[56,8,128]{2,1,0:T(8,128)S(1)}, f32[56,8,128]{2,1,0:T(8,128)S(1)}, u32[]{:S(2)}, u32[]{:S(2)}) collective-permute-start(f32[56,8,128]{2,1,0:T(8,128)S(1)} %maximum_select_fusion.7), channel_id=1, source_target_pairs={{0,6},{2,4},{4,2},{6,0},{1,7},{3,5},{5,3},{7,1},{8,14},{10,12},{12... | collective-permute-start | bytes 688136 | tf_op jit(solution)/shard_map/ppermute | solution.py:41
  121.2 5.8 %collective-permute-start.30 = (f32[2,38,8,128]{3,2,1,0:T(8,128)S(1)}, f32[2,38,8,128]{3,2,1,0:T(8,128)S(1)}, u32[]{:S(2)}, u32[]{:S(2)}) collective-permute-start(f32[2,38,8,128]{3,2,1,0:T(8,128)S(1)} %maximum_select_fusion.5), channel_id=1, source_target_pairs={{0,2},{2,0},{4,6},{6,4},{1,3},{3,1},{5,7},{7,5},{8,10},{10,8},{12,... | collective-permute-start | bytes 933896 | tf_op jit(solution)/shard_map/ppermute | solution.py:37
  121.5 7.3 %collective-permute-start.28 = (f32[2,38,8,128]{3,2,1,0:T(8,128)S(1)}, f32[2,38,8,128]{3,2,1,0:T(8,128)S(1)}, u32[]{:S(2)}, u32[]{:S(2)}) collective-permute-start(f32[2,38,8,128]{3,2,1,0:T(8,128)S(1)} %maximum_select_fusion.4), channel_id=1, source_target_pairs={{0,8},{8,0},{16,24},{24,16},{1,9},{9,1},{17,25},{25,17},{2,10},{10... | collective-permute-start | bytes 933896 | tf_op jit(solution)/shard_map/ppermute | solution.py:37
  125.7 7.4 %collective-permute-start.35 = (f32[2,36,8,128]{3,2,1,0:T(8,128)S(1)}, f32[2,36,8,128]{3,2,1,0:T(8,128)S(1)}, u32[]{:S(2)}, u32[]{:S(2)}) collective-permute-start(f32[2,36,8,128]{3,2,1,0:T(8,128)S(1)} %maximum_select_fusion.6), channel_id=1, source_target_pairs={{0,32},{32,0},{64,96},{96,64},{1,33},{33,1},{65,97},{97,65},{2,34}... | collective-permute-start | bytes 884744 | tf_op jit(solution)/shard_map/ppermute | solution.py:37
  127.1 29.1 %collective-permute-start.32 = (f32[4,38,8,128]{3,2,1,0:T(8,128)S(1)}, f32[4,38,8,128]{3,2,1,0:T(8,128)S(1)}, u32[]{:S(2)}, u32[]{:S(2)}) collective-permute-start(f32[4,38,8,128]{3,2,1,0:T(8,128)S(1)} %maximum_select_fusion.1.rest_0_), channel_id=1, source_target_pairs={{0,8},{8,0},{16,24},{24,16},{1,9},{9,1},{17,25},{25,17},{2,10},{10... | collective-permute-start | bytes 1867784 | tf_op jit(solution)/shard_map/ppermute | solution.py:37
  128.8 27.5 %collective-permute-start.40 = (f32[4,38,8,128]{3,2,1,0:T(8,128)S(1)}, f32[4,38,8,128]{3,2,1,0:T(8,128)S(1)}, u32[]{:S(2)}, u32[]{:S(2)}) collective-permute-start(f32[4,38,8,128]{3,2,1,0:T(8,128)S(1)} %maximum_select_fusion.block_ref.rest_4_), channel_id=1, source_target_pairs={{0,32},{32,0},{64,96},{96,64},{1,33},{33,1},{65,97},{97,65},{2,34}... | collective-permute-start | bytes 1867784 | tf_op jit(solution)/shard_map/ppermute | solution.py:37
  133.2 22.0 %collective-permute-start.37 = (f32[4,36,8,128]{3,2,1,0:T(8,128)S(1)}, f32[4,36,8,128]{3,2,1,0:T(8,128)}, u32[]{:S(2)}, u32[]{:S(2)}) collective-permute-start(f32[4,36,8,128]{3,2,1,0:T(8,128)S(1)} %maximum_select_fusion.2.rest_2_), channel_id=1, source_target_pairs={{0,2},{2,0},{4,6},{6,4},{1,3},{3,1},{5,7},{7,5},{8,10},{10,8},{12,... | collective-permute-start | bytes 1769480 | tf_op jit(solution)/shard_map/ppermute | solution.py:37
  133.3 23.5 %collective-permute-start.36 = (f32[4,36,8,128]{3,2,1,0:T(8,128)S(1)}, f32[4,36,8,128]{3,2,1,0:T(8,128)S(1)}, u32[]{:S(2)}, u32[]{:S(2)}) collective-permute-start(f32[4,36,8,128]{3,2,1,0:T(8,128)S(1)} %maximum_select_fusion.2.rest_2_), channel_id=1, source_target_pairs={{0,1},{1,0},{2,3},{3,2},{4,5},{5,4},{6,7},{7,6},{8,9},{9,8},{10,11... | collective-permute-start | bytes 1769480 | tf_op jit(solution)/shard_map/ppermute | solution.py:45
  148.2 16.6 %collective-permute-start.31 = (f32[4,38,8,128]{3,2,1,0:T(8,128)S(1)}, f32[4,38,8,128]{3,2,1,0:T(8,128)S(1)}, u32[]{:S(2)}, u32[]{:S(2)}) collective-permute-start(f32[4,38,8,128]{3,2,1,0:T(8,128)S(1)} %maximum_select_fusion.1.rest_0_), channel_id=1, source_target_pairs={{0,1},{1,0},{2,3},{3,2},{4,5},{5,4},{6,7},{7,6},{8,9},{9,8},{10,11... | collective-permute-start | bytes 1867784 | tf_op jit(solution)/shard_map/ppermute | solution.py:45
  155.2 9.7 %collective-permute-start.39 = (f32[4,38,8,128]{3,2,1,0:T(8,128)S(1)}, f32[4,38,8,128]{3,2,1,0:T(8,128)S(1)}, u32[]{:S(2)}, u32[]{:S(2)}) collective-permute-start(f32[4,38,8,128]{3,2,1,0:T(8,128)S(1)} %get-tuple-element.60), channel_id=1, source_target_pairs={{0,1},{1,0},{2,3},{3,2},{4,5},{5,4},{6,7},{7,6},{8,9},{9,8},{10,11... | collective-permute-start | bytes 1867784 | tf_op jit(solution)/shard_map/ppermute | solution.py:45
  156.2 8.7 %collective-permute-start.33 = (f32[4,38,8,128]{3,2,1,0:T(8,128)S(1)}, f32[4,38,8,128]{3,2,1,0:T(8,128)S(1)}, u32[]{:S(2)}, u32[]{:S(2)}) collective-permute-start(f32[4,38,8,128]{3,2,1,0:T(8,128)S(1)} %collective-permute-done.32.rest_1_), channel_id=1, source_target_pairs={{0,1},{1,0},{2,3},{3,2},{4,5},{5,4},{6,7},{7,6},{8,9},{9,8},{10,11... | collective-permute-start | bytes 1867784 | tf_op jit(solution)/shard_map/ppermute | solution.py:45
  156.3 8.6 %collective-permute-start.41 = (f32[4,38,8,128]{3,2,1,0:T(8,128)S(1)}, f32[4,38,8,128]{3,2,1,0:T(8,128)}, u32[]{:S(2)}, u32[]{:S(2)}) collective-permute-start(f32[4,38,8,128]{3,2,1,0:T(8,128)S(1)} %collective-permute-done.40.rest_5_), channel_id=1, source_target_pairs={{0,1},{1,0},{2,3},{3,2},{4,5},{5,4},{6,7},{7,6},{8,9},{9,8},{10,11... | collective-permute-start | bytes 1867784 | tf_op jit(solution)/shard_map/ppermute | solution.py:45
  157.6 7.3 %collective-permute-start.38 = (f32[4,36,8,128]{3,2,1,0:T(8,128)}, f32[4,36,8,128]{3,2,1,0:T(8,128)S(1)}, u32[]{:S(2)}, u32[]{:S(2)}) collective-permute-start(f32[4,36,8,128]{3,2,1,0:T(8,128)} %collective-permute-done.37.rest_3_), channel_id=1, source_target_pairs={{0,1},{1,0},{2,3},{3,2},{4,5},{5,4},{6,7},{7,6},{8,9},{9,8},{10,11... | collective-permute-start | bytes 1769480 | tf_op jit(solution)/shard_map/ppermute | solution.py:45
  (26 other events, 142.6 us)
